TPU v7x, 128 devices: a whole 4x4x4 slice. The times are simulated.
128 devices in a mesh: fsdp: 16 (over x, y_hi, core), node: 8 (over y_lo, z).
Axes of the slice: x: 4, y: 4 (y_hi: 2, y_lo: 2; y = y_hi * 2 + y_lo), z: 4, core: 2. Of those that a mesh axis runs over, the one named last changes fastest.
Arguments:
- activations: bfloat16 [8192, 8192], P('fsdp', 'node'), may hold values from -6 to 6
- qkv_weight: bfloat16 [8192, 5120], P('fsdp', 'node'), may hold values from -0.09375 to 0.09375
- qkv_grad: bfloat16 [8192, 5120], P('fsdp', 'node'), may hold values from -6 to 6
Outputs:
- projected: bfloat16 [8192, 5120], P('fsdp', 'node')
- input_grad: bfloat16 [8192, 8192], P('fsdp', 'node')
- weight_grad: float32 [8192, 5120], P('fsdp', 'node')
All inputs are finite; a program needn't handle non-finite values.
Results may differ from a plain program's by a relative error of at most 0.017.
Values may be sent and summed in bfloat16 or wider, within the bound.
No kernel may reach another device: no remote copies, remote signals or barrier semaphores. Data moves between devices by JAX's collectives and lax.ppermute only.
A program may use at most 128 MiB of HBM per device.

v0:
```python
import jax
import jax.numpy as jnp
from jax import lax
from jax.sharding import PartitionSpec as P


def body(activations, qkv_weight, qkv_grad):
    gathered = lax.all_gather(activations, "node", axis=1, tiled=True)
    feature_cols = gathered
    forward = jnp.dot(
        feature_cols,
        lax.all_gather(qkv_weight, "fsdp", axis=0, tiled=True),
        preferred_element_type=jnp.float32,
    )
    partial_sum = lax.dot_general(
        qkv_grad,
        lax.all_gather(qkv_weight, "fsdp", axis=0, tiled=True),
        (((1,), (1,)), ((), ())),
        preferred_element_type=jnp.float32,
    )
    projected = forward.astype(jnp.bfloat16)
    input_grad = lax.psum_scatter(
        partial_sum.astype(jnp.bfloat16), "node", scatter_dimension=1, tiled=True
    )
    feature_cols = gathered
    weight_grad = lax.psum_scatter(
        lax.dot_general(
            feature_cols, qkv_grad, (((0,), (0,)), ((), ())), preferred_element_type=jnp.float32
        ).astype(jnp.bfloat16),
        "fsdp",
        scatter_dimension=0,
        tiled=True,
    ).astype(jnp.float32)
    return (projected, input_grad, weight_grad)


def solution(mesh):
    in_specs = (P("fsdp", "node"), P("fsdp", "node"), P("fsdp", "node"))
    out_specs = (P("fsdp", "node"), P("fsdp", "node"), P("fsdp", "node"))
    return jax.shard_map(body, mesh=mesh, in_specs=in_specs, out_specs=out_specs, check_vma=False)
```

profile of v0, /device:TPU:1, one launch (start us, length us, event | category | flops | bytes accessed | tf_op | source)
XLA Modules:
  0.0 403.2 jit_solution(3688470017451927738)
XLA Ops:
  7.2 0.0 copy-start
  7.2 0.0 all-gather.3.cloned.1.call-start
  7.2 0.7 all-gather.3.cloned.1.call-update
  7.9 0.0 all-gather.5.cloned.1.call-start
  8.0 0.7 all-gather.5.cloned.1.call-update
  8.7 0.0 reduce-scatter.5.cloned.1.call-start
  8.7 96.3 %all-gather.3.cloned.1.call-done = bf16[512,8192]{1,0:T(8,128)(2,1)} async-done(((bf16[512,1024]{1,0:T(8,128)(2,1)}), bf16[512,8192]{1,0:T(8,128)(2,1)}) %all-gather.3.cloned.1.call-update) | async-done | bytes 8388624 | tf_op jit(solution)/shard_map/all_gather | solution.py:8
  105.0 0.0 copy-done
  105.0 11.4 %convolution_convert_fusion = bf16[8192,640]{1,0:T(8,128)(2,1)} fusion(bf16[512,8192]{1,0:T(8,128)(2,1)} %all-gather.3.cloned.1.call-done, bf16[512,640]{1,0:T(8,128)(2,1)S(1)} %copy-done), kind=kOutput, calls=%fused_computation | convolution fusion | flops 5373952000 | bytes 19529728 | tf_op jit(solution)/shard_map/dot_general | solution.py:27
  116.4 0.0 reduce-scatter.5.cloned.1.call-update
  116.5 0.0 reduce-scatter.3.cloned.1.call-start
  116.5 71.4 %all-gather.5.cloned.1.call-done = bf16[8192,640]{1,0:T(8,128)(2,1)} async-done(((bf16[512,640]{1,0:T(8,128)(2,1)}), bf16[8192,640]{1,0:T(8,128)(2,1)}) %all-gather.5.cloned.1.call-update) | async-done | bytes 10485776 | tf_op jit(solution)/shard_map/all_gather | solution.py:12
  188.0 13.0 %convolution_convert_fusion.1 = bf16[512,8192]{1,0:T(8,128)(2,1)} fusion(bf16[512,640]{1,0:T(8,128)(2,1)S(1)} %copy-done, bf16[8192,640]{1,0:T(8,128)(2,1)} %all-gather.5.cloned.1.call-done), kind=kOutput, calls=%fused_computation.1 | convolution fusion | flops 5372903424 | bytes 19529728 | tf_op jit(solution)/shard_map/dot_general | solution.py:15
  200.9 0.0 reduce-scatter.3.cloned.1.call-update
  200.9 14.5 %convolution_convert_fusion.2 = bf16[512,640]{1,0:T(8,128)(2,1)} fusion(bf16[512,8192]{1,0:T(8,128)(2,1)} %all-gather.3.cloned.1.call-done, bf16[8192,640]{1,0:T(8,128)(2,1)} %all-gather.5.cloned.1.call-done), kind=kOutput, calls=%fused_computation.2 | convolution fusion | flops 5369036800 | bytes 19529728 | tf_op jit(solution)/shard_map/dot_general | solution.py:10
  215.5 85.6 %reduce-scatter.5.cloned.1.call-done = bf16[512,640]{1,0:T(8,128)(2,1)} async-done(((bf16[8192,640]{1,0:T(8,128)(2,1)}), bf16[512,640]{1,0:T(8,128)(2,1)}) %reduce-scatter.5.cloned.1.call-update) | async-done | bytes 655376 | tf_op jit(solution)/shard_map/reduce_scatter | solution.py:26
  301.1 2.2 convert_element_type.15
  303.3 93.3 %reduce-scatter.3.cloned.1.call-done = bf16[512,1024]{1,0:T(8,128)(2,1)} async-done(((bf16[512,8192]{1,0:T(8,128)(2,1)}), bf16[512,1024]{1,0:T(8,128)(2,1)}) %reduce-scatter.3.cloned.1.call-update) | async-done | bytes 1048592 | tf_op jit(solution)/shard_map/reduce_scatter | solution.py:22
Async XLA Ops:
  7.2 97.8 %copy-start = (bf16[512,640]{1,0:T(8,128)(2,1)S(1)}, bf16[512,640]{1,0:T(8,128)(2,1)}, u32[]{:S(2)}) copy-start(bf16[512,640]{1,0:T(8,128)(2,1)} %param.5) | copy-start | bytes 1966084
  7.2 97.8 %all-gather.3.cloned.1.call-start = ((), (), s32[]{:S(2)}) async-start(), calls=%async_computation.2 | async-start | bytes 9437184 | tf_op jit(solution)/shard_map/all_gather | solution.py:8
  7.9 180.0 %all-gather.5.cloned.1.call-start = ((), (), s32[]{:S(2)}) async-start(), calls=%async_computation.3 | async-start | bytes 11141120 | tf_op jit(solution)/shard_map/all_gather | solution.py:12
  8.7 292.4 %reduce-scatter.5.cloned.1.call-start = ((), (), s32[]{:S(2)}) async-start(), calls=%async_computation.5 | async-start | bytes 11141120 | tf_op jit(solution)/shard_map/reduce_scatter | solution.py:26
  116.5 280.2 %reduce-scatter.3.cloned.1.call-start = ((), (), s32[]{:S(2)}) async-start(), calls=%async_computation.4 | async-start | bytes 9437184 | tf_op jit(solution)/shard_map/reduce_scatter | solution.py:22
Sparse Core Ops, SparseCore 0:
  9.7 95.2 all-gather.2
  107.4 80.5 all-gather.4
  192.3 108.7 reduce-scatter.4
  304.1 92.5 reduce-scatter.2
where the time goes:
time: 403 us
  waiting for transfers between devices  348 us (86%)
  matrix products  38.9 us (10%)
  between operations  13.8 us (3%)
    all_gather x1, waiting for transfers between devices, body(): gathered = lax.all_gather(activations, 'node', axis=1, tiled=True)  96.3 us
    reduce_scatter x1, waiting for transfers between devices, body(): lax.psum_scatter(partial_sum.astype(jnp.bfloat16), 'node', scatter_dimens...  93.3 us
    reduce_scatter x1, waiting for transfers between devices, body(): lax.psum_scatter(lax.dot_general(feature_cols, qkv_grad, (((0,), (0,)), (...  85.6 us
    all_gather x1, waiting for transfers between devices, body(): lax.all_gather(qkv_weight, 'fsdp', axis=0, tiled=True)  71.4 us
    dot_general x1, matrix products, body(): jnp.dot(feature_cols, lax.all_gather(qkv_weight, 'fsdp', axis=0, tiled=Tr...  14.5 us
    dot_general x1, matrix products, body(): lax.dot_general(qkv_grad, lax.all_gather(qkv_weight, 'fsdp', axis=0, tile...  13 us
    dot_general x1, matrix products, body(): lax.dot_general(feature_cols, qkv_grad, (((0,), (0,)), ((), ())), preferr...  11.4 us
  transfers between devices with their start and end apart: 4, of which 4 were waited for; matrix products, arithmetic and copies ran while one was open for 10% of the time, Pallas kernels for 0%

commit v1 on v0

v1 whole, which is shorter than its diff:
```python
import functools

import jax
import jax.numpy as jnp
from jax import lax
from jax.experimental import pallas as pl
from jax.experimental.pallas import tpu as pltpu
from jax.sharding import PartitionSpec as P

AXES = ("fsdp", "node")
BF16, F32 = jnp.bfloat16, jnp.float32


def flip(value, x=0, y=0, z=0, c=0):
    pairs = []
    for i in range(128):
        p, q = divmod(i, 8)
        px, py, pc = p // 4, (p // 2 % 2) * 2 + q // 4, p % 2
        px, py, pz, pc = px ^ x, py ^ y, q % 4 ^ z, pc ^ c
        pairs.append((i, ((px * 2 + py // 2) * 2 + pc) * 8 + py % 2 * 4 + pz))
    return lax.ppermute(value, AXES, pairs)


def add(*terms):
    total = terms[0].astype(F32)
    for term in terms[1:]:
        total = total + term.astype(F32)
    return total


def gather4(value, axis):
    one, three = flip(value, **{axis: 1}), flip(value, **{axis: 3})
    half = value.shape[0] // 2
    far = [flip(three[:half], **{axis: 1}), flip(one[half:], **{axis: 3})]
    return [value, one, jnp.concatenate(far, 0), three]


def scatter4(pieces, axis):
    (own_t, own_b), (one_t, one_b), (far_t, far_b), (three_t, three_b) = pieces
    top3 = flip(far_t, **{axis: 1})
    bottom1 = flip(far_b, **{axis: 3})
    got1_t = flip(one_t, **{axis: 1})
    got3_b = flip(three_b, **{axis: 3})
    got1_b = flip(add(one_b, bottom1).astype(BF16), **{axis: 1})
    got3_t = flip(add(three_t, top3).astype(BF16), **{axis: 3})
    return add(own_t, got1_t, got3_t), add(own_b, got1_b, got3_b)


def dw_kernel(m, a, g, out):
    out[0] = lax.dot_general(a[0], g[...], (((0,), (0,)), ((), ())), preferred_element_type=F32).astype(BF16)


def weight_terms(mask, a, g):
    n, t, d = a.shape
    return pl.pallas_call(
        dw_kernel,
        grid_spec=pltpu.PrefetchScalarGridSpec(
            num_scalar_prefetch=1,
            grid=(n,),
            in_specs=[
                pl.BlockSpec((1, t, d), lambda k, m: (k ^ m[0], 0, 0)),
                pl.BlockSpec(g.shape, lambda k, m: (0, 0)),
            ],
            out_specs=pl.BlockSpec((1, d, g.shape[1]), lambda k, m: (k, 0, 0)),
        ),
        out_shape=jax.ShapeDtypeStruct((n, d, g.shape[1]), BF16),
        compiler_params=pltpu.CompilerParams(vmem_limit_bytes=32 << 20),
        name="weight_terms",
    )(mask, a, g)


def da_kernel(m, g, w1, w2, out):
    i = pl.program_id(0) ^ m[0]
    n = w1.shape[2]
    contract = (((1,), (1,)), ((), ()))

    @pl.when(i % 2 == 0)
    def _():
        total = lax.dot_general(g[:, :n], w1[0], contract, preferred_element_type=F32)
        total += lax.dot_general(g[:, n:], w2[0, 0], contract, preferred_element_type=F32)
        out[0] = total.astype(BF16)

    @pl.when(i % 2 == 1)
    def _():
        total = lax.dot_general(g[:, :n], w2[0, 1], contract, preferred_element_type=F32)
        total += lax.dot_general(g[:, n:], w2[0, 2], contract, preferred_element_type=F32)
        out[0] = total.astype(BF16)


def input_terms(mask, g, w1, w2):
    t, d = g.shape[0], w1.shape[1]
    return pl.pallas_call(
        da_kernel,
        grid_spec=pltpu.PrefetchScalarGridSpec(
            num_scalar_prefetch=1,
            grid=(8,),
            in_specs=[
                pl.BlockSpec(g.shape, lambda i, m: (0, 0)),
                pl.BlockSpec((1, *w1.shape[1:]), lambda i, m: ((i ^ m[0]) // 2, 0, 0)),
                pl.BlockSpec((1, *w2.shape[1:]), lambda i, m: ((i ^ m[0]) // 2, 0, 0, 0)),
            ],
            out_specs=pl.BlockSpec((1, t, d), lambda i, m: (i, 0, 0)),
        ),
        out_shape=jax.ShapeDtypeStruct((8, t, d), BF16),
        compiler_params=pltpu.CompilerParams(vmem_limit_bytes=32 << 20),
        name="input_terms",
    )(mask, g, w1, w2)


def fwd_kernel(m, a0, a1, w1, w2, out, total):
    k = pl.program_id(0)
    n = w1.shape[2]

    def dot(left, right):
        return jnp.dot(left, right, preferred_element_type=F32)

    own = dot(a0[0], w1[0]) + dot(a1[0], w2[0, 1])
    other = dot(a0[0], w2[0, 0]) + dot(a1[0], w2[0, 2])

    @pl.when(k == 0)
    def _():
        total[:, :n] = own
        total[:, n:] = other

    @pl.when(k > 0)
    def _():
        total[:, :n] += own
        total[:, n:] += other

    @pl.when(k == 3)
    def _():
        out[...] = total[...].astype(BF16)


def forward_terms(mask, a, w1, w2):
    t, d, n = a.shape[1], a.shape[2], w1.shape[2]
    return pl.pallas_call(
        fwd_kernel,
        grid_spec=pltpu.PrefetchScalarGridSpec(
            num_scalar_prefetch=1,
            grid=(4,),
            in_specs=[
                pl.BlockSpec((1, t, d), lambda k, m: ((2 * k) ^ m[0], 0, 0)),
                pl.BlockSpec((1, t, d), lambda k, m: ((2 * k + 1) ^ m[0], 0, 0)),
                pl.BlockSpec((1, *w1.shape[1:]), lambda k, m: (k, 0, 0)),
                pl.BlockSpec((1, *w2.shape[1:]), lambda k, m: (k, 0, 0, 0)),
            ],
            out_specs=pl.BlockSpec((t, 2 * n), lambda k, m: (0, 0)),
            scratch_shapes=[pltpu.VMEM((t, 2 * n), F32)],
        ),
        out_shape=jax.ShapeDtypeStruct((t, 2 * n), BF16),
        compiler_params=pltpu.CompilerParams(vmem_limit_bytes=40 << 20),
        name="forward_terms",
    )(mask, a, a, w1, w2)


def body(activations, qkv_weight, qkv_grad):
    p, q = lax.axis_index("fsdp"), lax.axis_index("node")
    x, y_hi, c, y_lo, z = p // 4, p // 2 % 2, p % 2, q // 4, q % 4
    mask = ((x // 2 ^ y_lo) * 4 + (x % 2 ^ z // 2) * 2 + (y_hi ^ z % 2)).astype(jnp.int32).reshape(1)
    tok, wide = activations.shape
    cols = qkv_grad.shape[1]
    sub = wide // 4

    w_keep = lax.dynamic_slice_in_dim(qkv_weight, c * sub, sub, 0)
    w_got = flip(lax.dynamic_slice_in_dim(qkv_weight, (1 - c) * sub, sub, 0), c=1)
    same = c == y_lo
    w_same, w_diff = jnp.where(same, w_keep, w_got), jnp.where(same, w_got, w_keep)
    w_y1, w_y3, w_y2 = flip(w_diff, y=1), flip(w_diff, y=3), flip(w_same, y=2)

    a_keep = lax.dynamic_slice_in_dim(activations, y_lo * 2 * sub, 2 * sub, 1)
    a_y = flip(lax.dynamic_slice_in_dim(activations, (1 - y_lo) * 2 * sub, 2 * sub, 1), y=1)
    g_y = flip(qkv_grad, y=1)

    def by_core(a):
        mine = lax.dynamic_slice_in_dim(a, c * sub, sub, 1)
        theirs = flip(lax.dynamic_slice_in_dim(a, (1 - c) * sub, sub, 1), c=1)
        return jnp.concatenate([mine, theirs], 0)

    a0 = gather4(by_core(a_keep), "z")
    w1 = jnp.stack(gather4(w_same, "x"))
    a1 = gather4(by_core(a_y), "z")
    a = jnp.stack(a0 + a1)
    w2 = jnp.stack(gather4(jnp.concatenate([w_y1, w_y2, w_y3], 0), "x")).reshape(4, 3, sub, cols)
    g_rows = jnp.concatenate([qkv_grad, g_y], 1)
    g = jnp.concatenate([g_rows, flip(g_rows, c=1)], 0)

    dw = weight_terms(mask, a, g)
    dw_top, dw_bottom = scatter4([(dw[2 * k], dw[2 * k + 1]) for k in range(4)], "x")
    dw_00 = dw_top[:, :cols]
    dw_y1 = flip(dw_top[:, cols:].astype(BF16), y=1)
    dw_y2 = flip(dw_bottom[:, :cols].astype(BF16), y=2)
    dw_y3 = flip(dw_bottom[:, cols:].astype(BF16), y=3)
    b_same, b_diff = add(dw_00, dw_y2), add(dw_y1, dw_y3)
    b_keep = jnp.where(same, b_same, b_diff)
    b_got = flip(jnp.where(same, b_diff, b_same).astype(BF16), c=1).astype(F32)
    weight_grad = jnp.where(c == 0, jnp.concatenate([b_keep, b_got], 0), jnp.concatenate([b_got, b_keep], 0))

    da = input_terms(mask, g, w1, w2)
    da_keep, da_send = scatter4([(da[k], da[4 + k]) for k in range(4)], "z")
    da_y = flip(da_send.astype(BF16), y=1)
    da_keep = da_keep.astype(BF16)
    da_h0, da_h1 = jnp.where(y_lo == 0, da_keep, da_y), jnp.where(y_lo == 0, da_y, da_keep)
    both = jnp.concatenate([da_h0, da_h1], 1)
    mine, theirs = both[:tok], flip(both[tok:], c=1)
    r0, r1 = jnp.where(c == 0, mine, theirs), jnp.where(c == 0, theirs, mine)
    input_grad = jnp.concatenate([r0[:, :sub], r1[:, :sub], r0[:, sub:], r1[:, sub:]], 1)

    fwd = forward_terms(mask, a, w1, w2)
    fwd = add(fwd[:tok], flip(fwd[tok:], c=1))
    projected = add(fwd[:, :cols], flip(fwd[:, cols:].astype(BF16), y=1)).astype(BF16)
    return projected, input_grad, weight_grad


def solution(mesh):
    spec = P("fsdp", "node")
    return jax.shard_map(body, mesh=mesh, in_specs=(spec,) * 3, out_specs=(spec,) * 3, check_vma=False)
```

time: 403 us -> 207 us (0.51)
  waiting for transfers between devices: 348 us -> 84.4 us
  starting transfers between devices: 0.16 us -> 69.8 us
  matrix products: 38.9 us -> 0 us
  Pallas kernels: 0 us -> 24.7 us
  other arithmetic: 2.23 us -> 16.3 us
  between operations: 13.8 us -> 1.28 us
  local copies, waits for them, and re-layouts: 0.01 us -> 10.1 us
    reduce_scatter x2 -> x0, waiting for transfers between devices: 179 us -> none  [the longest x1 93.3 us: body(): lax.psum_scatter(partial_sum.astype(jnp.bfloat16), 'node', scatter_dimens...]
    all_gather x2 -> x0, waiting for transfers between devices: 168 us -> none  [the longest x1 96.3 us: body(): gathered = lax.all_gather(activations, 'node', axis=1, tiled=True)]
    ppermute x0 -> x45, waiting for transfers between devices: none -> 84.4 us  [flip(): return lax.ppermute(value, AXES, pairs)]
    ppermute x0 -> x45, starting transfers between devices: none -> 69.8 us  [flip(): return lax.ppermute(value, AXES, pairs)]
    dot_general x3 -> x0, matrix products: 38.9 us -> none  [the longest x1 14.5 us: body(): jnp.dot(feature_cols, lax.all_gather(qkv_weight, 'fsdp', axis=0, tiled=Tr...]
    pallas_call x0 -> x3, Pallas kernels: none -> 24.7 us  [the longest x1 9.37 us: forward_terms(): pl.pallas_call(fwd_kernel, grid_spec=pltpu.PrefetchScalarGridSpec(num_sca...]
    dynamic_slice x0 -> x4, local copies, waits for them, and re-layouts: none -> 4.3 us  [the longest x1 1.87 us: body(): lax.dynamic_slice_in_dim(activations, (1 - y_lo) * 2 * sub, 2 * sub, 1)]
  transfers between devices with their start and end apart: 4 -> 45, of which waited for: 4 -> 16; matrix products, arithmetic and copies ran while one was open for 10% -> 10% of each run, Pallas kernels for 0% -> 8%
where the time goes in v1:
time: 207 us
  waiting for transfers between devices  84.4 us (41%)
  starting transfers between devices  69.8 us (34%)
  Pallas kernels  24.7 us (12%)
  other arithmetic  16.3 us (8%)
  local copies, waits for them, and re-layouts  10.1 us (5%)
    ppermute x45, waiting for transfers between devices, flip(): return lax.ppermute(value, AXES, pairs)  84.4 us
    ppermute x45, starting transfers between devices, flip(): return lax.ppermute(value, AXES, pairs)  69.8 us
    pallas_call x1, Pallas kernels, forward_terms(): pl.pallas_call(fwd_kernel, grid_spec=pltpu.PrefetchScalarGridSpec(num_sca...  9.37 us
    pallas_call x1, Pallas kernels, input_terms(): pl.pallas_call(da_kernel, grid_spec=pltpu.PrefetchScalarGridSpec(num_scal...  8.11 us
    pallas_call x1, Pallas kernels, weight_terms(): pl.pallas_call(dw_kernel, grid_spec=pltpu.PrefetchScalarGridSpec(num_scal...  7.24 us
  transfers between devices with their start and end apart: 45, of which 16 were waited for; matrix products, arithmetic and copies ran while one was open for 10% of the time, Pallas kernels for 8%

profile of v1, /device:TPU:1, one launch (start us, length us, event | category | flops | bytes accessed | tf_op | source)
XLA Modules:
  0.0 206.6 jit_solution(650989990210208170)
XLA Ops:
  0.7 1.1 constant_dynamic-slice_fusion
  1.8 1.5 collective-permute-start.11
  3.3 1.9 constant_dynamic-slice_fusion.3
  5.2 1.4 collective-permute-start.5
  7.3 0.9 broadcast_select_fusion.4
  8.2 2.6 %collective-permute-start.13 = (bf16[256,640]{1,0:T(8,128)(2,1)S(1)}, bf16[256,640]{1,0:T(8,128)(2,1)S(1)}, u32[]{:S(2)}, u32[]{:S(2)}) collective-permute-start(bf16[256,640]{1,0:T(8,128)(2,1)S(1)} %get-tuple-element.24), channel_id=1, source_target_pairs={{0,96},{1,97},{2,98},{3,99},{4,100},{5,101},{6,102},{7,103},{8,104... | collective-permute-start | bytes 983048 | tf_op jit(solution)/shard_map/ppermute | solution.py:21
  10.7 1.1 constant_dynamic-update-slice_fusion.4
  12.0 1.4 collective-permute-start.16
  13.4 5.6 %collective-permute-done.5 = bf16[512,512]{1,0:T(8,128)(2,1)} collective-permute-done((bf16[512,512]{1,0:T(8,128)(2,1)}, bf16[512,512]{1,0:T(8,128)(2,1)}, u32[]{:S(2)}, u32[]{:S(2)}) %collective-permute-start.5) | collective-permute-done | bytes 524320 | tf_op jit(solution)/shard_map/ppermute | solution.py:21
  19.0 3.0 %collective-permute-start.17 = (bf16[256,640]{1,0:T(8,128)(2,1)S(1)}, bf16[256,640]{1,0:T(8,128)(2,1)S(1)}, u32[]{:S(2)}, u32[]{:S(2)}) collective-permute-start(bf16[256,640]{1,0:T(8,128)(2,1)S(1)} %get-tuple-element.24), channel_id=1, source_target_pairs={{0,16},{1,17},{2,18},{3,19},{4,20},{5,21},{6,22},{7,23},{8,24},{9,... | collective-permute-start | bytes 983048 | tf_op jit(solution)/shard_map/ppermute | solution.py:21
  22.0 1.7 collective-permute-start.1
  23.8 2.2 %collective-permute-start.2 = (bf16[1024,256]{1,0:T(8,128)(2,1)S(1)}, bf16[1024,256]{1,0:T(8,128)(2,1)S(1)}, u32[]{:S(2)}, u32[]{:S(2)}) collective-permute-start(bf16[1024,256]{1,0:T(8,128)(2,1)S(1)} %pad_maximum_fusion.6), channel_id=1, source_target_pairs={{0,3},{1,2},{2,1},{3,0},{4,7},{5,6},{6,5},{7,4},{8,11},{9,10},{10,... | collective-permute-start | bytes 1572872 | tf_op jit(solution)/shard_map/ppermute | solution.py:21
  26.0 1.1 constant_dynamic-slice_fusion.2
  27.1 12.8 %collective-permute-done.16 = bf16[256,640]{1,0:T(8,128)(2,1)S(1)} collective-permute-done((bf16[256,640]{1,0:T(8,128)(2,1)}, bf16[256,640]{1,0:T(8,128)(2,1)S(1)}, u32[]{:S(2)}, u32[]{:S(2)}) %collective-permute-start.16) | collective-permute-done | bytes 327712 | tf_op jit(solution)/shard_map/ppermute | solution.py:21
  40.0 2.8 %collective-permute-start.18 = (bf16[256,640]{1,0:T(8,128)(2,1)}, bf16[256,640]{1,0:T(8,128)(2,1)S(1)}, u32[]{:S(2)}, u32[]{:S(2)}) collective-permute-start(bf16[256,640]{1,0:T(8,128)(2,1)} %get-tuple-element.23), channel_id=1, source_target_pairs={{0,20},{1,21},{2,22},{3,23},{4,16},{5,17},{6,18},{7,19},{8,28},{9,... | collective-permute-start | bytes 983048 | tf_op jit(solution)/shard_map/ppermute | solution.py:21
  42.8 6.7 %collective-permute-done.17 = bf16[256,640]{1,0:T(8,128)(2,1)S(1)} collective-permute-done((bf16[256,640]{1,0:T(8,128)(2,1)S(1)}, bf16[256,640]{1,0:T(8,128)(2,1)S(1)}, u32[]{:S(2)}, u32[]{:S(2)}) %collective-permute-start.17) | collective-permute-done | bytes 327712 | tf_op jit(solution)/shard_map/ppermute | solution.py:21
  49.6 0.9 collective-permute-start.6
  50.5 2.6 %collective-permute-start.15 = (bf16[128,640]{1,0:T(8,128)(2,1)S(1)}, bf16[128,640]{1,0:T(8,128)(2,1)S(1)}, u32[]{:S(2)}, u32[]{:S(2)}) collective-permute-start(bf16[128,640]{1,0:T(8,128)(2,1)S(1)} %slice.161), channel_id=1, source_target_pairs={{0,96},{1,97},{2,98},{3,99},{4,100},{5,101},{6,102},{7,103},{8,104... | collective-permute-start | bytes 491528 | tf_op jit(solution)/shard_map/ppermute | solution.py:21
  53.1 1.2 constant_dynamic-update-slice_fusion.3
  54.3 2.6 %collective-permute-done.18 = bf16[256,640]{1,0:T(8,128)(2,1)S(1)} collective-permute-done((bf16[256,640]{1,0:T(8,128)(2,1)}, bf16[256,640]{1,0:T(8,128)(2,1)S(1)}, u32[]{:S(2)}, u32[]{:S(2)}) %collective-permute-start.18) | collective-permute-done | bytes 327712 | tf_op jit(solution)/shard_map/ppermute | solution.py:21
  56.9 1.2 collective-permute-start.14
  58.2 3.8 %collective-permute-start.4 = (bf16[512,256]{1,0:T(8,128)(2,1)S(1)}, bf16[512,256]{1,0:T(8,128)(2,1)S(1)}, u32[]{:S(2)}, u32[]{:S(2)}) collective-permute-start(bf16[512,256]{1,0:T(8,128)(2,1)S(1)} %slice.157), channel_id=1, source_target_pairs={{0,3},{1,2},{2,1},{3,0},{4,7},{5,6},{6,5},{7,4},{8,11},{9,10},{10,... | collective-permute-start | bytes 786440 | tf_op jit(solution)/shard_map/ppermute | solution.py:21
  62.2 1.1 collective-permute-start.26
  63.4 1.8 collective-permute-start.7
  65.2 0.7 collective-permute-start.8
  65.9 2.0 collective-permute-done.4
  67.9 1.8 collective-permute-start.20
  70.3 9.7 %collective-permute-done.7 = bf16[1024,256]{1,0:T(8,128)(2,1)S(1)} collective-permute-done((bf16[1024,256]{1,0:T(8,128)(2,1)S(1)}, bf16[1024,256]{1,0:T(8,128)(2,1)S(1)}, u32[]{:S(2)}, u32[]{:S(2)}) %collective-permute-start.7) | collective-permute-done | bytes 524320 | tf_op jit(solution)/shard_map/ppermute | solution.py:21
  80.7 6.5 %collective-permute-done.10 = bf16[512,256]{1,0:T(8,128)(2,1)S(1)} collective-permute-done((bf16[512,256]{1,0:T(8,128)(2,1)S(1)}, bf16[512,256]{1,0:T(8,128)(2,1)S(1)}, u32[]{:S(2)}, u32[]{:S(2)}) %collective-permute-start.10) | collective-permute-done | bytes 262176 | tf_op jit(solution)/shard_map/ppermute | solution.py:21
  87.3 3.1 %collective-permute-done.19 = bf16[768,640]{1,0:T(8,128)(2,1)S(1)} collective-permute-done((bf16[768,640]{1,0:T(8,128)(2,1)S(1)}, bf16[768,640]{1,0:T(8,128)(2,1)S(1)}, u32[]{:S(2)}, u32[]{:S(2)}) %collective-permute-start.19) | collective-permute-done | bytes 983072 | tf_op jit(solution)/shard_map/ppermute | solution.py:21
  91.2 7.2 %weight_terms.1 = bf16[8,256,1280]{2,1,0:T(8,128)(2,1)S(1)} custom-call(s32[1]{0:T(128)} %bitcast.m, bf16[8,1024,256]{2,1,0:T(8,128)(2,1)S(1)} %bitcast_dynamic-update-slice_fusion.a0.a1.a, bf16[1024,1280]{1,0:T(8,128)(2,1)S(1)} %pad_maximum_fusion.1.g), custom_call_target="tpu_custom_call" | custom-call | tf_op jit(solution)/shard_map/weight_terms/pallas_call | solution.py:55
  98.5 2.2 %collective-permute-done.22 = bf16[384,640]{1,0:T(8,128)(2,1)S(1)} collective-permute-done((bf16[384,640]{1,0:T(8,128)(2,1)S(1)}, bf16[384,640]{1,0:T(8,128)(2,1)S(1)}, u32[]{:S(2)}, u32[]{:S(2)}) %collective-permute-start.22) | collective-permute-done | bytes 491552 | tf_op jit(solution)/shard_map/ppermute | solution.py:21
  100.8 0.6 pad_maximum_fusion.w2
  101.4 8.1 %input_terms.1 = bf16[8,1024,256]{2,1,0:T(8,128)(2,1)S(1)} custom-call(s32[1]{0:T(128)} %bitcast.m, bf16[1024,1280]{1,0:T(8,128)(2,1)S(1)} %pad_maximum_fusion.1.g, bf16[4,256,640]{2,1,0:T(8,128)(2,1)S(1)} %pad_maximum_fusion.2.w1, bf16[4,3,256,640]{3,2,1,0:T(8,128)(2,1)S(1)} %pad_maximum_fusion.w2), custom_call_target="tpu_custom_call" | custom-call | tf_op jit(solution)/shard_map/input_terms/pallas_call | solution.py:92
  109.6 1.4 slice_bitcast_fusion.14
  111.0 1.9 collective-permute-start.30
  112.9 1.2 slice_bitcast_fusion.6
  114.1 1.5 collective-permute-start.35
  115.6 1.3 collective-permute-start.38
  116.9 9.4 %forward_terms.1 = bf16[1024,1280]{1,0:T(8,128)(2,1)S(1)} custom-call(s32[1]{0:T(128)} %bitcast.m, bf16[8,1024,256]{2,1,0:T(8,128)(2,1)S(1)} %bitcast_dynamic-update-slice_fusion.a0.a1.a, bf16[8,1024,256]{2,1,0:T(8,128)(2,1)S(1)} %bitcast_dynamic-update-slice_fusion.a0.a1.a, bf16[4,256,640]{2,1,0:T(8,128)(2,1)S(1)} %pad_maximum_fusion.2.w1, ...), custom_call_target="tpu_custom_call" | custom-call | tf_op jit(solution)/shard_map/forward_terms/pallas_call | solution.py:137
  126.4 6.2 %collective-permute-start.23 = (bf16[512,1280]{1,0:T(8,128)(2,1)S(1)}, bf16[512,1280]{1,0:T(8,128)(2,1)S(1)}, u32[]{:S(2)}, u32[]{:S(2)}) collective-permute-start(bf16[512,1280]{1,0:T(8,128)(2,1)S(1)} %slice.165), channel_id=1, source_target_pairs={{0,8},{1,9},{2,10},{3,11},{4,12},{5,13},{6,14},{7,15},{8,0},{9,1},... | collective-permute-start | bytes 3932168 | tf_op jit(solution)/shard_map/ppermute | solution.py:21
  133.3 2.5 %fusion.9 = (bf16[1024,256]{1,0:T(8,128)(2,1)}, bf16[1024,256]{1,0:T(8,128)(2,1)}) fusion(bf16[1024,256]{1,0:T(8,128)(2,1)} %collective-permute-done.28, bf16[8,1024,256]{2,1,0:T(8,128)(2,1)S(1)} %input_terms.1, bf16[1024,256]{1,0:T(8,128)(2,1)} %collective-permute-done.30), kind=kLoop, calls=%fused_computation.26 | loop fusion | flops 2097152 | bytes 3145728 | tf_op jit(solution)/shard_map/convert_element_type | solution.py:45
  135.7 0.6 collective-permute-start.31
  136.3 1.0 fusion.4
  137.3 8.9 %collective-permute-done.32 = bf16[1024,256]{1,0:T(8,128)(2,1)} collective-permute-done((bf16[1024,256]{1,0:T(8,128)(2,1)S(1)}, bf16[1024,256]{1,0:T(8,128)(2,1)}, u32[]{:S(2)}, u32[]{:S(2)}) %collective-permute-start.32) | collective-permute-done | bytes 524320 | tf_op jit(solution)/shard_map/ppermute | solution.py:21
  146.2 1.1 collective-permute-start.37
  147.3 0.7 collective-permute-done.31
  148.0 1.3 collective-permute-start.40
  149.3 1.5 fusion.8
  151.0 2.5 %collective-permute-start.29 = (bf16[1024,256]{1,0:T(8,128)(2,1)S(1)}, bf16[1024,256]{1,0:T(8,128)(2,1)S(1)}, u32[]{:S(2)}, u32[]{:S(2)}) collective-permute-start(bf16[1024,256]{1,0:T(8,128)(2,1)S(1)} %copy-done.8), channel_id=1, source_target_pairs={{0,3},{1,2},{2,1},{3,0},{4,7},{5,6},{6,5},{7,4},{8,11},{9,10},{10,... | collective-permute-start | bytes 1572872 | tf_op jit(solution)/shard_map/ppermute | solution.py:21
  153.4 8.3 %collective-permute-done.37 = bf16[256,1280]{1,0:T(8,128)(2,1)} collective-permute-done((bf16[256,1280]{1,0:T(8,128)(2,1)}, bf16[256,1280]{1,0:T(8,128)(2,1)}, u32[]{:S(2)}, u32[]{:S(2)}) %collective-permute-start.37) | collective-permute-done | bytes 655392 | tf_op jit(solution)/shard_map/ppermute | solution.py:21
  161.8 2.2 %fusion.5 = (f32[256,1280]{1,0:T(8,128)S(1)}, bf16[256,1280]{1,0:T(8,128)(2,1)S(1)}) fusion(bf16[256,1280]{1,0:T(8,128)(2,1)} %collective-permute-done.37, bf16[256,1280]{1,0:T(8,128)(2,1)} %collective-permute-done.35, bf16[8,256,1280]{2,1,0:T(8,128)(2,1)} %copy-done, bf16[256,1280]{1,0:T(8,128)(2,1)} %collective-permute-done.38), kind=kLoop, calls=%fused_computation.16 | loop fusion | flops 2949120 | bytes 5242880 | tf_op jit(solution)/shard_map/add | solution.py:27
  164.6 1.5 collective-permute-start.42
  166.3 3.8 %collective-permute-done.33 = bf16[1024,256]{1,0:T(8,128)(2,1)S(1)} collective-permute-done((bf16[1024,256]{1,0:T(8,128)(2,1)S(1)}, bf16[1024,256]{1,0:T(8,128)(2,1)S(1)}, u32[]{:S(2)}, u32[]{:S(2)}) %collective-permute-start.33) | collective-permute-done | bytes 524320 | tf_op jit(solution)/shard_map/ppermute | solution.py:21
  170.1 1.4 broadcast_select_fusion.1
  171.6 12.3 %collective-permute-start.34 = (bf16[512,512]{1,0:T(8,128)(2,1)S(1)}, bf16[512,512]{1,0:T(8,128)(2,1)S(1)}, u32[]{:S(2)}, u32[]{:S(2)}) collective-permute-start(bf16[512,512]{1,0:T(8,128)(2,1)S(1)} %pad_maximum_fusion.5), channel_id=1, source_target_pairs={{0,8},{1,9},{2,10},{3,11},{4,12},{5,13},{6,14},{7,15},{8,0},{9,1},... | collective-permute-start | bytes 1572872 | tf_op jit(solution)/shard_map/ppermute | solution.py:21
  183.9 1.4 fusion.3
  185.5 1.6 collective-permute-start.41
  187.1 3.5 %collective-permute-done.24 = bf16[512,640]{1,0:T(8,128)(2,1)S(1)} collective-permute-done((bf16[512,640]{1,0:T(8,128)(2,1)S(1)}, bf16[512,640]{1,0:T(8,128)(2,1)S(1)}, u32[]{:S(2)}, u32[]{:S(2)}) %collective-permute-start.24) | collective-permute-done | bytes 655392 | tf_op jit(solution)/shard_map/ppermute | solution.py:21
  190.5 1.0 fusion
  191.8 7.7 %collective-permute-done.43 = bf16[256,640]{1,0:T(8,128)(2,1)S(1)} collective-permute-done((bf16[256,640]{1,0:T(8,128)(2,1)S(1)}, bf16[256,640]{1,0:T(8,128)(2,1)S(1)}, u32[]{:S(2)}, u32[]{:S(2)}) %collective-permute-start.43) | collective-permute-done | bytes 327712 | tf_op jit(solution)/shard_map/ppermute | solution.py:21
  199.7 4.5 %collective-permute-start.44 = (bf16[256,640]{1,0:T(8,128)(2,1)S(1)}, bf16[256,640]{1,0:T(8,128)(2,1)S(1)}, u32[]{:S(2)}, u32[]{:S(2)}) collective-permute-start(bf16[256,640]{1,0:T(8,128)(2,1)S(1)} %get-tuple-element.18), channel_id=1, source_target_pairs={{0,8},{1,9},{2,10},{3,11},{4,12},{5,13},{6,14},{7,15},{8,0},{9,1},... | collective-permute-start | bytes 983048 | tf_op jit(solution)/shard_map/ppermute | solution.py:21
  204.2 1.1 pad_maximum_fusion.3
  205.4 1.1 maximum_select_fusion
  (105 shorter events, 5.6 us)
Async XLA Ops:
  0.6 6.7 %copy-start.7 = (bf16[512,640]{1,0:T(8,128)(2,1)S(1)}, bf16[512,640]{1,0:T(8,128)(2,1)}, u32[]{:S(2)}) copy-start(bf16[512,640]{1,0:T(8,128)(2,1)} %param.4) | copy-start | bytes 1966084
  0.6 5.9 %copy-start.4 = (bf16[512,1024]{1,0:T(8,128)(2,1)S(1)}, bf16[512,1024]{1,0:T(8,128)(2,1)}, u32[]{:S(2)}) copy-start(bf16[512,1024]{1,0:T(8,128)(2,1)} %param.3) | copy-start | bytes 3145732
  1.8 5.5 %collective-permute-start.11 = (bf16[256,640]{1,0:T(8,128)(2,1)S(1)}, bf16[256,640]{1,0:T(8,128)(2,1)S(1)}, u32[]{:S(2)}, u32[]{:S(2)}) collective-permute-start(bf16[256,640]{1,0:T(8,128)(2,1)S(1)} %constant_dynamic-slice_fusion), channel_id=1, source_target_pairs={{0,8},{1,9},{2,10},{3,11},{4,12},{5,13},{6,14},{7,15},{8,0},{9,1},... | collective-permute-start | bytes 983048 | tf_op jit(solution)/shard_map/ppermute | solution.py:21
  5.2 13.8 %collective-permute-start.5 = (bf16[512,512]{1,0:T(8,128)(2,1)}, bf16[512,512]{1,0:T(8,128)(2,1)}, u32[]{:S(2)}, u32[]{:S(2)}) collective-permute-start(bf16[512,512]{1,0:T(8,128)(2,1)} %constant_dynamic-slice_fusion.3), channel_id=1, source_target_pairs={{0,4},{1,5},{2,6},{3,7},{4,0},{5,1},{6,2},{7,3},{8,12},{9,13},{10,... | collective-permute-start | bytes 1572872 | tf_op jit(solution)/shard_map/ppermute | solution.py:21
  6.8 5.2 %collective-permute-start = (bf16[512,256]{1,0:T(8,128)(2,1)S(1)}, bf16[512,256]{1,0:T(8,128)(2,1)S(1)}, u32[]{:S(2)}, u32[]{:S(2)}) collective-permute-start(bf16[512,256]{1,0:T(8,128)(2,1)S(1)} %get-tuple-element.22), channel_id=1, source_target_pairs={{0,8},{1,9},{2,10},{3,11},{4,12},{5,13},{6,14},{7,15},{8,0},{9,1},... | collective-permute-start | bytes 786440 | tf_op jit(solution)/shard_map/ppermute | solution.py:21
  7.2 43.3 %collective-permute-start.25 = (bf16[512,640]{1,0:T(8,128)(2,1)}, bf16[512,640]{1,0:T(8,128)(2,1)}, u32[]{:S(2)}, u32[]{:S(2)}) collective-permute-start(bf16[512,640]{1,0:T(8,128)(2,1)} %param.5), channel_id=1, source_target_pairs={{0,4},{1,5},{2,6},{3,7},{4,0},{5,1},{6,2},{7,3},{8,12},{9,13},{10,... | collective-permute-start | bytes 1966088 | tf_op jit(solution)/shard_map/ppermute | solution.py:21
  8.2 13.9 %collective-permute-start.13 = (bf16[256,640]{1,0:T(8,128)(2,1)S(1)}, bf16[256,640]{1,0:T(8,128)(2,1)S(1)}, u32[]{:S(2)}, u32[]{:S(2)}) collective-permute-start(bf16[256,640]{1,0:T(8,128)(2,1)S(1)} %get-tuple-element.24), channel_id=1, source_target_pairs={{0,96},{1,97},{2,98},{3,99},{4,100},{5,101},{6,102},{7,103},{8,104... | collective-permute-start | bytes 983048 | tf_op jit(solution)/shard_map/ppermute | solution.py:21
  10.7 13.0 %collective-permute-start.12 = (bf16[256,640]{1,0:T(8,128)(2,1)S(1)}, bf16[256,640]{1,0:T(8,128)(2,1)S(1)}, u32[]{:S(2)}, u32[]{:S(2)}) collective-permute-start(bf16[256,640]{1,0:T(8,128)(2,1)S(1)} %get-tuple-element.24), channel_id=1, source_target_pairs={{0,32},{1,33},{2,34},{3,35},{4,36},{5,37},{6,38},{7,39},{8,40},{9,... | collective-permute-start | bytes 983048 | tf_op jit(solution)/shard_map/ppermute | solution.py:21
  12.0 28.0 %collective-permute-start.16 = (bf16[256,640]{1,0:T(8,128)(2,1)}, bf16[256,640]{1,0:T(8,128)(2,1)S(1)}, u32[]{:S(2)}, u32[]{:S(2)}) collective-permute-start(bf16[256,640]{1,0:T(8,128)(2,1)} %get-tuple-element.23), channel_id=1, source_target_pairs={{0,4},{1,5},{2,6},{3,7},{4,0},{5,1},{6,2},{7,3},{8,12},{9,13},{10,... | collective-permute-start | bytes 983048 | tf_op jit(solution)/shard_map/ppermute | solution.py:21
  19.0 30.6 %collective-permute-start.17 = (bf16[256,640]{1,0:T(8,128)(2,1)S(1)}, bf16[256,640]{1,0:T(8,128)(2,1)S(1)}, u32[]{:S(2)}, u32[]{:S(2)}) collective-permute-start(bf16[256,640]{1,0:T(8,128)(2,1)S(1)} %get-tuple-element.24), channel_id=1, source_target_pairs={{0,16},{1,17},{2,18},{3,19},{4,20},{5,21},{6,22},{7,23},{8,24},{9,... | collective-permute-start | bytes 983048 | tf_op jit(solution)/shard_map/ppermute | solution.py:21
  22.0 36.1 %collective-permute-start.1 = (bf16[1024,256]{1,0:T(8,128)(2,1)S(1)}, bf16[1024,256]{1,0:T(8,128)(2,1)S(1)}, u32[]{:S(2)}, u32[]{:S(2)}) collective-permute-start(bf16[1024,256]{1,0:T(8,128)(2,1)S(1)} %pad_maximum_fusion.6), channel_id=1, source_target_pairs={{0,1},{1,0},{2,3},{3,2},{4,5},{5,4},{6,7},{7,6},{8,9},{9,8},{10,11... | collective-permute-start | bytes 1572872 | tf_op jit(solution)/shard_map/ppermute | solution.py:21
  23.8 30.5 %copy-start.5 = (bf16[256,640]{1,0:T(8,128)(2,1)}, bf16[256,640]{1,0:T(8,128)(2,1)S(1)}, u32[]{:S(2)}) copy-start(bf16[256,640]{1,0:T(8,128)(2,1)S(1)} %collective-permute-done.12) | copy-start | bytes 983044
  23.8 38.2 %collective-permute-start.2 = (bf16[1024,256]{1,0:T(8,128)(2,1)S(1)}, bf16[1024,256]{1,0:T(8,128)(2,1)S(1)}, u32[]{:S(2)}, u32[]{:S(2)}) collective-permute-start(bf16[1024,256]{1,0:T(8,128)(2,1)S(1)} %pad_maximum_fusion.6), channel_id=1, source_target_pairs={{0,3},{1,2},{2,1},{3,0},{4,7},{5,6},{6,5},{7,4},{8,11},{9,10},{10,... | collective-permute-start | bytes 1572872 | tf_op jit(solution)/shard_map/ppermute | solution.py:21
  40.0 16.9 %collective-permute-start.18 = (bf16[256,640]{1,0:T(8,128)(2,1)}, bf16[256,640]{1,0:T(8,128)(2,1)S(1)}, u32[]{:S(2)}, u32[]{:S(2)}) collective-permute-start(bf16[256,640]{1,0:T(8,128)(2,1)} %get-tuple-element.23), channel_id=1, source_target_pairs={{0,20},{1,21},{2,22},{3,23},{4,16},{5,17},{6,18},{7,19},{8,28},{9,... | collective-permute-start | bytes 983048 | tf_op jit(solution)/shard_map/ppermute | solution.py:21
  49.6 12.6 %collective-permute-start.6 = (bf16[512,256]{1,0:T(8,128)(2,1)S(1)}, bf16[512,256]{1,0:T(8,128)(2,1)S(1)}, u32[]{:S(2)}, u32[]{:S(2)}) collective-permute-start(bf16[512,256]{1,0:T(8,128)(2,1)S(1)} %get-tuple-element.32), channel_id=1, source_target_pairs={{0,8},{1,9},{2,10},{3,11},{4,12},{5,13},{6,14},{7,15},{8,0},{9,1},... | collective-permute-start | bytes 786440 | tf_op jit(solution)/shard_map/ppermute | solution.py:21
  50.5 12.8 %collective-permute-start.15 = (bf16[128,640]{1,0:T(8,128)(2,1)S(1)}, bf16[128,640]{1,0:T(8,128)(2,1)S(1)}, u32[]{:S(2)}, u32[]{:S(2)}) collective-permute-start(bf16[128,640]{1,0:T(8,128)(2,1)S(1)} %slice.161), channel_id=1, source_target_pairs={{0,96},{1,97},{2,98},{3,99},{4,100},{5,101},{6,102},{7,103},{8,104... | collective-permute-start | bytes 491528 | tf_op jit(solution)/shard_map/ppermute | solution.py:21
  56.9 13.2 %copy-start.6 = (bf16[256,640]{1,0:T(8,128)(2,1)S(1)}, bf16[256,640]{1,0:T(8,128)(2,1)}, u32[]{:S(2)}) copy-start(bf16[256,640]{1,0:T(8,128)(2,1)} %copy-done.5) | copy-start | bytes 983044
  56.9 8.3 %collective-permute-start.14 = (bf16[128,640]{1,0:T(8,128)(2,1)S(1)}, bf16[128,640]{1,0:T(8,128)(2,1)S(1)}, u32[]{:S(2)}, u32[]{:S(2)}) collective-permute-start(bf16[128,640]{1,0:T(8,128)(2,1)S(1)} %slice.160), channel_id=1, source_target_pairs={{0,32},{1,33},{2,34},{3,35},{4,36},{5,37},{6,38},{7,39},{8,40},{9,... | collective-permute-start | bytes 491528 | tf_op jit(solution)/shard_map/ppermute | solution.py:21
  58.2 9.8 %collective-permute-start.4 = (bf16[512,256]{1,0:T(8,128)(2,1)S(1)}, bf16[512,256]{1,0:T(8,128)(2,1)S(1)}, u32[]{:S(2)}, u32[]{:S(2)}) collective-permute-start(bf16[512,256]{1,0:T(8,128)(2,1)S(1)} %slice.157), channel_id=1, source_target_pairs={{0,3},{1,2},{2,1},{3,0},{4,7},{5,6},{6,5},{7,4},{8,11},{9,10},{10,... | collective-permute-start | bytes 786440 | tf_op jit(solution)/shard_map/ppermute | solution.py:21
  62.0 7.7 %collective-permute-start.3 = (bf16[512,256]{1,0:T(8,128)(2,1)S(1)}, bf16[512,256]{1,0:T(8,128)(2,1)S(1)}, u32[]{:S(2)}, u32[]{:S(2)}) collective-permute-start(bf16[512,256]{1,0:T(8,128)(2,1)S(1)} %slice.156), channel_id=1, source_target_pairs={{0,1},{1,0},{2,3},{3,2},{4,5},{5,4},{6,7},{7,6},{8,9},{9,8},{10,11... | collective-permute-start | bytes 786440 | tf_op jit(solution)/shard_map/ppermute | solution.py:21
  62.2 28.9 %collective-permute-start.26 = (bf16[512,1280]{1,0:T(8,128)(2,1)S(1)}, bf16[512,1280]{1,0:T(8,128)(2,1)S(1)}, u32[]{:S(2)}, u32[]{:S(2)}) collective-permute-start(bf16[512,1280]{1,0:T(8,128)(2,1)S(1)} %constant_dynamic-update-slice_fusion.3), channel_id=1, source_target_pairs={{0,8},{1,9},{2,10},{3,11},{4,12},{5,13},{6,14},{7,15},{8,0},{9,1},... | collective-permute-start | bytes 3932168 | tf_op jit(solution)/shard_map/ppermute | solution.py:21
  63.4 16.7 %collective-permute-start.7 = (bf16[1024,256]{1,0:T(8,128)(2,1)S(1)}, bf16[1024,256]{1,0:T(8,128)(2,1)S(1)}, u32[]{:S(2)}, u32[]{:S(2)}) collective-permute-start(bf16[1024,256]{1,0:T(8,128)(2,1)S(1)} %pad_maximum_fusion.7), channel_id=1, source_target_pairs={{0,1},{1,0},{2,3},{3,2},{4,5},{5,4},{6,7},{7,6},{8,9},{9,8},{10,11... | collective-permute-start | bytes 1572872 | tf_op jit(solution)/shard_map/ppermute | solution.py:21
  65.2 15.4 %collective-permute-start.8 = (bf16[1024,256]{1,0:T(8,128)(2,1)S(1)}, bf16[1024,256]{1,0:T(8,128)(2,1)S(1)}, u32[]{:S(2)}, u32[]{:S(2)}) collective-permute-start(bf16[1024,256]{1,0:T(8,128)(2,1)S(1)} %pad_maximum_fusion.7), channel_id=1, source_target_pairs={{0,3},{1,2},{2,1},{3,0},{4,7},{5,6},{6,5},{7,4},{8,11},{9,10},{10,... | collective-permute-start | bytes 1572872 | tf_op jit(solution)/shard_map/ppermute | solution.py:21
  67.9 22.6 %collective-permute-start.20 = (bf16[768,640]{1,0:T(8,128)(2,1)S(1)}, bf16[768,640]{1,0:T(8,128)(2,1)S(1)}, u32[]{:S(2)}, u32[]{:S(2)}) collective-permute-start(bf16[768,640]{1,0:T(8,128)(2,1)S(1)} %constant_dynamic-update-slice_fusion), channel_id=1, source_target_pairs={{0,96},{1,97},{2,98},{3,99},{4,100},{5,101},{6,102},{7,103},{8,104... | collective-permute-start | bytes 2949128 | tf_op jit(solution)/shard_map/ppermute | solution.py:21
  69.7 20.6 %collective-permute-start.19 = (bf16[768,640]{1,0:T(8,128)(2,1)S(1)}, bf16[768,640]{1,0:T(8,128)(2,1)S(1)}, u32[]{:S(2)}, u32[]{:S(2)}) collective-permute-start(bf16[768,640]{1,0:T(8,128)(2,1)S(1)} %constant_dynamic-update-slice_fusion), channel_id=1, source_target_pairs={{0,32},{1,33},{2,34},{3,35},{4,36},{5,37},{6,38},{7,39},{8,40},{9,... | collective-permute-start | bytes 2949128 | tf_op jit(solution)/shard_map/ppermute | solution.py:21
  80.1 7.1 %collective-permute-start.10 = (bf16[512,256]{1,0:T(8,128)(2,1)S(1)}, bf16[512,256]{1,0:T(8,128)(2,1)S(1)}, u32[]{:S(2)}, u32[]{:S(2)}) collective-permute-start(bf16[512,256]{1,0:T(8,128)(2,1)S(1)} %slice.159), channel_id=1, source_target_pairs={{0,3},{1,2},{2,1},{3,0},{4,7},{5,6},{6,5},{7,4},{8,11},{9,10},{10,... | collective-permute-start | bytes 786440 | tf_op jit(solution)/shard_map/ppermute | solution.py:21
  80.6 6.7 %collective-permute-start.9 = (bf16[512,256]{1,0:T(8,128)(2,1)S(1)}, bf16[512,256]{1,0:T(8,128)(2,1)S(1)}, u32[]{:S(2)}, u32[]{:S(2)}) collective-permute-start(bf16[512,256]{1,0:T(8,128)(2,1)S(1)} %slice.158), channel_id=1, source_target_pairs={{0,1},{1,0},{2,3},{3,2},{4,5},{5,4},{6,7},{7,6},{8,9},{9,8},{10,11... | collective-permute-start | bytes 786440 | tf_op jit(solution)/shard_map/ppermute | solution.py:21
  90.4 10.3 %collective-permute-start.22 = (bf16[384,640]{1,0:T(8,128)(2,1)S(1)}, bf16[384,640]{1,0:T(8,128)(2,1)S(1)}, u32[]{:S(2)}, u32[]{:S(2)}) collective-permute-start(bf16[384,640]{1,0:T(8,128)(2,1)S(1)} %slice.163), channel_id=1, source_target_pairs={{0,96},{1,97},{2,98},{3,99},{4,100},{5,101},{6,102},{7,103},{8,104... | collective-permute-start | bytes 1474568 | tf_op jit(solution)/shard_map/ppermute | solution.py:21
  90.6 10.1 %collective-permute-start.21 = (bf16[384,640]{1,0:T(8,128)(2,1)S(1)}, bf16[384,640]{1,0:T(8,128)(2,1)S(1)}, u32[]{:S(2)}, u32[]{:S(2)}) collective-permute-start(bf16[384,640]{1,0:T(8,128)(2,1)S(1)} %slice.162), channel_id=1, source_target_pairs={{0,32},{1,33},{2,34},{3,35},{4,36},{5,37},{6,38},{7,39},{8,40},{9,... | collective-permute-start | bytes 1474568 | tf_op jit(solution)/shard_map/ppermute | solution.py:21
  98.5 37.9 %copy-start = (bf16[8,256,1280]{2,1,0:T(8,128)(2,1)}, bf16[8,256,1280]{2,1,0:T(8,128)(2,1)S(1)}, u32[]{:S(2)}) copy-start(bf16[8,256,1280]{2,1,0:T(8,128)(2,1)S(1)} %weight_terms.1) | copy-start | bytes 15728644
  109.6 23.7 %copy-start.1 = (bf16[8,1024,256]{2,1,0:T(8,128)(2,1)}, bf16[8,1024,256]{2,1,0:T(8,128)(2,1)S(1)}, u32[]{:S(2)}) copy-start(bf16[8,1024,256]{2,1,0:T(8,128)(2,1)S(1)} %input_terms.1) | copy-start | bytes 12582916
  111.0 15.4 %collective-permute-start.28 = (bf16[1024,256]{1,0:T(8,128)(2,1)}, bf16[1024,256]{1,0:T(8,128)(2,1)}, u32[]{:S(2)}, u32[]{:S(2)}) collective-permute-start(bf16[1024,256]{1,0:T(8,128)(2,1)} %get-tuple-element.14), channel_id=1, source_target_pairs={{0,1},{1,0},{2,3},{3,2},{4,5},{5,4},{6,7},{7,6},{8,9},{9,8},{10,11... | collective-permute-start | bytes 1572872 | tf_op jit(solution)/shard_map/ppermute | solution.py:21
  111.0 21.7 %collective-permute-start.30 = (bf16[1024,256]{1,0:T(8,128)(2,1)}, bf16[1024,256]{1,0:T(8,128)(2,1)}, u32[]{:S(2)}, u32[]{:S(2)}) collective-permute-start(bf16[1024,256]{1,0:T(8,128)(2,1)} %get-tuple-element.13), channel_id=1, source_target_pairs={{0,3},{1,2},{2,1},{3,0},{4,7},{5,6},{6,5},{7,4},{8,11},{9,10},{10,... | collective-permute-start | bytes 1572872 | tf_op jit(solution)/shard_map/ppermute | solution.py:21
  114.1 21.6 %collective-permute-start.36 = (bf16[256,1280]{1,0:T(8,128)(2,1)S(1)}, bf16[256,1280]{1,0:T(8,128)(2,1)S(1)}, u32[]{:S(2)}, u32[]{:S(2)}) collective-permute-start(bf16[256,1280]{1,0:T(8,128)(2,1)S(1)} %get-tuple-element.10), channel_id=1, source_target_pairs={{0,32},{1,33},{2,34},{3,35},{4,36},{5,37},{6,38},{7,39},{8,40},{9,... | collective-permute-start | bytes 1966088 | tf_op jit(solution)/shard_map/ppermute | solution.py:21
  114.1 36.7 %collective-permute-start.35 = (bf16[256,1280]{1,0:T(8,128)(2,1)}, bf16[256,1280]{1,0:T(8,128)(2,1)}, u32[]{:S(2)}, u32[]{:S(2)}) collective-permute-start(bf16[256,1280]{1,0:T(8,128)(2,1)} %get-tuple-element.7), channel_id=1, source_target_pairs={{0,32},{1,33},{2,34},{3,35},{4,36},{5,37},{6,38},{7,39},{8,40},{9,... | collective-permute-start | bytes 1966088 | tf_op jit(solution)/shard_map/ppermute | solution.py:21
  115.6 35.3 %collective-permute-start.38 = (bf16[256,1280]{1,0:T(8,128)(2,1)}, bf16[256,1280]{1,0:T(8,128)(2,1)}, u32[]{:S(2)}, u32[]{:S(2)}) collective-permute-start(bf16[256,1280]{1,0:T(8,128)(2,1)} %get-tuple-element.9), channel_id=1, source_target_pairs={{0,96},{1,97},{2,98},{3,99},{4,100},{5,101},{6,102},{7,103},{8,104... | collective-permute-start | bytes 1966088 | tf_op jit(solution)/shard_map/ppermute | solution.py:21
  126.3 9.4 %copy-start.2 = (bf16[1024,1280]{1,0:T(8,128)(2,1)}, bf16[1024,1280]{1,0:T(8,128)(2,1)S(1)}, u32[]{:S(2)}) copy-start(bf16[1024,1280]{1,0:T(8,128)(2,1)S(1)} %forward_terms.1) | copy-start | bytes 7864324
  126.3 6.4 %copy-start.10 = (bf16[1024,256]{1,0:T(8,128)(2,1)S(1)}, bf16[1024,256]{1,0:T(8,128)(2,1)}, u32[]{:S(2)}) copy-start(bf16[1024,256]{1,0:T(8,128)(2,1)} %get-tuple-element.12) | copy-start | bytes 1572868
  126.4 37.7 %collective-permute-start.23 = (bf16[512,1280]{1,0:T(8,128)(2,1)S(1)}, bf16[512,1280]{1,0:T(8,128)(2,1)S(1)}, u32[]{:S(2)}, u32[]{:S(2)}) collective-permute-start(bf16[512,1280]{1,0:T(8,128)(2,1)S(1)} %slice.165), channel_id=1, source_target_pairs={{0,8},{1,9},{2,10},{3,11},{4,12},{5,13},{6,14},{7,15},{8,0},{9,1},... | collective-permute-start | bytes 3932168 | tf_op jit(solution)/shard_map/ppermute | solution.py:21
  132.7 13.5 %collective-permute-start.32 = (bf16[1024,256]{1,0:T(8,128)(2,1)S(1)}, bf16[1024,256]{1,0:T(8,128)(2,1)}, u32[]{:S(2)}, u32[]{:S(2)}) collective-permute-start(bf16[1024,256]{1,0:T(8,128)(2,1)S(1)} %copy-done.10), channel_id=1, source_target_pairs={{0,3},{1,2},{2,1},{3,0},{4,7},{5,6},{6,5},{7,4},{8,11},{9,10},{10,... | collective-permute-start | bytes 1572872 | tf_op jit(solution)/shard_map/ppermute | solution.py:21
  135.7 12.3 %collective-permute-start.31 = (bf16[1024,256]{1,0:T(8,128)(2,1)}, bf16[1024,256]{1,0:T(8,128)(2,1)}, u32[]{:S(2)}, u32[]{:S(2)}) collective-permute-start(bf16[1024,256]{1,0:T(8,128)(2,1)} %get-tuple-element.16), channel_id=1, source_target_pairs={{0,1},{1,0},{2,3},{3,2},{4,5},{5,4},{6,7},{7,6},{8,9},{9,8},{10,11... | collective-permute-start | bytes 1572872 | tf_op jit(solution)/shard_map/ppermute | solution.py:21
  146.2 15.6 %collective-permute-start.37 = (bf16[256,1280]{1,0:T(8,128)(2,1)}, bf16[256,1280]{1,0:T(8,128)(2,1)}, u32[]{:S(2)}, u32[]{:S(2)}) collective-permute-start(bf16[256,1280]{1,0:T(8,128)(2,1)} %fusion.4), channel_id=1, source_target_pairs={{0,96},{1,97},{2,98},{3,99},{4,100},{5,101},{6,102},{7,103},{8,104... | collective-permute-start | bytes 1966088 | tf_op jit(solution)/shard_map/ppermute | solution.py:21
  147.3 3.6 %copy-start.9 = (bf16[1024,256]{1,0:T(8,128)(2,1)S(1)}, bf16[1024,256]{1,0:T(8,128)(2,1)}, u32[]{:S(2)}) copy-start(bf16[1024,256]{1,0:T(8,128)(2,1)} %get-tuple-element.11) | copy-start | bytes 1572868
  147.3 3.7 %copy-start.8 = (bf16[1024,256]{1,0:T(8,128)(2,1)S(1)}, bf16[1024,256]{1,0:T(8,128)(2,1)}, u32[]{:S(2)}) copy-start(bf16[1024,256]{1,0:T(8,128)(2,1)} %get-tuple-element.15) | copy-start | bytes 1572868
  148.0 35.9 %collective-permute-start.40 = (bf16[256,1280]{1,0:T(8,128)(2,1)S(1)}, bf16[256,1280]{1,0:T(8,128)(2,1)S(1)}, u32[]{:S(2)}, u32[]{:S(2)}) collective-permute-start(bf16[256,1280]{1,0:T(8,128)(2,1)S(1)} %get-tuple-element.8), channel_id=1, source_target_pairs={{0,96},{1,97},{2,98},{3,99},{4,100},{5,101},{6,102},{7,103},{8,104... | collective-permute-start | bytes 1966088 | tf_op jit(solution)/shard_map/ppermute | solution.py:21
  150.8 13.8 %collective-permute-start.27 = (bf16[1024,256]{1,0:T(8,128)(2,1)S(1)}, bf16[1024,256]{1,0:T(8,128)(2,1)S(1)}, u32[]{:S(2)}, u32[]{:S(2)}) collective-permute-start(bf16[1024,256]{1,0:T(8,128)(2,1)S(1)} %copy-done.9), channel_id=1, source_target_pairs={{0,1},{1,0},{2,3},{3,2},{4,5},{5,4},{6,7},{7,6},{8,9},{9,8},{10,11... | collective-permute-start | bytes 1572872 | tf_op jit(solution)/shard_map/ppermute | solution.py:21
  151.0 13.2 %copy-start.3 = (bf16[1024,1280]{1,0:T(8,128)(2,1)S(1)}, bf16[1024,1280]{1,0:T(8,128)(2,1)}, u32[]{:S(2)}) copy-start(bf16[1024,1280]{1,0:T(8,128)(2,1)} %copy-done.2) | copy-start | bytes 7864324
  151.0 15.2 %collective-permute-start.29 = (bf16[1024,256]{1,0:T(8,128)(2,1)S(1)}, bf16[1024,256]{1,0:T(8,128)(2,1)S(1)}, u32[]{:S(2)}, u32[]{:S(2)}) collective-permute-start(bf16[1024,256]{1,0:T(8,128)(2,1)S(1)} %copy-done.8), channel_id=1, source_target_pairs={{0,3},{1,2},{2,1},{3,0},{4,7},{5,6},{6,5},{7,4},{8,11},{9,10},{10,... | collective-permute-start | bytes 1572872 | tf_op jit(solution)/shard_map/ppermute | solution.py:21
  161.8 8.3 %collective-permute-start.33 = (bf16[1024,256]{1,0:T(8,128)(2,1)S(1)}, bf16[1024,256]{1,0:T(8,128)(2,1)S(1)}, u32[]{:S(2)}, u32[]{:S(2)}) collective-permute-start(bf16[1024,256]{1,0:T(8,128)(2,1)S(1)} %fusion.8), channel_id=1, source_target_pairs={{0,4},{1,5},{2,6},{3,7},{4,0},{5,1},{6,2},{7,3},{8,12},{9,13},{10,... | collective-permute-start | bytes 1572872 | tf_op jit(solution)/shard_map/ppermute | solution.py:21
  164.1 19.8 %collective-permute-start.39 = (bf16[256,1280]{1,0:T(8,128)(2,1)S(1)}, bf16[256,1280]{1,0:T(8,128)(2,1)S(1)}, u32[]{:S(2)}, u32[]{:S(2)}) collective-permute-start(bf16[256,1280]{1,0:T(8,128)(2,1)S(1)} %get-tuple-element.6), channel_id=1, source_target_pairs={{0,32},{1,33},{2,34},{3,35},{4,36},{5,37},{6,38},{7,39},{8,40},{9,... | collective-permute-start | bytes 1966088 | tf_op jit(solution)/shard_map/ppermute | solution.py:21
  164.6 27.1 %collective-permute-start.42 = (bf16[256,640]{1,0:T(8,128)(2,1)S(1)}, bf16[256,640]{1,0:T(8,128)(2,1)S(1)}, u32[]{:S(2)}, u32[]{:S(2)}) collective-permute-start(bf16[256,640]{1,0:T(8,128)(2,1)S(1)} %slice.256), channel_id=1, source_target_pairs={{0,4},{1,5},{2,6},{3,7},{4,0},{5,1},{6,2},{7,3},{8,12},{9,13},{10,... | collective-permute-start | bytes 983048 | tf_op jit(solution)/shard_map/ppermute | solution.py:21
  166.2 24.4 %collective-permute-start.24 = (bf16[512,640]{1,0:T(8,128)(2,1)S(1)}, bf16[512,640]{1,0:T(8,128)(2,1)S(1)}, u32[]{:S(2)}, u32[]{:S(2)}) collective-permute-start(bf16[512,640]{1,0:T(8,128)(2,1)S(1)} %slice.255), channel_id=1, source_target_pairs={{0,4},{1,5},{2,6},{3,7},{4,0},{5,1},{6,2},{7,3},{8,12},{9,13},{10,... | collective-permute-start | bytes 1966088 | tf_op jit(solution)/shard_map/ppermute | solution.py:21
  171.6 20.0 %collective-permute-start.34 = (bf16[512,512]{1,0:T(8,128)(2,1)S(1)}, bf16[512,512]{1,0:T(8,128)(2,1)S(1)}, u32[]{:S(2)}, u32[]{:S(2)}) collective-permute-start(bf16[512,512]{1,0:T(8,128)(2,1)S(1)} %pad_maximum_fusion.5), channel_id=1, source_target_pairs={{0,8},{1,9},{2,10},{3,11},{4,12},{5,13},{6,14},{7,15},{8,0},{9,1},... | collective-permute-start | bytes 1572872 | tf_op jit(solution)/shard_map/ppermute | solution.py:21
  185.4 14.1 %collective-permute-start.43 = (bf16[256,640]{1,0:T(8,128)(2,1)S(1)}, bf16[256,640]{1,0:T(8,128)(2,1)S(1)}, u32[]{:S(2)}, u32[]{:S(2)}) collective-permute-start(bf16[256,640]{1,0:T(8,128)(2,1)S(1)} %get-tuple-element.26), channel_id=1, source_target_pairs={{0,20},{1,21},{2,22},{3,23},{4,16},{5,17},{6,18},{7,19},{8,28},{9,... | collective-permute-start | bytes 983048 | tf_op jit(solution)/shard_map/ppermute | solution.py:21
  185.5 14.0 %collective-permute-start.41 = (bf16[256,640]{1,0:T(8,128)(2,1)S(1)}, bf16[256,640]{1,0:T(8,128)(2,1)S(1)}, u32[]{:S(2)}, u32[]{:S(2)}) collective-permute-start(bf16[256,640]{1,0:T(8,128)(2,1)S(1)} %get-tuple-element.25), channel_id=1, source_target_pairs={{0,16},{1,17},{2,18},{3,19},{4,20},{5,21},{6,22},{7,23},{8,24},{9,... | collective-permute-start | bytes 983048 | tf_op jit(solution)/shard_map/ppermute | solution.py:21
  199.7 5.7 %collective-permute-start.44 = (bf16[256,640]{1,0:T(8,128)(2,1)S(1)}, bf16[256,640]{1,0:T(8,128)(2,1)S(1)}, u32[]{:S(2)}, u32[]{:S(2)}) collective-permute-start(bf16[256,640]{1,0:T(8,128)(2,1)S(1)} %get-tuple-element.18), channel_id=1, source_target_pairs={{0,8},{1,9},{2,10},{3,11},{4,12},{5,13},{6,14},{7,15},{8,0},{9,1},... | collective-permute-start | bytes 983048 | tf_op jit(solution)/shard_map/ppermute | solution.py:21

commit v2 on v0

v2 whole, which is shorter than its diff:
```python
import functools

import jax
import jax.numpy as jnp
from jax import lax
from jax.experimental import pallas as pl
from jax.experimental.pallas import tpu as pltpu
from jax.sharding import PartitionSpec as P

AXES = ("fsdp", "node")
BF16, F32 = jnp.bfloat16, jnp.float32
FAR = 2


def flip(value, x=0, y=0, z=0, c=0):
    pairs = []
    for i in range(128):
        p, q = divmod(i, 8)
        place = p // 4, (p // 2 % 2) * 2 + q // 4, q % 4, p % 2
        bits = [b if isinstance(b, int) else b[place[3]] for b in (x, y, z, c)]
        px, py, pz, pc = (a ^ b for a, b in zip(place, bits, strict=True))
        pairs.append((i, ((px * 2 + py // 2) * 2 + pc) * 8 + py % 2 * 4 + pz))
    return lax.ppermute(value, AXES, pairs)


ONE, TWO = (1, 3), (3, 1)


def tie(*values):
    return lax.optimization_barrier(values)


def add(*terms):
    total = terms[0].astype(F32)
    for term in terms[1:]:
        total = total + term.astype(F32)
    return total


def gather4(value, axis):
    one, two = flip(value, **{axis: ONE}), flip(value, **{axis: TWO})
    half = value.shape[0] // 2
    far = [flip(two[:half], **{axis: ONE}), flip(one[half:], **{axis: TWO})]
    return [value, one, jnp.concatenate(far, 0), two]


def scatter4(far_one, far_two, one, two, own, axis):
    got_one, got_two = flip(far_one, **{axis: ONE}), flip(far_two, **{axis: TWO})
    got_bottom1 = flip(add(one[0], got_two[0]).astype(BF16), **{axis: ONE})
    got_top2 = flip(add(two[0], got_one[0]).astype(BF16), **{axis: TWO})
    return add(own[0], got_one[1], got_top2), add(own[1], got_two[1], got_bottom1)


def pieces_of(top, bottom):
    return [[top(2), top(1)], [bottom(2), bottom(3)], [bottom(1)], [top(3)], [top(0), bottom(0)]]


def pick(k, values):
    chosen = values[0]
    for at in range(1, len(values)):
        chosen = jnp.where(k == at, values[at], chosen)
    return chosen


def cost(products):
    return pl.CostEstimate(flops=4 * products, bytes_accessed=products // 512, transcendentals=0)


def turned(slot, m):
    return slot ^ ((slot & 1) * m[1])


def a_block(xs, yh, m):
    i = (turned(xs, m) * 2 + yh) ^ m[0]
    return i // 4 * 4 + turned(i % 4, m)


def w_block(ylo, zs, m):
    i = (ylo * 4 + turned(zs, m)) ^ m[0]
    return turned(i // 2, m), i % 2


def sub_of(yh, ylo, m):
    return turned(yh * 2 + ylo, m)


def put(step, groups, outs, store):
    at = 0
    for group, out in zip(groups, outs, strict=True):
        for place in range(len(group)):

            @pl.when(step == at)
            def _():
                store(out.at[place])

            at += 1


def dw_kernel(groups, m, a, g, *outs):
    block = lax.dot_general(a[0], g[...], (((0,), (0,)), ((), ())), preferred_element_type=F32).astype(BF16)
    cols = block.shape[1] // 2

    def store(out):
        out[0] = block[:, :cols]
        out[1] = block[:, cols:]

    put(pl.program_id(0), groups, outs, store)


def weight_terms(scalars, a, g):
    _, t, d = a.shape
    cols = g.shape[1] // 2
    groups = pieces_of(lambda slot: (slot, 0), lambda slot: (slot, 1))
    blocks = sum(groups, [])

    def a_index(k, m):
        return (a_block(pick(k, [b[0] for b in blocks]), pick(k, [b[1] for b in blocks]), m), 0, 0)

    return pl.pallas_call(
        functools.partial(dw_kernel, groups),
        grid_spec=pltpu.PrefetchScalarGridSpec(
            num_scalar_prefetch=1,
            grid=(8,),
            in_specs=[pl.BlockSpec((1, t, d), a_index), pl.BlockSpec(g.shape, lambda k, m: (0, 0))],
            out_specs=[pl.BlockSpec((len(group), 2, d, cols), lambda k, m: (0, 0, 0, 0)) for group in groups],
        ),
        out_shape=[jax.ShapeDtypeStruct((len(group), 2, d, cols), BF16) for group in groups],
        compiler_params=pltpu.CompilerParams(vmem_limit_bytes=32 << 20),
        cost_estimate=cost(8 * t * d * 2 * cols),
        name="weight_terms",
    )(scalars, a, g)


def da_kernel(groups, m, g, w0, w1, *outs):
    cols = w0.shape[-1]
    contract = (((1,), (1,)), ((), ()))
    block = lax.dot_general(g[:, :cols], w0[0, 0], contract, preferred_element_type=F32)
    block += lax.dot_general(g[:, cols:], w1[0, 0], contract, preferred_element_type=F32)
    block = block.astype(BF16)

    def store(out):
        out[...] = block

    put(pl.program_id(0), groups, outs, store)


def input_terms(scalars, g, w):
    t, d, cols = g.shape[0], w.shape[2], w.shape[3]
    groups = pieces_of(lambda slot: (0, slot), lambda slot: (1, slot))
    blocks = sum(groups, [])

    def w_index(ylo, k, m):
        xs, yh = w_block(pick(k, [b[0] for b in blocks]), pick(k, [b[1] for b in blocks]), m)
        return (xs, sub_of(yh, ylo, m), 0, 0)

    return pl.pallas_call(
        functools.partial(da_kernel, groups),
        grid_spec=pltpu.PrefetchScalarGridSpec(
            num_scalar_prefetch=1,
            grid=(8,),
            in_specs=[
                pl.BlockSpec(g.shape, lambda k, m: (0, 0)),
                pl.BlockSpec((1, 1, d, cols), functools.partial(w_index, 0)),
                pl.BlockSpec((1, 1, d, cols), functools.partial(w_index, 1)),
            ],
            out_specs=[pl.BlockSpec((len(group), t, d), lambda k, m: (0, 0, 0)) for group in groups],
        ),
        out_shape=[jax.ShapeDtypeStruct((len(group), t, d), BF16) for group in groups],
        compiler_params=pltpu.CompilerParams(vmem_limit_bytes=32 << 20),
        cost_estimate=cost(8 * t * d * 2 * cols),
        name="input_terms",
    )(scalars, g, w, w)


def fwd_kernel(m, a0, a1, w, mine, theirs, total):
    k = pl.program_id(0)
    cols = w.shape[-1]
    t = mine.shape[0]

    def dot(left, right):
        return jnp.dot(left, right, preferred_element_type=F32)

    for ylo in range(2):
        s0, s1 = sub_of(0, ylo, m), sub_of(1, ylo, m)
        part = dot(a0[0], w[0, s0]) + dot(a1[0], w[0, s1])
        at = slice(ylo * cols, (ylo + 1) * cols)

        @pl.when(k == 0)
        def _():
            total[:, at] = part

        @pl.when((k > 0) & (k < 3))
        def _():
            total[:, at] += part

        @pl.when(k == 3)
        def _():
            final = (total[:, at] + part).astype(BF16)
            mine[:, at] = final[:t]
            theirs[:, at] = final[t:]


def forward_terms(scalars, a, w):
    t, d, cols = a.shape[1], a.shape[2], w.shape[3]
    return pl.pallas_call(
        fwd_kernel,
        grid_spec=pltpu.PrefetchScalarGridSpec(
            num_scalar_prefetch=1,
            grid=(4,),
            in_specs=[
                pl.BlockSpec((1, t, d), lambda k, m: (a_block(k, 0, m), 0, 0)),
                pl.BlockSpec((1, t, d), lambda k, m: (a_block(k, 1, m), 0, 0)),
                pl.BlockSpec((1, *w.shape[1:]), lambda k, m: (k, 0, 0, 0)),
            ],
            out_specs=[pl.BlockSpec((t // 2, 2 * cols), lambda k, m: (0, 0))] * 2,
            scratch_shapes=[pltpu.VMEM((t, 2 * cols), F32)],
        ),
        out_shape=[jax.ShapeDtypeStruct((t // 2, 2 * cols), BF16)] * 2,
        compiler_params=pltpu.CompilerParams(vmem_limit_bytes=40 << 20),
        cost_estimate=cost(8 * t * d * 2 * cols),
        name="forward_terms",
    )(scalars, a, a, w)


def body(activations, qkv_weight, qkv_grad):
    p, q = lax.axis_index("fsdp"), lax.axis_index("node")
    x, y_hi, c, y_lo, z = p // 4, p // 2 % 2, p % 2, q // 4, q % 4
    mask = (x // 2 ^ y_lo) * 4 + (x % 2 ^ z // 2) * 2 + (y_hi ^ z % 2)
    scalars = jnp.stack([mask, 2 * c]).astype(jnp.int32)
    tok, wide = activations.shape
    cols = qkv_grad.shape[1]
    sub = wide // 4

    w_same = lax.dynamic_slice_in_dim(qkv_weight, y_lo * sub, sub, 0)
    w_diff = lax.dynamic_slice_in_dim(qkv_weight, (1 - y_lo) * sub, sub, 0)
    ws_one, ws_two = flip(w_same, x=ONE), flip(w_same, x=TWO)
    w_one, w_two = flip(w_diff, y=ONE), flip(w_diff, y=TWO)
    ws_one, ws_two, w_same = tie(ws_one, ws_two, w_same)
    w_far = flip(w_same, y=2)

    halves = [activations[:, : 2 * sub], activations[:, 2 * sub :]]
    a_mine, a_theirs = jnp.where(c == 0, halves[0], halves[1]), jnp.where(c == 0, halves[1], halves[0])
    a_rows = jnp.concatenate([a_mine, flip(a_theirs, c=1)], 0)
    a_keep = lax.dynamic_slice_in_dim(a_rows, y_lo * sub, sub, 1)
    a_send = lax.dynamic_slice_in_dim(a_rows, (1 - y_lo) * sub, sub, 1)
    w_one, a_send = tie(w_one, a_send)
    a_y = flip(a_send, y=1)
    w_near = jnp.concatenate([w_one, w_far, w_two], 0)
    wn_one, wn_two = flip(w_near, x=ONE), flip(w_near, x=TWO)
    ka_one, ka_two = flip(a_keep, z=ONE), flip(a_keep, z=TWO)
    a_y, grad = tie(a_y, qkv_grad)
    g_y = flip(grad, y=1)
    ya_one, ya_two = flip(a_y, z=ONE), flip(a_y, z=TWO)
    far_one, far_two = flip(ka_two[:tok], z=ONE), flip(ka_one[tok:], z=TWO)
    ka_far = jnp.concatenate([far_one, far_two], 0)
    far_one, far_two = flip(ya_two[:tok], z=ONE), flip(ya_one[tok:], z=TWO)
    ya_far = jnp.concatenate([far_one, far_two], 0)
    a = jnp.stack([a_keep, ka_one, ka_far, ka_two, a_y, ya_one, ya_far, ya_two])

    w_own, w_1, w_2 = (jnp.concatenate(v, 0) for v in ((w_same, w_near), (ws_one, wn_one), (ws_two, wn_two)))
    w_2far = jnp.concatenate([flip(w_2[: 2 * sub], x=ONE), flip(w_1[2 * sub :], x=TWO)], 0)
    w = jnp.stack([w_own, w_1, w_2far, w_2]).reshape(4, 4, sub, cols)
    g_rows = jnp.concatenate([grad, g_y], 1)
    g = jnp.concatenate([g_rows, flip(g_rows, c=1)], 0)

    dw_first, *dw = weight_terms(scalars, a, g)
    dw_first, scalars = tie(dw_first, scalars)
    da_first, *da = input_terms(scalars, g, w)
    da_first, scalars = tie(da_first, scalars)
    da_keep, da_send = scatter4(da_first, *da, "z")
    dw_0, dw_1 = scatter4(dw_first, *dw, "x")

    mine, theirs = forward_terms(scalars, a, w)
    fwd = add(mine, flip(theirs, c=1))
    fwd_y = flip(fwd[:, cols:].astype(BF16), y=1)
    fwd_y, da_send = tie(fwd_y, da_send)
    projected = add(fwd[:, :cols], fwd_y).astype(BF16)

    da_y = flip(da_send.astype(BF16), y=1)
    da_keep = da_keep.astype(BF16)
    r0, r1 = jnp.where(y_lo == 0, da_keep, da_y), jnp.where(y_lo == 0, da_y, da_keep)
    both = jnp.concatenate([r0, r1], 1)
    mine, theirs = both[:tok], flip(both[tok:], c=1)
    input_grad = jnp.concatenate([jnp.where(c == 0, mine, theirs), jnp.where(c == 0, theirs, mine)], 1)

    send1, send3 = dw_0[1].astype(BF16), dw_1[1].astype(BF16)
    got_one = flip(jnp.where(c == 0, send1, send3), y=ONE)
    got_two = flip(jnp.where(c == 0, send3, send1), y=TWO)
    got_far = flip(dw_1[0].astype(BF16), y=2)
    same, diff = add(dw_0[0], got_far), add(got_one, got_two)
    weight_grad = jnp.where(y_lo == 0, jnp.concatenate([same, diff], 0), jnp.concatenate([diff, same], 0))

    return projected, input_grad, weight_grad


def solution(mesh):
    spec = P("fsdp", "node")
    return jax.shard_map(body, mesh=mesh, in_specs=(spec,) * 3, out_specs=(spec,) * 3, check_vma=False)
```

time: 403 us -> 165 us (0.41)
  waiting for transfers between devices: 348 us -> 67 us
  starting transfers between devices: 0.16 us -> 46.7 us
  matrix products: 38.9 us -> 0 us
  Pallas kernels: 0 us -> 31.2 us
  other arithmetic: 2.23 us -> 16.5 us
  between operations: 13.8 us -> 1.02 us
    reduce_scatter x2 -> x0, waiting for transfers between devices: 179 us -> none  [the longest x1 93.3 us: body(): lax.psum_scatter(partial_sum.astype(jnp.bfloat16), 'node', scatter_dimens...]
    all_gather x2 -> x0, waiting for transfers between devices: 168 us -> none  [the longest x1 96.3 us: body(): gathered = lax.all_gather(activations, 'node', axis=1, tiled=True)]
    ppermute x0 -> x36, waiting for transfers between devices: none -> 67 us  [flip(): return lax.ppermute(value, AXES, pairs)]
    ppermute x0 -> x36, starting transfers between devices: none -> 46.7 us  [flip(): return lax.ppermute(value, AXES, pairs)]
    dot_general x3 -> x0, matrix products: 38.9 us -> none  [the longest x1 14.5 us: body(): jnp.dot(feature_cols, lax.all_gather(qkv_weight, 'fsdp', axis=0, tiled=Tr...]
    pallas_call x0 -> x3, Pallas kernels: none -> 31.2 us  [the longest x1 12.3 us: forward_terms(): pl.pallas_call(fwd_kernel, grid_spec=pltpu.PrefetchScalarGridSpec(num_sca...]
    select_n x0 -> x5, other arithmetic: none -> 4.15 us  [the longest x1 1.38 us: body(): jnp.where(y_lo == 0, da_keep, da_y)]
  transfers between devices with their start and end apart: 4 -> 36, of which waited for: 4 -> 19; matrix products, arithmetic and copies ran while one was open for 10% -> 9% of each run, Pallas kernels for 0% -> 14%
where the time goes in v2:
time: 165 us; the launch traced here: 164 us
  waiting for transfers between devices  67 us (41%)
  starting transfers between devices  46.7 us (28%)
  Pallas kernels  31.2 us (19%)
  other arithmetic  16.5 us (10%)
  local copies, waits for them, and re-layouts  1.94 us (1%)
    ppermute x36, waiting for transfers between devices, flip(): return lax.ppermute(value, AXES, pairs)  67 us
    ppermute x36, starting transfers between devices, flip(): return lax.ppermute(value, AXES, pairs)  46.7 us
    pallas_call x1, Pallas kernels, forward_terms(): pl.pallas_call(fwd_kernel, grid_spec=pltpu.PrefetchScalarGridSpec(num_sca...  12.3 us
    pallas_call x1, Pallas kernels, input_terms(): pl.pallas_call(functools.partial(da_kernel, groups), grid_spec=pltpu.Pref...  10.3 us
    pallas_call x1, Pallas kernels, weight_terms(): pl.pallas_call(functools.partial(dw_kernel, groups), grid_spec=pltpu.Pref...  8.63 us
    add x5, other arithmetic, add(): total = total + term.astype(F32)  3.54 us
  transfers between devices with their start and end apart: 36, of which 19 were waited for; matrix products, arithmetic and copies ran while one was open for 9% of the time, Pallas kernels for 14%

profile of v2, /device:TPU:1, one launch (start us, length us, event | category | flops | bytes accessed | tf_op | source)
XLA Modules:
  0.0 164.3 jit_solution(3953408392162641035)
XLA Ops:
  0.7 1.3 broadcast_select_fusion.5
  2.0 1.5 collective-permute-start
  3.6 2.6 %collective-permute-start.13 = (bf16[256,640]{1,0:T(8,128)(2,1)S(1)}, bf16[256,640]{1,0:T(8,128)(2,1)S(1)}, u32[]{:S(2)}, u32[]{:S(2)}) collective-permute-start(bf16[256,640]{1,0:T(8,128)(2,1)S(1)} %get-tuple-element.33), channel_id=1, source_target_pairs={{0,32},{1,33},{2,34},{3,35},{4,36},{5,37},{6,38},{7,39},{8,104},{9... | collective-permute-start | bytes 983048 | tf_op jit(solution)/shard_map/ppermute | solution.py:23
  6.2 2.7 %collective-permute-start.5 = (bf16[256,640]{1,0:T(8,128)(2,1)S(1)}, bf16[256,640]{1,0:T(8,128)(2,1)S(1)}, u32[]{:S(2)}, u32[]{:S(2)}) collective-permute-start(bf16[256,640]{1,0:T(8,128)(2,1)S(1)} %get-tuple-element.67), channel_id=1, source_target_pairs={{0,4},{1,5},{2,6},{3,7},{4,0},{5,1},{6,2},{7,3},{8,28},{9,29},{10,... | collective-permute-start | bytes 983048 | tf_op jit(solution)/shard_map/ppermute | solution.py:23
  9.0 3.4 %collective-permute-done.13 = bf16[256,640]{1,0:T(8,128)(2,1)S(1)} collective-permute-done((bf16[256,640]{1,0:T(8,128)(2,1)S(1)}, bf16[256,640]{1,0:T(8,128)(2,1)S(1)}, u32[]{:S(2)}, u32[]{:S(2)}) %collective-permute-start.13) | collective-permute-done | bytes 327712 | tf_op jit(solution)/shard_map/ppermute | solution.py:23
  12.4 1.5 collective-permute-done.14
  13.9 3.0 %collective-permute-start.15 = (bf16[256,640]{1,0:T(8,128)(2,1)S(1)}, bf16[256,640]{1,0:T(8,128)(2,1)S(1)}, u32[]{:S(2)}, u32[]{:S(2)}) collective-permute-start(bf16[256,640]{1,0:T(8,128)(2,1)S(1)} %get-tuple-element.33), channel_id=1, source_target_pairs={{0,16},{1,17},{2,18},{3,19},{4,20},{5,21},{6,22},{7,23},{8,24},{9,... | collective-permute-start | bytes 983048 | tf_op jit(solution)/shard_map/ppermute | solution.py:23
  17.0 3.8 %collective-permute-start.1 = (bf16[1024,256]{1,0:T(8,128)(2,1)S(1)}, bf16[1024,256]{1,0:T(8,128)(2,1)S(1)}, u32[]{:S(2)}, u32[]{:S(2)}) collective-permute-start(bf16[1024,256]{1,0:T(8,128)(2,1)S(1)} %get-tuple-element.54), channel_id=1, source_target_pairs={{0,1},{1,0},{2,3},{3,2},{4,5},{5,4},{6,7},{7,6},{8,11},{9,10},{10,... | collective-permute-start | bytes 1572872 | tf_op jit(solution)/shard_map/ppermute | solution.py:23
  20.9 0.5 collective-permute-start.6
  21.4 2.7 %collective-permute-done.15 = bf16[256,640]{1,0:T(8,128)(2,1)S(1)} collective-permute-done((bf16[256,640]{1,0:T(8,128)(2,1)S(1)}, bf16[256,640]{1,0:T(8,128)(2,1)S(1)}, u32[]{:S(2)}, u32[]{:S(2)}) %collective-permute-start.15) | collective-permute-done | bytes 327712 | tf_op jit(solution)/shard_map/ppermute | solution.py:23
  24.2 2.5 %collective-permute-start.18 = (bf16[768,640]{1,0:T(8,128)(2,1)S(1)}, bf16[768,640]{1,0:T(8,128)(2,1)S(1)}, u32[]{:S(2)}, u32[]{:S(2)}) collective-permute-start(bf16[768,640]{1,0:T(8,128)(2,1)S(1)} %constant_dynamic-update-slice_fusion.2), channel_id=1, source_target_pairs={{0,96},{1,97},{2,98},{3,99},{4,100},{5,101},{6,102},{7,103},{8,40}... | collective-permute-start | bytes 2949128 | tf_op jit(solution)/shard_map/ppermute | solution.py:23
  26.9 5.9 %collective-permute-done.2 = bf16[1024,256]{1,0:T(8,128)(2,1)S(1)} collective-permute-done((bf16[1024,256]{1,0:T(8,128)(2,1)S(1)}, bf16[1024,256]{1,0:T(8,128)(2,1)S(1)}, u32[]{:S(2)}, u32[]{:S(2)}) %collective-permute-start.2) | collective-permute-done | bytes 524320 | tf_op jit(solution)/shard_map/ppermute | solution.py:23
  32.8 0.3 collective-permute-start.3
  33.2 1.5 collective-permute-start.4
  34.7 0.5 collective-permute-done.6
  35.2 3.8 %collective-permute-start.7 = (bf16[1024,256]{1,0:T(8,128)(2,1)S(1)}, bf16[1024,256]{1,0:T(8,128)(2,1)S(1)}, u32[]{:S(2)}, u32[]{:S(2)}) collective-permute-start(bf16[1024,256]{1,0:T(8,128)(2,1)S(1)} %collective-permute-done.6), channel_id=1, source_target_pairs={{0,1},{1,0},{2,3},{3,2},{4,5},{5,4},{6,7},{7,6},{8,11},{9,10},{10,... | collective-permute-start | bytes 1572872 | tf_op jit(solution)/shard_map/ppermute | solution.py:23
  39.0 1.9 %collective-permute-done.3 = bf16[512,256]{1,0:T(8,128)(2,1)S(1)} collective-permute-done((bf16[512,256]{1,0:T(8,128)(2,1)S(1)}, bf16[512,256]{1,0:T(8,128)(2,1)S(1)}, u32[]{:S(2)}, u32[]{:S(2)}) %collective-permute-start.3) | collective-permute-done | bytes 262176 | tf_op jit(solution)/shard_map/ppermute | solution.py:23
  40.9 0.4 collective-permute-start.11
  41.5 7.7 %collective-permute-done.7 = bf16[1024,256]{1,0:T(8,128)(2,1)S(1)} collective-permute-done((bf16[1024,256]{1,0:T(8,128)(2,1)S(1)}, bf16[1024,256]{1,0:T(8,128)(2,1)S(1)}, u32[]{:S(2)}, u32[]{:S(2)}) %collective-permute-start.7) | collective-permute-done | bytes 524320 | tf_op jit(solution)/shard_map/ppermute | solution.py:23
  49.2 1.7 %collective-permute-start.10 = (bf16[512,256]{1,0:T(8,128)(2,1)S(1)}, bf16[512,256]{1,0:T(8,128)(2,1)S(1)}, u32[]{:S(2)}, u32[]{:S(2)}) collective-permute-start(bf16[512,256]{1,0:T(8,128)(2,1)S(1)} %slice.119), channel_id=1, source_target_pairs={{0,3},{1,2},{2,1},{3,0},{4,7},{5,6},{6,5},{7,4},{8,9},{9,8},{10,11... | collective-permute-start | bytes 786440 | tf_op jit(solution)/shard_map/ppermute | solution.py:23
  50.9 1.9 %collective-permute-done.8 = bf16[1024,256]{1,0:T(8,128)(2,1)S(1)} collective-permute-done((bf16[1024,256]{1,0:T(8,128)(2,1)S(1)}, bf16[1024,256]{1,0:T(8,128)(2,1)S(1)}, u32[]{:S(2)}, u32[]{:S(2)}) %collective-permute-start.8) | collective-permute-done | bytes 524320 | tf_op jit(solution)/shard_map/ppermute | solution.py:23
  52.8 1.5 collective-permute-start.9
  54.3 0.2 constant_dynamic-update-slice_fusion.5
  54.5 3.3 %collective-permute-start.19 = (bf16[512,640]{1,0:T(8,128)(2,1)S(1)}, bf16[512,640]{1,0:T(8,128)(2,1)S(1)}, u32[]{:S(2)}, u32[]{:S(2)}) collective-permute-start(bf16[512,640]{1,0:T(8,128)(2,1)S(1)} %slice.120), channel_id=1, source_target_pairs={{0,32},{1,33},{2,34},{3,35},{4,36},{5,37},{6,38},{7,39},{8,104},{9... | collective-permute-start | bytes 1966088 | tf_op jit(solution)/shard_map/ppermute | solution.py:23
  58.1 2.3 %collective-permute-start.12 = (bf16[512,1280]{1,0:T(8,128)(2,1)S(1)}, bf16[512,1280]{1,0:T(8,128)(2,1)S(1)}, u32[]{:S(2)}, u32[]{:S(2)}) collective-permute-start(bf16[512,1280]{1,0:T(8,128)(2,1)S(1)} %constant_dynamic-update-slice_fusion), channel_id=1, source_target_pairs={{0,8},{1,9},{2,10},{3,11},{4,12},{5,13},{6,14},{7,15},{8,0},{9,1},... | collective-permute-start | bytes 3932168 | tf_op jit(solution)/shard_map/ppermute | solution.py:23
  60.5 0.1 pad_maximum_fusion.3
  60.6 0.4 collective-permute-done.9
  61.1 8.6 %collective-permute-done.19 = bf16[512,640]{1,0:T(8,128)(2,1)S(1)} collective-permute-done((bf16[512,640]{1,0:T(8,128)(2,1)S(1)}, bf16[512,640]{1,0:T(8,128)(2,1)S(1)}, u32[]{:S(2)}, u32[]{:S(2)}) %collective-permute-start.19) | collective-permute-done | bytes 655392 | tf_op jit(solution)/shard_map/ppermute | solution.py:23
  69.7 5.0 %collective-permute-done.20 = bf16[512,640]{1,0:T(8,128)(2,1)S(1)} collective-permute-done((bf16[512,640]{1,0:T(8,128)(2,1)S(1)}, bf16[512,640]{1,0:T(8,128)(2,1)S(1)}, u32[]{:S(2)}, u32[]{:S(2)}) %collective-permute-start.20) | collective-permute-done | bytes 655392 | tf_op jit(solution)/shard_map/ppermute | solution.py:23
  74.8 1.0 pad_maximum_fusion.w0.w1.w
  75.9 0.2 pad_maximum_fusion.1.g
  76.1 8.6 %weight_terms.1 = (bf16[2,2,256,640]{3,2,1,0:T(8,128)(2,1)S(1)}, bf16[2,2,256,640]{3,2,1,0:T(8,128)(2,1)S(1)}, bf16[1,2,256,640]{3,2,1,0:T(8,128)(2,1)S(1)}, bf1...) custom-call(s32[2]{0:T(128)S(1)} %pad_add_fusion.m, ...), custom_call_target="tpu_custom_call" | custom-call | flops 10737418240 | bytes 5242880 | tf_op jit(solution)/shard_map/weight_terms/pallas_call | solution.py:119
  84.8 10.3 %input_terms.1 = (bf16[2,1024,256]{2,1,0:T(8,128)(2,1)}, bf16[2,1024,256]{2,1,0:T(8,128)(2,1)S(1)}, bf16[1,1024,256]{2,1,0:T(8,128)(2,1)S(1)}, bf16[1,1024,256]{...) custom-call(s32[2]{0:T(128)S(1)} %pad_add_fusion.m, bf16[1024,1280]{1,0:T(8,128)(2,1)S(1)} %pad_maximum_fusion.1.g, ...), custom_call_target="tpu_custom_call" | custom-call | flops 10737418240 | bytes 5242880 | tf_op jit(solution)/shard_map/input_terms/pallas_call | solution.py:156
  95.1 12.3 %forward_terms.1 = (bf16[512,1280]{1,0:T(8,128)(2,1)S(1)}, bf16[512,1280]{1,0:T(8,128)(2,1)S(1)}) custom-call(s32[2]{0:T(128)S(1)} %pad_add_fusion.m, bf16[8,1024,256]{2,1,0:T(8,128)(2,1)S(1)} %bitcast_dynamic-update-slice_fusion.a.a0.a1, bf16[8,1024,256]{2,1,0:T(8,128)(2,1)S(1)} %bitcast_dynamic-update-slice_fusion.a.a0.a1, ...), custom_call_target="tpu_custom_call" | custom-call | flops 10737418240 | bytes 5242880 | tf_op jit(solution)/shard_map/forward_terms/pallas_call | solution.py:205
  107.4 2.5 %collective-permute-start.21 = (bf16[512,1280]{1,0:T(8,128)(2,1)S(1)}, bf16[512,1280]{1,0:T(8,128)(2,1)S(1)}, u32[]{:S(2)}, u32[]{:S(2)}) collective-permute-start(bf16[512,1280]{1,0:T(8,128)(2,1)S(1)} %get-tuple-element.40), channel_id=1, source_target_pairs={{0,8},{1,9},{2,10},{3,11},{4,12},{5,13},{6,14},{7,15},{8,0},{9,1},... | collective-permute-start | bytes 3932168 | tf_op jit(solution)/shard_map/ppermute | solution.py:23
  109.8 1.0 collective-permute-start.29
  110.8 3.0 %collective-permute-start.25 = (bf16[2,1024,256]{2,1,0:T(8,128)(2,1)}, bf16[2,1024,256]{2,1,0:T(8,128)(2,1)}, u32[]{:S(2)}, u32[]{:S(2)}) collective-permute-start(bf16[2,1024,256]{2,1,0:T(8,128)(2,1)} %get-tuple-element.45), channel_id=1, source_target_pairs={{0,1},{1,0},{2,3},{3,2},{4,5},{5,4},{6,7},{7,6},{8,11},{9,10},{10,... | collective-permute-start | bytes 3145736 | tf_op jit(solution)/shard_map/ppermute | solution.py:23
  113.7 1.1 fusion.6
  114.9 1.2 fusion.4
  116.1 1.4 collective-permute-start.32
  117.5 0.3 convert_add_fusion
  117.8 1.0 slice.191
  118.8 0.4 collective-permute-start.22
  119.2 8.3 %collective-permute-done.29 = bf16[2,2,256,640]{3,2,1,0:T(8,128)(2,1)S(1)} collective-permute-done((bf16[2,2,256,640]{3,2,1,0:T(8,128)(2,1)S(1)}, bf16[2,2,256,640]{3,2,1,0:T(8,128)(2,1)S(1)}, u32[]{:S(2)}, u32[]{:S(2)}) %collective-permute-start.29) | collective-permute-done | bytes 1310752 | tf_op jit(solution)/shard_map/ppermute | solution.py:23
  127.5 1.2 fusion.3
  128.8 1.3 fusion.7
  130.2 1.7 %collective-permute-done.24 = bf16[1024,256]{1,0:T(8,128)(2,1)} collective-permute-done((bf16[1024,256]{1,0:T(8,128)(2,1)}, bf16[1024,256]{1,0:T(8,128)(2,1)}, u32[]{:S(2)}, u32[]{:S(2)}) %collective-permute-start.24) | collective-permute-done | bytes 524320 | tf_op jit(solution)/shard_map/ppermute | solution.py:23
  131.9 1.2 bitcast_add_fusion.3
  133.1 2.0 %collective-permute-done.22 = bf16[512,640]{1,0:T(8,128)(2,1)S(1)} collective-permute-done((bf16[512,640]{1,0:T(8,128)(2,1)}, bf16[512,640]{1,0:T(8,128)(2,1)S(1)}, u32[]{:S(2)}, u32[]{:S(2)}) %collective-permute-start.22) | collective-permute-done | bytes 655392 | tf_op jit(solution)/shard_map/ppermute | solution.py:23
  135.1 0.4 collective-permute-start.27
  135.5 0.8 collective-permute-done.32
  136.3 5.0 %collective-permute-done.30 = bf16[2,256,640]{2,1,0:T(8,128)(2,1)} collective-permute-done((bf16[2,256,640]{2,1,0:T(8,128)(2,1)}, bf16[2,256,640]{2,1,0:T(8,128)(2,1)}, u32[]{:S(2)}, u32[]{:S(2)}) %collective-permute-start.30) | collective-permute-done | bytes 655392 | tf_op jit(solution)/shard_map/ppermute | solution.py:23
  141.3 1.9 %bitcast_add_fusion.1 = (f32[2,256,640]{2,1,0:T(8,128)S(1)}, bf16[2,256,640]{2,1,0:T(8,128)(2,1)S(1)}) fusion(bf16[2,256,640]{2,1,0:T(8,128)(2,1)} %collective-permute-done.30, bf16[2,2,256,640]{3,2,1,0:T(8,128)(2,1)S(1)} %copy-done.5, bf16[2,2,256,640]{3,2,1,0:T(8,128)(2,1)S(1)} %get-tuple-element.48, bf16[2,256,640]{2,1,0:T(8,128)(2,1)} %collective-permute-done.32, ...), kind=kLoop, calls=%fused_computation.12 | loop fusion | flops 3604480 | bytes 5898240 | tf_op jit(solution)/shard_map/add | solution.py:36
  143.3 0.5 collective-permute-start.33
  143.8 2.4 %collective-permute-start.34 = (bf16[256,640]{1,0:T(8,128)(2,1)S(1)}, bf16[256,640]{1,0:T(8,128)(2,1)S(1)}, u32[]{:S(2)}, u32[]{:S(2)}) collective-permute-start(bf16[256,640]{1,0:T(8,128)(2,1)S(1)} %get-tuple-element.57), channel_id=1, source_target_pairs={{0,4},{1,5},{2,6},{3,7},{4,0},{5,1},{6,2},{7,3},{8,28},{9,29},{10,... | collective-permute-start | bytes 983048 | tf_op jit(solution)/shard_map/ppermute | solution.py:23
  146.1 1.0 fusion
  147.2 0.4 collective-permute-done.27
  147.6 1.4 broadcast_select_fusion.1
  149.0 3.4 %collective-permute-start.28 = (bf16[512,512]{1,0:T(8,128)(2,1)S(1)}, bf16[512,512]{1,0:T(8,128)(2,1)S(1)}, u32[]{:S(2)}, u32[]{:S(2)}) collective-permute-start(bf16[512,512]{1,0:T(8,128)(2,1)S(1)} %pad_maximum_fusion.6), channel_id=1, source_target_pairs={{0,8},{1,9},{2,10},{3,11},{4,12},{5,13},{6,14},{7,15},{8,0},{9,1},... | collective-permute-start | bytes 1572872 | tf_op jit(solution)/shard_map/ppermute | solution.py:23
  152.4 7.6 %collective-permute-done.34 = bf16[256,640]{1,0:T(8,128)(2,1)S(1)} collective-permute-done((bf16[256,640]{1,0:T(8,128)(2,1)S(1)}, bf16[256,640]{1,0:T(8,128)(2,1)S(1)}, u32[]{:S(2)}, u32[]{:S(2)}) %collective-permute-start.34) | collective-permute-done | bytes 327712 | tf_op jit(solution)/shard_map/ppermute | solution.py:23
  160.0 1.7 %collective-permute-done.35 = bf16[256,640]{1,0:T(8,128)(2,1)S(1)} collective-permute-done((bf16[256,640]{1,0:T(8,128)(2,1)S(1)}, bf16[256,640]{1,0:T(8,128)(2,1)S(1)}, u32[]{:S(2)}, u32[]{:S(2)}) %collective-permute-start.35) | collective-permute-done | bytes 327712 | tf_op jit(solution)/shard_map/ppermute | solution.py:23
  161.8 1.1 maximum_select_fusion
  163.0 0.2 broadcast_select_fusion.3
  163.2 1.1 pad_maximum_fusion.5
  (78 shorter events, 2.0 us)
Async XLA Ops:
  0.6 2.9 %copy-start.9 = (bf16[512,640]{1,0:T(8,128)(2,1)S(1)}, bf16[512,640]{1,0:T(8,128)(2,1)}, u32[]{:S(2)}) copy-start(bf16[512,640]{1,0:T(8,128)(2,1)} %param.4) | copy-start | bytes 1966084
  2.0 14.9 %collective-permute-start = (bf16[512,512]{1,0:T(8,128)(2,1)S(1)}, bf16[512,512]{1,0:T(8,128)(2,1)S(1)}, u32[]{:S(2)}, u32[]{:S(2)}) collective-permute-start(bf16[512,512]{1,0:T(8,128)(2,1)S(1)} %get-tuple-element.64), channel_id=1, source_target_pairs={{0,8},{1,9},{2,10},{3,11},{4,12},{5,13},{6,14},{7,15},{8,0},{9,1},... | collective-permute-start | bytes 1572872 | tf_op jit(solution)/shard_map/ppermute | solution.py:23
  3.6 8.9 %collective-permute-start.13 = (bf16[256,640]{1,0:T(8,128)(2,1)S(1)}, bf16[256,640]{1,0:T(8,128)(2,1)S(1)}, u32[]{:S(2)}, u32[]{:S(2)}) collective-permute-start(bf16[256,640]{1,0:T(8,128)(2,1)S(1)} %get-tuple-element.33), channel_id=1, source_target_pairs={{0,32},{1,33},{2,34},{3,35},{4,36},{5,37},{6,38},{7,39},{8,104},{9... | collective-permute-start | bytes 983048 | tf_op jit(solution)/shard_map/ppermute | solution.py:23
  6.2 7.7 %collective-permute-start.14 = (bf16[256,640]{1,0:T(8,128)(2,1)S(1)}, bf16[256,640]{1,0:T(8,128)(2,1)S(1)}, u32[]{:S(2)}, u32[]{:S(2)}) collective-permute-start(bf16[256,640]{1,0:T(8,128)(2,1)S(1)} %get-tuple-element.33), channel_id=1, source_target_pairs={{0,96},{1,97},{2,98},{3,99},{4,100},{5,101},{6,102},{7,103},{8,40}... | collective-permute-start | bytes 983048 | tf_op jit(solution)/shard_map/ppermute | solution.py:23
  6.2 14.6 %collective-permute-start.5 = (bf16[256,640]{1,0:T(8,128)(2,1)S(1)}, bf16[256,640]{1,0:T(8,128)(2,1)S(1)}, u32[]{:S(2)}, u32[]{:S(2)}) collective-permute-start(bf16[256,640]{1,0:T(8,128)(2,1)S(1)} %get-tuple-element.67), channel_id=1, source_target_pairs={{0,4},{1,5},{2,6},{3,7},{4,0},{5,1},{6,2},{7,3},{8,28},{9,29},{10,... | collective-permute-start | bytes 983048 | tf_op jit(solution)/shard_map/ppermute | solution.py:23
  8.9 15.2 %collective-permute-start.16 = (bf16[256,640]{1,0:T(8,128)(2,1)S(1)}, bf16[256,640]{1,0:T(8,128)(2,1)S(1)}, u32[]{:S(2)}, u32[]{:S(2)}) collective-permute-start(bf16[256,640]{1,0:T(8,128)(2,1)S(1)} %get-tuple-element.67), channel_id=1, source_target_pairs={{0,20},{1,21},{2,22},{3,23},{4,16},{5,17},{6,18},{7,19},{8,12},{9,... | collective-permute-start | bytes 983048 | tf_op jit(solution)/shard_map/ppermute | solution.py:23
  13.9 10.2 %collective-permute-start.15 = (bf16[256,640]{1,0:T(8,128)(2,1)S(1)}, bf16[256,640]{1,0:T(8,128)(2,1)S(1)}, u32[]{:S(2)}, u32[]{:S(2)}) collective-permute-start(bf16[256,640]{1,0:T(8,128)(2,1)S(1)} %get-tuple-element.33), channel_id=1, source_target_pairs={{0,16},{1,17},{2,18},{3,19},{4,20},{5,21},{6,22},{7,23},{8,24},{9,... | collective-permute-start | bytes 983048 | tf_op jit(solution)/shard_map/ppermute | solution.py:23
  17.0 16.2 %collective-permute-start.1 = (bf16[1024,256]{1,0:T(8,128)(2,1)S(1)}, bf16[1024,256]{1,0:T(8,128)(2,1)S(1)}, u32[]{:S(2)}, u32[]{:S(2)}) collective-permute-start(bf16[1024,256]{1,0:T(8,128)(2,1)S(1)} %get-tuple-element.54), channel_id=1, source_target_pairs={{0,1},{1,0},{2,3},{3,2},{4,5},{5,4},{6,7},{7,6},{8,11},{9,10},{10,... | collective-permute-start | bytes 1572872 | tf_op jit(solution)/shard_map/ppermute | solution.py:23
  20.8 12.0 %collective-permute-start.2 = (bf16[1024,256]{1,0:T(8,128)(2,1)S(1)}, bf16[1024,256]{1,0:T(8,128)(2,1)S(1)}, u32[]{:S(2)}, u32[]{:S(2)}) collective-permute-start(bf16[1024,256]{1,0:T(8,128)(2,1)S(1)} %get-tuple-element.54), channel_id=1, source_target_pairs={{0,3},{1,2},{2,1},{3,0},{4,7},{5,6},{6,5},{7,4},{8,9},{9,8},{10,11... | collective-permute-start | bytes 1572872 | tf_op jit(solution)/shard_map/ppermute | solution.py:23
  20.9 14.3 %collective-permute-start.6 = (bf16[1024,256]{1,0:T(8,128)(2,1)S(1)}, bf16[1024,256]{1,0:T(8,128)(2,1)S(1)}, u32[]{:S(2)}, u32[]{:S(2)}) collective-permute-start(bf16[1024,256]{1,0:T(8,128)(2,1)S(1)} %fusion.9), channel_id=1, source_target_pairs={{0,4},{1,5},{2,6},{3,7},{4,0},{5,1},{6,2},{7,3},{8,12},{9,13},{10,... | collective-permute-start | bytes 1572872 | tf_op jit(solution)/shard_map/ppermute | solution.py:23
  24.2 14.7 %copy-start.8 = (bf16[512,640]{1,0:T(8,128)(2,1)S(1)}, bf16[512,640]{1,0:T(8,128)(2,1)}, u32[]{:S(2)}) copy-start(bf16[512,640]{1,0:T(8,128)(2,1)} %param.5) | copy-start | bytes 1966084
  24.2 30.1 %collective-permute-start.18 = (bf16[768,640]{1,0:T(8,128)(2,1)S(1)}, bf16[768,640]{1,0:T(8,128)(2,1)S(1)}, u32[]{:S(2)}, u32[]{:S(2)}) collective-permute-start(bf16[768,640]{1,0:T(8,128)(2,1)S(1)} %constant_dynamic-update-slice_fusion.2), channel_id=1, source_target_pairs={{0,96},{1,97},{2,98},{3,99},{4,100},{5,101},{6,102},{7,103},{8,40}... | collective-permute-start | bytes 2949128 | tf_op jit(solution)/shard_map/ppermute | solution.py:23
  26.7 31.2 %collective-permute-start.17 = (bf16[768,640]{1,0:T(8,128)(2,1)S(1)}, bf16[768,640]{1,0:T(8,128)(2,1)S(1)}, u32[]{:S(2)}, u32[]{:S(2)}) collective-permute-start(bf16[768,640]{1,0:T(8,128)(2,1)S(1)} %constant_dynamic-update-slice_fusion.2), channel_id=1, source_target_pairs={{0,32},{1,33},{2,34},{3,35},{4,36},{5,37},{6,38},{7,39},{8,104},{9... | collective-permute-start | bytes 2949128 | tf_op jit(solution)/shard_map/ppermute | solution.py:23
  32.8 8.1 %collective-permute-start.3 = (bf16[512,256]{1,0:T(8,128)(2,1)S(1)}, bf16[512,256]{1,0:T(8,128)(2,1)S(1)}, u32[]{:S(2)}, u32[]{:S(2)}) collective-permute-start(bf16[512,256]{1,0:T(8,128)(2,1)S(1)} %slice.116), channel_id=1, source_target_pairs={{0,1},{1,0},{2,3},{3,2},{4,5},{5,4},{6,7},{7,6},{8,11},{9,10},{10,... | collective-permute-start | bytes 786440 | tf_op jit(solution)/shard_map/ppermute | solution.py:23
  33.2 7.8 %collective-permute-start.4 = (bf16[512,256]{1,0:T(8,128)(2,1)S(1)}, bf16[512,256]{1,0:T(8,128)(2,1)S(1)}, u32[]{:S(2)}, u32[]{:S(2)}) collective-permute-start(bf16[512,256]{1,0:T(8,128)(2,1)S(1)} %slice.117), channel_id=1, source_target_pairs={{0,3},{1,2},{2,1},{3,0},{4,7},{5,6},{6,5},{7,4},{8,9},{9,8},{10,11... | collective-permute-start | bytes 786440 | tf_op jit(solution)/shard_map/ppermute | solution.py:23
  35.2 14.0 %collective-permute-start.7 = (bf16[1024,256]{1,0:T(8,128)(2,1)S(1)}, bf16[1024,256]{1,0:T(8,128)(2,1)S(1)}, u32[]{:S(2)}, u32[]{:S(2)}) collective-permute-start(bf16[1024,256]{1,0:T(8,128)(2,1)S(1)} %collective-permute-done.6), channel_id=1, source_target_pairs={{0,1},{1,0},{2,3},{3,2},{4,5},{5,4},{6,7},{7,6},{8,11},{9,10},{10,... | collective-permute-start | bytes 1572872 | tf_op jit(solution)/shard_map/ppermute | solution.py:23
  40.9 11.9 %collective-permute-start.8 = (bf16[1024,256]{1,0:T(8,128)(2,1)S(1)}, bf16[1024,256]{1,0:T(8,128)(2,1)S(1)}, u32[]{:S(2)}, u32[]{:S(2)}) collective-permute-start(bf16[1024,256]{1,0:T(8,128)(2,1)S(1)} %collective-permute-done.6), channel_id=1, source_target_pairs={{0,3},{1,2},{2,1},{3,0},{4,7},{5,6},{6,5},{7,4},{8,9},{9,8},{10,11... | collective-permute-start | bytes 1572872 | tf_op jit(solution)/shard_map/ppermute | solution.py:23
  40.9 17.0 %collective-permute-start.11 = (bf16[512,640]{1,0:T(8,128)(2,1)S(1)}, bf16[512,640]{1,0:T(8,128)(2,1)S(1)}, u32[]{:S(2)}, u32[]{:S(2)}) collective-permute-start(bf16[512,640]{1,0:T(8,128)(2,1)S(1)} %copy-done.8), channel_id=1, source_target_pairs={{0,4},{1,5},{2,6},{3,7},{4,0},{5,1},{6,2},{7,3},{8,12},{9,13},{10,... | collective-permute-start | bytes 1966088 | tf_op jit(solution)/shard_map/ppermute | solution.py:23
  49.2 11.4 %collective-permute-start.10 = (bf16[512,256]{1,0:T(8,128)(2,1)S(1)}, bf16[512,256]{1,0:T(8,128)(2,1)S(1)}, u32[]{:S(2)}, u32[]{:S(2)}) collective-permute-start(bf16[512,256]{1,0:T(8,128)(2,1)S(1)} %slice.119), channel_id=1, source_target_pairs={{0,3},{1,2},{2,1},{3,0},{4,7},{5,6},{6,5},{7,4},{8,9},{9,8},{10,11... | collective-permute-start | bytes 786440 | tf_op jit(solution)/shard_map/ppermute | solution.py:23
  52.8 8.2 %collective-permute-start.9 = (bf16[512,256]{1,0:T(8,128)(2,1)S(1)}, bf16[512,256]{1,0:T(8,128)(2,1)S(1)}, u32[]{:S(2)}, u32[]{:S(2)}) collective-permute-start(bf16[512,256]{1,0:T(8,128)(2,1)S(1)} %slice.118), channel_id=1, source_target_pairs={{0,1},{1,0},{2,3},{3,2},{4,5},{5,4},{6,7},{7,6},{8,11},{9,10},{10,... | collective-permute-start | bytes 786440 | tf_op jit(solution)/shard_map/ppermute | solution.py:23
  54.5 15.2 %collective-permute-start.19 = (bf16[512,640]{1,0:T(8,128)(2,1)S(1)}, bf16[512,640]{1,0:T(8,128)(2,1)S(1)}, u32[]{:S(2)}, u32[]{:S(2)}) collective-permute-start(bf16[512,640]{1,0:T(8,128)(2,1)S(1)} %slice.120), channel_id=1, source_target_pairs={{0,32},{1,33},{2,34},{3,35},{4,36},{5,37},{6,38},{7,39},{8,104},{9... | collective-permute-start | bytes 1966088 | tf_op jit(solution)/shard_map/ppermute | solution.py:23
  57.9 16.8 %collective-permute-start.20 = (bf16[512,640]{1,0:T(8,128)(2,1)S(1)}, bf16[512,640]{1,0:T(8,128)(2,1)S(1)}, u32[]{:S(2)}, u32[]{:S(2)}) collective-permute-start(bf16[512,640]{1,0:T(8,128)(2,1)S(1)} %slice.121), channel_id=1, source_target_pairs={{0,96},{1,97},{2,98},{3,99},{4,100},{5,101},{6,102},{7,103},{8,40}... | collective-permute-start | bytes 1966088 | tf_op jit(solution)/shard_map/ppermute | solution.py:23
  58.1 17.8 %collective-permute-start.12 = (bf16[512,1280]{1,0:T(8,128)(2,1)S(1)}, bf16[512,1280]{1,0:T(8,128)(2,1)S(1)}, u32[]{:S(2)}, u32[]{:S(2)}) collective-permute-start(bf16[512,1280]{1,0:T(8,128)(2,1)S(1)} %constant_dynamic-update-slice_fusion), channel_id=1, source_target_pairs={{0,8},{1,9},{2,10},{3,11},{4,12},{5,13},{6,14},{7,15},{8,0},{9,1},... | collective-permute-start | bytes 3932168 | tf_op jit(solution)/shard_map/ppermute | solution.py:23
  84.7 30.2 %collective-permute-start.31 = (bf16[2,2,256,640]{3,2,1,0:T(8,128)(2,1)S(1)}, bf16[2,2,256,640]{3,2,1,0:T(8,128)(2,1)S(1)}, u32[]{:S(2)}, u32[]{:S(2)}) collective-permute-start(bf16[2,2,256,640]{3,2,1,0:T(8,128)(2,1)S(1)} %get-tuple-element.51), channel_id=1, source_target_pairs={{0,96},{1,97},{2,98},{3,99},{4,100},{5,101},{6,102},{7,103},{8,40}... | collective-permute-start | bytes 3932168 | tf_op jit(solution)/shard_map/ppermute | solution.py:23
  95.1 18.7 %collective-permute-start.23 = (bf16[2,1024,256]{2,1,0:T(8,128)(2,1)S(1)}, bf16[2,1024,256]{2,1,0:T(8,128)(2,1)S(1)}, u32[]{:S(2)}, u32[]{:S(2)}) collective-permute-start(bf16[2,1024,256]{2,1,0:T(8,128)(2,1)S(1)} %get-tuple-element.42), channel_id=1, source_target_pairs={{0,3},{1,2},{2,1},{3,0},{4,7},{5,6},{6,5},{7,4},{8,9},{9,8},{10,11... | collective-permute-start | bytes 3145736 | tf_op jit(solution)/shard_map/ppermute | solution.py:23
  107.4 10.1 %collective-permute-start.21 = (bf16[512,1280]{1,0:T(8,128)(2,1)S(1)}, bf16[512,1280]{1,0:T(8,128)(2,1)S(1)}, u32[]{:S(2)}, u32[]{:S(2)}) collective-permute-start(bf16[512,1280]{1,0:T(8,128)(2,1)S(1)} %get-tuple-element.40), channel_id=1, source_target_pairs={{0,8},{1,9},{2,10},{3,11},{4,12},{5,13},{6,14},{7,15},{8,0},{9,1},... | collective-permute-start | bytes 3932168 | tf_op jit(solution)/shard_map/ppermute | solution.py:23
  109.8 17.7 %collective-permute-start.29 = (bf16[2,2,256,640]{3,2,1,0:T(8,128)(2,1)S(1)}, bf16[2,2,256,640]{3,2,1,0:T(8,128)(2,1)S(1)}, u32[]{:S(2)}, u32[]{:S(2)}) collective-permute-start(bf16[2,2,256,640]{3,2,1,0:T(8,128)(2,1)S(1)} %get-tuple-element.49), channel_id=1, source_target_pairs={{0,32},{1,33},{2,34},{3,35},{4,36},{5,37},{6,38},{7,39},{8,104},{9... | collective-permute-start | bytes 3932168 | tf_op jit(solution)/shard_map/ppermute | solution.py:23
  110.8 18.0 %collective-permute-start.25 = (bf16[2,1024,256]{2,1,0:T(8,128)(2,1)}, bf16[2,1024,256]{2,1,0:T(8,128)(2,1)}, u32[]{:S(2)}, u32[]{:S(2)}) collective-permute-start(bf16[2,1024,256]{2,1,0:T(8,128)(2,1)} %get-tuple-element.45), channel_id=1, source_target_pairs={{0,1},{1,0},{2,3},{3,2},{4,5},{5,4},{6,7},{7,6},{8,11},{9,10},{10,... | collective-permute-start | bytes 3145736 | tf_op jit(solution)/shard_map/ppermute | solution.py:23
  113.7 2.3 %copy-start.6 = (bf16[2,1024,256]{2,1,0:T(8,128)(2,1)}, bf16[2,1024,256]{2,1,0:T(8,128)(2,1)S(1)}, u32[]{:S(2)}) copy-start(bf16[2,1024,256]{2,1,0:T(8,128)(2,1)S(1)} %collective-permute-done.23) | copy-start | bytes 3145732
  114.9 17.0 %collective-permute-start.24 = (bf16[1024,256]{1,0:T(8,128)(2,1)}, bf16[1024,256]{1,0:T(8,128)(2,1)}, u32[]{:S(2)}, u32[]{:S(2)}) collective-permute-start(bf16[1024,256]{1,0:T(8,128)(2,1)} %fusion.6), channel_id=1, source_target_pairs={{0,1},{1,0},{2,3},{3,2},{4,5},{5,4},{6,7},{7,6},{8,11},{9,10},{10,... | collective-permute-start | bytes 1572872 | tf_op jit(solution)/shard_map/ppermute | solution.py:23
  114.9 2.9 %copy-start.2 = (bf16[2,2,256,640]{3,2,1,0:T(8,128)(2,1)}, bf16[2,2,256,640]{3,2,1,0:T(8,128)(2,1)S(1)}, u32[]{:S(2)}) copy-start(bf16[2,2,256,640]{3,2,1,0:T(8,128)(2,1)S(1)} %collective-permute-done.31) | copy-start | bytes 3932164
  116.1 20.2 %collective-permute-start.32 = (bf16[2,256,640]{2,1,0:T(8,128)(2,1)}, bf16[2,256,640]{2,1,0:T(8,128)(2,1)}, u32[]{:S(2)}, u32[]{:S(2)}) collective-permute-start(bf16[2,256,640]{2,1,0:T(8,128)(2,1)} %fusion.4), channel_id=1, source_target_pairs={{0,32},{1,33},{2,34},{3,35},{4,36},{5,37},{6,38},{7,39},{8,104},{9... | collective-permute-start | bytes 1966088 | tf_op jit(solution)/shard_map/ppermute | solution.py:23
  117.8 10.9 %copy-start = (f32[512,1280]{1,0:T(8,128)}, f32[512,1280]{1,0:T(8,128)S(1)}, u32[]{:S(2)}) copy-start(f32[512,1280]{1,0:T(8,128)S(1)} %convert_add_fusion) | copy-start | bytes 7864324
  118.8 16.3 %collective-permute-start.22 = (bf16[512,640]{1,0:T(8,128)(2,1)}, bf16[512,640]{1,0:T(8,128)(2,1)S(1)}, u32[]{:S(2)}, u32[]{:S(2)}) collective-permute-start(bf16[512,640]{1,0:T(8,128)(2,1)} %slice.191), channel_id=1, source_target_pairs={{0,4},{1,5},{2,6},{3,7},{4,0},{5,1},{6,2},{7,3},{8,12},{9,13},{10,... | collective-permute-start | bytes 1966088 | tf_op jit(solution)/shard_map/ppermute | solution.py:23
  127.5 1.3 copy-start.4
  128.8 12.5 %collective-permute-start.30 = (bf16[2,256,640]{2,1,0:T(8,128)(2,1)}, bf16[2,256,640]{2,1,0:T(8,128)(2,1)}, u32[]{:S(2)}, u32[]{:S(2)}) collective-permute-start(bf16[2,256,640]{2,1,0:T(8,128)(2,1)} %fusion.3), channel_id=1, source_target_pairs={{0,96},{1,97},{2,98},{3,99},{4,100},{5,101},{6,102},{7,103},{8,40}... | collective-permute-start | bytes 1966088 | tf_op jit(solution)/shard_map/ppermute | solution.py:23
  128.8 3.1 %copy-start.7 = (bf16[2,1024,256]{2,1,0:T(8,128)(2,1)S(1)}, bf16[2,1024,256]{2,1,0:T(8,128)(2,1)}, u32[]{:S(2)}) copy-start(bf16[2,1024,256]{2,1,0:T(8,128)(2,1)} %copy-done.6) | copy-start | bytes 3145732
  128.8 12.5 %copy-start.5 = (bf16[2,2,256,640]{3,2,1,0:T(8,128)(2,1)S(1)}, bf16[2,2,256,640]{3,2,1,0:T(8,128)(2,1)}, u32[]{:S(2)}) copy-start(bf16[2,2,256,640]{3,2,1,0:T(8,128)(2,1)} %copy-done.4) | copy-start | bytes 3932164
  130.1 11.2 %copy-start.3 = (bf16[2,2,256,640]{3,2,1,0:T(8,128)(2,1)S(1)}, bf16[2,2,256,640]{3,2,1,0:T(8,128)(2,1)}, u32[]{:S(2)}) copy-start(bf16[2,2,256,640]{3,2,1,0:T(8,128)(2,1)} %copy-done.2) | copy-start | bytes 3932164
  130.1 17.0 %collective-permute-start.26 = (bf16[1024,256]{1,0:T(8,128)(2,1)S(1)}, bf16[1024,256]{1,0:T(8,128)(2,1)S(1)}, u32[]{:S(2)}, u32[]{:S(2)}) collective-permute-start(bf16[1024,256]{1,0:T(8,128)(2,1)S(1)} %fusion.7), channel_id=1, source_target_pairs={{0,3},{1,2},{2,1},{3,0},{4,7},{5,6},{6,5},{7,4},{8,9},{9,8},{10,11... | collective-permute-start | bytes 1572872 | tf_op jit(solution)/shard_map/ppermute | solution.py:23
  135.1 12.5 %collective-permute-start.27 = (bf16[1024,256]{1,0:T(8,128)(2,1)S(1)}, bf16[1024,256]{1,0:T(8,128)(2,1)S(1)}, u32[]{:S(2)}, u32[]{:S(2)}) collective-permute-start(bf16[1024,256]{1,0:T(8,128)(2,1)S(1)} %bitcast_add_fusion.3), channel_id=1, source_target_pairs={{0,4},{1,5},{2,6},{3,7},{4,0},{5,1},{6,2},{7,3},{8,12},{9,13},{10,... | collective-permute-start | bytes 1572872 | tf_op jit(solution)/shard_map/ppermute | solution.py:23
  141.3 4.9 %copy-start.1 = (f32[512,1280]{1,0:T(8,128)S(1)}, f32[512,1280]{1,0:T(8,128)}, u32[]{:S(2)}) copy-start(f32[512,1280]{1,0:T(8,128)} %copy-done) | copy-start | bytes 7864324
  143.3 18.5 %collective-permute-start.33 = (bf16[256,640]{1,0:T(8,128)(2,1)S(1)}, bf16[256,640]{1,0:T(8,128)(2,1)S(1)}, u32[]{:S(2)}, u32[]{:S(2)}) collective-permute-start(bf16[256,640]{1,0:T(8,128)(2,1)S(1)} %get-tuple-element.65), channel_id=1, source_target_pairs={{0,16},{1,17},{2,18},{3,19},{4,20},{5,21},{6,22},{7,23},{8,24},{9,... | collective-permute-start | bytes 983048 | tf_op jit(solution)/shard_map/ppermute | solution.py:23
  143.8 16.2 %collective-permute-start.34 = (bf16[256,640]{1,0:T(8,128)(2,1)S(1)}, bf16[256,640]{1,0:T(8,128)(2,1)S(1)}, u32[]{:S(2)}, u32[]{:S(2)}) collective-permute-start(bf16[256,640]{1,0:T(8,128)(2,1)S(1)} %get-tuple-element.57), channel_id=1, source_target_pairs={{0,4},{1,5},{2,6},{3,7},{4,0},{5,1},{6,2},{7,3},{8,28},{9,29},{10,... | collective-permute-start | bytes 983048 | tf_op jit(solution)/shard_map/ppermute | solution.py:23
  146.1 15.5 %collective-permute-start.35 = (bf16[256,640]{1,0:T(8,128)(2,1)S(1)}, bf16[256,640]{1,0:T(8,128)(2,1)S(1)}, u32[]{:S(2)}, u32[]{:S(2)}) collective-permute-start(bf16[256,640]{1,0:T(8,128)(2,1)S(1)} %get-tuple-element.58), channel_id=1, source_target_pairs={{0,20},{1,21},{2,22},{3,23},{4,16},{5,17},{6,18},{7,19},{8,12},{9,... | collective-permute-start | bytes 983048 | tf_op jit(solution)/shard_map/ppermute | solution.py:23
  149.0 14.0 %collective-permute-start.28 = (bf16[512,512]{1,0:T(8,128)(2,1)S(1)}, bf16[512,512]{1,0:T(8,128)(2,1)S(1)}, u32[]{:S(2)}, u32[]{:S(2)}) collective-permute-start(bf16[512,512]{1,0:T(8,128)(2,1)S(1)} %pad_maximum_fusion.6), channel_id=1, source_target_pairs={{0,8},{1,9},{2,10},{3,11},{4,12},{5,13},{6,14},{7,15},{8,0},{9,1},... | collective-permute-start | bytes 1572872 | tf_op jit(solution)/shard_map/ppermute | solution.py:23

commit v3 on v2

--- a/solution.py
+++ b/solution.py
@@ -132,11 +132,8 @@
 
 
 def da_kernel(groups, m, g, w0, w1, *outs):
-    cols = w0.shape[-1]
-    contract = (((1,), (1,)), ((), ()))
-    block = lax.dot_general(g[:, :cols], w0[0, 0], contract, preferred_element_type=F32)
-    block += lax.dot_general(g[:, cols:], w1[0, 0], contract, preferred_element_type=F32)
-    block = block.astype(BF16)
+    rows = jnp.concatenate([w0[0, 0], w1[0, 0]], 1)
+    block = lax.dot_general(g[...], rows, (((1,), (1,)), ((), ())), preferred_element_type=F32).astype(BF16)
 
     def store(out):
         out[...] = block
@@ -172,54 +169,51 @@
     )(scalars, g, w, w)
 
 
-def fwd_kernel(m, a0, a1, w, mine, theirs, total):
-    k = pl.program_id(0)
+def fwd_kernel(m, a, w, mine, theirs, rows):
+    n, d = a.shape[0], a.shape[2]
     cols = w.shape[-1]
-    t = mine.shape[0]
-
-    def dot(left, right):
-        return jnp.dot(left, right, preferred_element_type=F32)
-
-    for ylo in range(2):
-        s0, s1 = sub_of(0, ylo, m), sub_of(1, ylo, m)
-        part = dot(a0[0], w[0, s0]) + dot(a1[0], w[0, s1])
-        at = slice(ylo * cols, (ylo + 1) * cols)
-
-        @pl.when(k == 0)
-        def _():
-            total[:, at] = part
-
-        @pl.when((k > 0) & (k < 3))
-        def _():
-            total[:, at] += part
-
-        @pl.when(k == 3)
-        def _():
-            final = (total[:, at] + part).astype(BF16)
-            mine[:, at] = final[:t]
-            theirs[:, at] = final[t:]
+
+    @pl.when(pl.program_id(0) == 0)
+    def _():
+        for k in range(n):
+            for ylo in range(2):
+                rows[k * d : (k + 1) * d, ylo * cols : (ylo + 1) * cols] = w[k // 2, sub_of(k % 2, ylo, m)]
+
+    left = jnp.concatenate([a[a_block(k // 2, k % 2, m)] for k in range(n)], 1)
+    block = jnp.dot(left, rows[...], preferred_element_type=F32).astype(BF16)
+
+    @pl.when(pl.program_id(0) < 2)
+    def _():
+        theirs[...] = block
+
+    @pl.when(pl.program_id(0) >= 2)
+    def _():
+        mine[...] = block
 
 
 def forward_terms(scalars, a, w):
-    t, d, cols = a.shape[1], a.shape[2], w.shape[3]
+    n, t, d = a.shape
+    cols = w.shape[3]
     return pl.pallas_call(
         fwd_kernel,
         grid_spec=pltpu.PrefetchScalarGridSpec(
             num_scalar_prefetch=1,
             grid=(4,),
             in_specs=[
-                pl.BlockSpec((1, t, d), lambda k, m: (a_block(k, 0, m), 0, 0)),
-                pl.BlockSpec((1, t, d), lambda k, m: (a_block(k, 1, m), 0, 0)),
-                pl.BlockSpec((1, *w.shape[1:]), lambda k, m: (k, 0, 0, 0)),
+                pl.BlockSpec((n, t // 4, d), lambda i, m: (0, (i + 2) % 4, 0)),
+                pl.BlockSpec(w.shape, lambda i, m: (0, 0, 0, 0)),
             ],
-            out_specs=[pl.BlockSpec((t // 2, 2 * cols), lambda k, m: (0, 0))] * 2,
-            scratch_shapes=[pltpu.VMEM((t, 2 * cols), F32)],
+            out_specs=[
+                pl.BlockSpec((t // 4, 2 * cols), lambda i, m: (jnp.maximum(i - 2, 0), 0)),
+                pl.BlockSpec((t // 4, 2 * cols), lambda i, m: (jnp.minimum(i, 1), 0)),
+            ],
+            scratch_shapes=[pltpu.VMEM((n * d, 2 * cols), BF16)],
         ),
         out_shape=[jax.ShapeDtypeStruct((t // 2, 2 * cols), BF16)] * 2,
         compiler_params=pltpu.CompilerParams(vmem_limit_bytes=40 << 20),
         cost_estimate=cost(8 * t * d * 2 * cols),
         name="forward_terms",
-    )(scalars, a, a, w)
+    )(scalars, a, w)
 
 
 def body(activations, qkv_weight, qkv_grad):
@@ -258,13 +252,13 @@
     a = jnp.stack([a_keep, ka_one, ka_far, ka_two, a_y, ya_one, ya_far, ya_two])
 
     w_own, w_1, w_2 = (jnp.concatenate(v, 0) for v in ((w_same, w_near), (ws_one, wn_one), (ws_two, wn_two)))
-    w_2far = jnp.concatenate([flip(w_2[: 2 * sub], x=ONE), flip(w_1[2 * sub :], x=TWO)], 0)
-    w = jnp.stack([w_own, w_1, w_2far, w_2]).reshape(4, 4, sub, cols)
+    far_one, far_two = flip(w_2[: 2 * sub], x=ONE), flip(w_1[2 * sub :], x=TWO)
     g_rows = jnp.concatenate([grad, g_y], 1)
     g = jnp.concatenate([g_rows, flip(g_rows, c=1)], 0)
 
     dw_first, *dw = weight_terms(scalars, a, g)
-    dw_first, scalars = tie(dw_first, scalars)
+    dw_first, far_one, far_two = tie(dw_first, far_one, far_two)
+    w = jnp.stack([w_own, w_1, jnp.concatenate([far_one, far_two], 0), w_2]).reshape(4, 4, sub, cols)
     da_first, *da = input_terms(scalars, g, w)
     da_first, scalars = tie(da_first, scalars)
     da_keep, da_send = scatter4(da_first, *da, "z")

time: 165 us -> 159 us (0.964)
  Pallas kernels: 31.2 us -> 25.7 us
  waiting for transfers between devices: 67 us -> 63.8 us
    pallas_call x1, Pallas kernels: 12.3 us -> 7.66 us  [forward_terms(): pl.pallas_call(fwd_kernel, grid_spec=pltpu.PrefetchScalarGridSpec(num_sca...]
    ppermute x36, waiting for transfers between devices: 67 us -> 63.8 us  [flip(): return lax.ppermute(value, AXES, pairs)]
  transfers between devices with their start and end apart: 36 -> 36, of which waited for: 19 -> 13; matrix products, arithmetic and copies ran while one was open for 9% -> 11% of each run, Pallas kernels for 14% -> 16%
where the time goes in v3:
time: 159 us; the launch traced here: 158 us
  waiting for transfers between devices  63.8 us (40%)
  starting transfers between devices  48 us (30%)
  Pallas kernels  25.7 us (16%)
  other arithmetic  17.5 us (11%)
  local copies, waits for them, and re-layouts  1.93 us (1%)
    ppermute x36, waiting for transfers between devices, flip(): return lax.ppermute(value, AXES, pairs)  63.8 us
    ppermute x36, starting transfers between devices, flip(): return lax.ppermute(value, AXES, pairs)  48 us
    pallas_call x1, Pallas kernels, input_terms(): pl.pallas_call(functools.partial(da_kernel, groups), grid_spec=pltpu.Pref...  9.4 us
    pallas_call x1, Pallas kernels, weight_terms(): pl.pallas_call(functools.partial(dw_kernel, groups), grid_spec=pltpu.Pref...  8.63 us
    pallas_call x1, Pallas kernels, forward_terms(): pl.pallas_call(fwd_kernel, grid_spec=pltpu.PrefetchScalarGridSpec(num_sca...  7.66 us
    add x5, other arithmetic, add(): total = total + term.astype(F32)  3.71 us
    convert_element_type x2, other arithmetic, scatter4(): got_bottom1 = flip(add(one[0], got_two[0]).astype(BF16), **{axis: ONE})  3.27 us
  transfers between devices with their start and end apart: 36, of which 13 were waited for; matrix products, arithmetic and copies ran while one was open for 11% of the time, Pallas kernels for 16%

profile of v3, /device:TPU:1, one launch (start us, length us, event | category | flops | bytes accessed | tf_op | source)
XLA Modules:
  0.0 158.1 jit_solution(4405363275857935930)
XLA Ops:
  0.7 1.3 broadcast_select_fusion.4
  2.0 1.5 collective-permute-start.1
  3.6 2.9 %collective-permute-start = (bf16[256,640]{1,0:T(8,128)(2,1)S(1)}, bf16[256,640]{1,0:T(8,128)(2,1)S(1)}, u32[]{:S(2)}, u32[]{:S(2)}) collective-permute-start(bf16[256,640]{1,0:T(8,128)(2,1)S(1)} %get-tuple-element.69), channel_id=1, source_target_pairs={{0,4},{1,5},{2,6},{3,7},{4,0},{5,1},{6,2},{7,3},{8,28},{9,29},{10,... | collective-permute-start | bytes 983048 | tf_op jit(solution)/shard_map/ppermute | solution.py:23
  6.5 2.5 %collective-permute-start.5 = (bf16[256,640]{1,0:T(8,128)(2,1)S(1)}, bf16[256,640]{1,0:T(8,128)(2,1)S(1)}, u32[]{:S(2)}, u32[]{:S(2)}) collective-permute-start(bf16[256,640]{1,0:T(8,128)(2,1)S(1)} %get-tuple-element.31), channel_id=1, source_target_pairs={{0,32},{1,33},{2,34},{3,35},{4,36},{5,37},{6,38},{7,39},{8,104},{9... | collective-permute-start | bytes 983048 | tf_op jit(solution)/shard_map/ppermute | solution.py:23
  9.0 1.9 %collective-permute-done = bf16[256,640]{1,0:T(8,128)(2,1)S(1)} collective-permute-done((bf16[256,640]{1,0:T(8,128)(2,1)S(1)}, bf16[256,640]{1,0:T(8,128)(2,1)S(1)}, u32[]{:S(2)}, u32[]{:S(2)}) %collective-permute-start) | collective-permute-done | bytes 327712 | tf_op jit(solution)/shard_map/ppermute | solution.py:23
  10.9 0.3 collective-permute-start.2
  11.3 5.2 %collective-permute-done.5 = bf16[256,640]{1,0:T(8,128)(2,1)S(1)} collective-permute-done((bf16[256,640]{1,0:T(8,128)(2,1)S(1)}, bf16[256,640]{1,0:T(8,128)(2,1)S(1)}, u32[]{:S(2)}, u32[]{:S(2)}) %collective-permute-start.5) | collective-permute-done | bytes 327712 | tf_op jit(solution)/shard_map/ppermute | solution.py:23
  16.6 1.6 %collective-permute-start.7 = (bf16[256,640]{1,0:T(8,128)(2,1)S(1)}, bf16[256,640]{1,0:T(8,128)(2,1)S(1)}, u32[]{:S(2)}, u32[]{:S(2)}) collective-permute-start(bf16[256,640]{1,0:T(8,128)(2,1)S(1)} %get-tuple-element.31), channel_id=1, source_target_pairs={{0,16},{1,17},{2,18},{3,19},{4,20},{5,21},{6,22},{7,23},{8,24},{9,... | collective-permute-start | bytes 983048 | tf_op jit(solution)/shard_map/ppermute | solution.py:23
  18.3 3.8 %collective-permute-start.10 = (bf16[1024,256]{1,0:T(8,128)(2,1)S(1)}, bf16[1024,256]{1,0:T(8,128)(2,1)S(1)}, u32[]{:S(2)}, u32[]{:S(2)}) collective-permute-start(bf16[1024,256]{1,0:T(8,128)(2,1)S(1)} %get-tuple-element.56), channel_id=1, source_target_pairs={{0,1},{1,0},{2,3},{3,2},{4,5},{5,4},{6,7},{7,6},{8,11},{9,10},{10,... | collective-permute-start | bytes 1572872 | tf_op jit(solution)/shard_map/ppermute | solution.py:23
  22.2 11.0 %collective-permute-done.7 = bf16[256,640]{1,0:T(8,128)(2,1)S(1)} collective-permute-done((bf16[256,640]{1,0:T(8,128)(2,1)S(1)}, bf16[256,640]{1,0:T(8,128)(2,1)S(1)}, u32[]{:S(2)}, u32[]{:S(2)}) %collective-permute-start.7) | collective-permute-done | bytes 327712 | tf_op jit(solution)/shard_map/ppermute | solution.py:23
  33.4 1.5 collective-permute-start.18
  34.9 1.8 %collective-permute-start.9 = (bf16[768,640]{1,0:T(8,128)(2,1)S(1)}, bf16[768,640]{1,0:T(8,128)(2,1)S(1)}, u32[]{:S(2)}, u32[]{:S(2)}) collective-permute-start(bf16[768,640]{1,0:T(8,128)(2,1)S(1)} %constant_dynamic-update-slice_fusion.2), channel_id=1, source_target_pairs={{0,32},{1,33},{2,34},{3,35},{4,36},{5,37},{6,38},{7,39},{8,104},{9... | collective-permute-start | bytes 2949128 | tf_op jit(solution)/shard_map/ppermute | solution.py:23
  36.7 0.1 pad_maximum_fusion.2
  36.9 3.8 %collective-permute-start.12 = (bf16[512,256]{1,0:T(8,128)(2,1)S(1)}, bf16[512,256]{1,0:T(8,128)(2,1)S(1)}, u32[]{:S(2)}, u32[]{:S(2)}) collective-permute-start(bf16[512,256]{1,0:T(8,128)(2,1)S(1)} %slice.116), channel_id=1, source_target_pairs={{0,1},{1,0},{2,3},{3,2},{4,5},{5,4},{6,7},{7,6},{8,11},{9,10},{10,... | collective-permute-start | bytes 786440 | tf_op jit(solution)/shard_map/ppermute | solution.py:23
  41.0 3.8 %collective-permute-done.12 = bf16[512,256]{1,0:T(8,128)(2,1)S(1)} collective-permute-done((bf16[512,256]{1,0:T(8,128)(2,1)S(1)}, bf16[512,256]{1,0:T(8,128)(2,1)S(1)}, u32[]{:S(2)}, u32[]{:S(2)}) %collective-permute-start.12) | collective-permute-done | bytes 262176 | tf_op jit(solution)/shard_map/ppermute | solution.py:23
  44.8 2.7 %collective-permute-start.14 = (bf16[1024,256]{1,0:T(8,128)(2,1)S(1)}, bf16[1024,256]{1,0:T(8,128)(2,1)S(1)}, u32[]{:S(2)}, u32[]{:S(2)}) collective-permute-start(bf16[1024,256]{1,0:T(8,128)(2,1)S(1)} %collective-permute-done.2), channel_id=1, source_target_pairs={{0,1},{1,0},{2,3},{3,2},{4,5},{5,4},{6,7},{7,6},{8,11},{9,10},{10,... | collective-permute-start | bytes 1572872 | tf_op jit(solution)/shard_map/ppermute | solution.py:23
  47.5 0.8 collective-permute-done.13
  48.2 0.3 collective-permute-start.15
  48.6 0.1 constant_dynamic-update-slice_fusion
  48.7 3.1 %collective-permute-start.4 = (bf16[512,1280]{1,0:T(8,128)(2,1)S(1)}, bf16[512,1280]{1,0:T(8,128)(2,1)S(1)}, u32[]{:S(2)}, u32[]{:S(2)}) collective-permute-start(bf16[512,1280]{1,0:T(8,128)(2,1)S(1)} %constant_dynamic-update-slice_fusion), channel_id=1, source_target_pairs={{0,8},{1,9},{2,10},{3,11},{4,12},{5,13},{6,14},{7,15},{8,0},{9,1},... | collective-permute-start | bytes 3932168 | tf_op jit(solution)/shard_map/ppermute | solution.py:23
  51.9 10.2 %collective-permute-done.15 = bf16[1024,256]{1,0:T(8,128)(2,1)S(1)} collective-permute-done((bf16[1024,256]{1,0:T(8,128)(2,1)S(1)}, bf16[1024,256]{1,0:T(8,128)(2,1)S(1)}, u32[]{:S(2)}, u32[]{:S(2)}) %collective-permute-start.15) | collective-permute-done | bytes 524320 | tf_op jit(solution)/shard_map/ppermute | solution.py:23
  62.2 0.1 collective-permute-start.16
  62.4 0.2 constant_dynamic-update-slice_fusion.5
  62.7 0.5 collective-permute-start.19
  63.4 0.1 pad_maximum_fusion.3
  63.5 7.4 %collective-permute-done.16 = bf16[512,256]{1,0:T(8,128)(2,1)S(1)} collective-permute-done((bf16[512,256]{1,0:T(8,128)(2,1)S(1)}, bf16[512,256]{1,0:T(8,128)(2,1)S(1)}, u32[]{:S(2)}, u32[]{:S(2)}) %collective-permute-start.16) | collective-permute-done | bytes 262176 | tf_op jit(solution)/shard_map/ppermute | solution.py:23
  71.0 0.2 pad_maximum_fusion.1.g
  71.2 8.6 %weight_terms.1 = (bf16[2,2,256,640]{3,2,1,0:T(8,128)(2,1)S(1)}, bf16[2,2,256,640]{3,2,1,0:T(8,128)(2,1)S(1)}, bf16[1,2,256,640]{3,2,1,0:T(8,128)(2,1)S(1)}, bf1...) custom-call(s32[2]{0:T(128)S(1)} %pad_add_fusion.m, ...), custom_call_target="tpu_custom_call" | custom-call | flops 10737418240 | bytes 5242880 | tf_op jit(solution)/shard_map/weight_terms/pallas_call | solution.py:119
  79.8 0.1 collective-permute-start.31
  79.9 0.1 pad_maximum_fusion.4
  80.0 1.0 pad_maximum_fusion.w0.w1.w
  81.1 9.4 %input_terms.1 = (bf16[2,1024,256]{2,1,0:T(8,128)(2,1)}, bf16[2,1024,256]{2,1,0:T(8,128)(2,1)S(1)}, bf16[1,1024,256]{2,1,0:T(8,128)(2,1)S(1)}, bf16[1,1024,256]{...) custom-call(s32[2]{0:T(128)S(1)} %pad_add_fusion.m, bf16[1024,1280]{1,0:T(8,128)(2,1)S(1)} %pad_maximum_fusion.1.g, ...), custom_call_target="tpu_custom_call" | custom-call | flops 10737418240 | bytes 5242880 | tf_op jit(solution)/shard_map/input_terms/pallas_call | solution.py:153
  90.5 0.1 collective-permute-start.23
  90.6 7.7 %forward_terms.1 = (bf16[512,1280]{1,0:T(8,128)(2,1)S(1)}, bf16[512,1280]{1,0:T(8,128)(2,1)S(1)}) custom-call(s32[2]{0:T(128)S(1)} %pad_add_fusion.m, bf16[8,1024,256]{2,1,0:T(8,128)(2,1)S(1)} %bitcast_dynamic-update-slice_fusion.a, bf16[4,4,256,640]{3,2,1,0:T(8,128)(2,1)S(1)} %pad_maximum_fusion.w0.w1.w), custom_call_target="tpu_custom_call" | custom-call | flops 10737418240 | bytes 5242880 | tf_op jit(solution)/shard_map/forward_terms/pallas_call | solution.py:197
  98.3 4.1 %collective-permute-start.21 = (bf16[512,1280]{1,0:T(8,128)(2,1)S(1)}, bf16[512,1280]{1,0:T(8,128)(2,1)S(1)}, u32[]{:S(2)}, u32[]{:S(2)}) collective-permute-start(bf16[512,1280]{1,0:T(8,128)(2,1)S(1)} %get-tuple-element.42), channel_id=1, source_target_pairs={{0,8},{1,9},{2,10},{3,11},{4,12},{5,13},{6,14},{7,15},{8,0},{9,1},... | collective-permute-start | bytes 3932168 | tf_op jit(solution)/shard_map/ppermute | solution.py:23
  102.4 0.4 collective-permute-start.29
  102.7 2.7 %collective-permute-start.25 = (bf16[2,1024,256]{2,1,0:T(8,128)(2,1)}, bf16[2,1024,256]{2,1,0:T(8,128)(2,1)}, u32[]{:S(2)}, u32[]{:S(2)}) collective-permute-start(bf16[2,1024,256]{2,1,0:T(8,128)(2,1)} %get-tuple-element.47), channel_id=1, source_target_pairs={{0,1},{1,0},{2,3},{3,2},{4,5},{5,4},{6,7},{7,6},{8,11},{9,10},{10,... | collective-permute-start | bytes 3145736 | tf_op jit(solution)/shard_map/ppermute | solution.py:23
  105.4 1.1 fusion.6
  106.5 3.2 %collective-permute-start.24 = (bf16[1024,256]{1,0:T(8,128)(2,1)}, bf16[1024,256]{1,0:T(8,128)(2,1)}, u32[]{:S(2)}, u32[]{:S(2)}) collective-permute-start(bf16[1024,256]{1,0:T(8,128)(2,1)} %fusion.6), channel_id=1, source_target_pairs={{0,1},{1,0},{2,3},{3,2},{4,5},{5,4},{6,7},{7,6},{8,11},{9,10},{10,... | collective-permute-start | bytes 1572872 | tf_op jit(solution)/shard_map/ppermute | solution.py:23
  109.8 2.2 %fusion.4 = bf16[2,256,640]{2,1,0:T(8,128)(2,1)} fusion(bf16[1,2,256,640]{3,2,1,0:T(8,128)(2,1)S(1)} %get-tuple-element.54, bf16[2,2,256,640]{3,2,1,0:T(8,128)(2,1)} %collective-permute-done.31), kind=kLoop, calls=%fused_computation.28 | loop fusion | flops 1310720 | bytes 1966080 | tf_op jit(solution)/shard_map/convert_element_type | solution.py:49
  111.9 0.3 convert_add_fusion
  112.2 1.0 slice.191
  113.2 1.2 collective-permute-start.22
  114.4 5.6 %collective-permute-done.29 = bf16[2,2,256,640]{3,2,1,0:T(8,128)(2,1)S(1)} collective-permute-done((bf16[2,2,256,640]{3,2,1,0:T(8,128)(2,1)S(1)}, bf16[2,2,256,640]{3,2,1,0:T(8,128)(2,1)S(1)}, u32[]{:S(2)}, u32[]{:S(2)}) %collective-permute-start.29) | collective-permute-done | bytes 1310752 | tf_op jit(solution)/shard_map/ppermute | solution.py:23
  120.0 1.2 fusion.3
  121.3 1.3 fusion.7
  122.6 0.9 collective-permute-start.26
  123.5 0.8 collective-permute-done.24
  124.3 1.2 bitcast_add_fusion.3
  125.6 1.4 collective-permute-done.22
  127.0 1.3 collective-permute-start.27
  128.3 0.5 collective-permute-done.32
  128.8 5.0 %collective-permute-done.30 = bf16[2,256,640]{2,1,0:T(8,128)(2,1)} collective-permute-done((bf16[2,256,640]{2,1,0:T(8,128)(2,1)}, bf16[2,256,640]{2,1,0:T(8,128)(2,1)}, u32[]{:S(2)}, u32[]{:S(2)}) %collective-permute-start.30) | collective-permute-done | bytes 655392 | tf_op jit(solution)/shard_map/ppermute | solution.py:23
  133.8 2.1 %bitcast_add_fusion.1 = (f32[2,256,640]{2,1,0:T(8,128)S(1)}, bf16[2,256,640]{2,1,0:T(8,128)(2,1)S(1)}) fusion(bf16[2,256,640]{2,1,0:T(8,128)(2,1)} %collective-permute-done.30, bf16[2,2,256,640]{3,2,1,0:T(8,128)(2,1)S(1)} %copy-done.3, bf16[2,2,256,640]{3,2,1,0:T(8,128)(2,1)S(1)} %get-tuple-element.50, bf16[2,256,640]{2,1,0:T(8,128)(2,1)} %collective-permute-done.32, ...), kind=kLoop, calls=%fused_computation.12 | loop fusion | flops 3604480 | bytes 5898240 | tf_op jit(solution)/shard_map/add | solution.py:36
  135.9 0.1 select_bitcast_fusion.1
  136.0 3.7 %collective-permute-start.33 = (bf16[256,640]{1,0:T(8,128)(2,1)S(1)}, bf16[256,640]{1,0:T(8,128)(2,1)S(1)}, u32[]{:S(2)}, u32[]{:S(2)}) collective-permute-start(bf16[256,640]{1,0:T(8,128)(2,1)S(1)} %get-tuple-element.67), channel_id=1, source_target_pairs={{0,16},{1,17},{2,18},{3,19},{4,20},{5,21},{6,22},{7,23},{8,24},{9,... | collective-permute-start | bytes 983048 | tf_op jit(solution)/shard_map/ppermute | solution.py:23
  139.7 0.3 collective-permute-start.34
  140.0 1.0 fusion
  141.0 1.4 broadcast_select_fusion.1
  142.4 3.2 %collective-permute-start.28 = (bf16[512,512]{1,0:T(8,128)(2,1)S(1)}, bf16[512,512]{1,0:T(8,128)(2,1)S(1)}, u32[]{:S(2)}, u32[]{:S(2)}) collective-permute-start(bf16[512,512]{1,0:T(8,128)(2,1)S(1)} %pad_maximum_fusion.6), channel_id=1, source_target_pairs={{0,8},{1,9},{2,10},{3,11},{4,12},{5,13},{6,14},{7,15},{8,0},{9,1},... | collective-permute-start | bytes 1572872 | tf_op jit(solution)/shard_map/ppermute | solution.py:23
  145.6 9.9 %collective-permute-done.34 = bf16[256,640]{1,0:T(8,128)(2,1)S(1)} collective-permute-done((bf16[256,640]{1,0:T(8,128)(2,1)S(1)}, bf16[256,640]{1,0:T(8,128)(2,1)S(1)}, u32[]{:S(2)}, u32[]{:S(2)}) %collective-permute-start.34) | collective-permute-done | bytes 327712 | tf_op jit(solution)/shard_map/ppermute | solution.py:23
  155.6 1.1 maximum_select_fusion
  156.8 0.2 broadcast_select_fusion.3
  157.0 1.1 pad_maximum_fusion.5
  (74 shorter events, 1.5 us)
Async XLA Ops:
  0.6 2.9 %copy-start.7 = (bf16[512,640]{1,0:T(8,128)(2,1)S(1)}, bf16[512,640]{1,0:T(8,128)(2,1)}, u32[]{:S(2)}) copy-start(bf16[512,640]{1,0:T(8,128)(2,1)} %param.4) | copy-start | bytes 1966084
  2.0 7.0 %collective-permute-start.1 = (bf16[512,512]{1,0:T(8,128)(2,1)S(1)}, bf16[512,512]{1,0:T(8,128)(2,1)S(1)}, u32[]{:S(2)}, u32[]{:S(2)}) collective-permute-start(bf16[512,512]{1,0:T(8,128)(2,1)S(1)} %get-tuple-element.65), channel_id=1, source_target_pairs={{0,8},{1,9},{2,10},{3,11},{4,12},{5,13},{6,14},{7,15},{8,0},{9,1},... | collective-permute-start | bytes 1572872 | tf_op jit(solution)/shard_map/ppermute | solution.py:23
  3.6 7.4 %collective-permute-start = (bf16[256,640]{1,0:T(8,128)(2,1)S(1)}, bf16[256,640]{1,0:T(8,128)(2,1)S(1)}, u32[]{:S(2)}, u32[]{:S(2)}) collective-permute-start(bf16[256,640]{1,0:T(8,128)(2,1)S(1)} %get-tuple-element.69), channel_id=1, source_target_pairs={{0,4},{1,5},{2,6},{3,7},{4,0},{5,1},{6,2},{7,3},{8,28},{9,29},{10,... | collective-permute-start | bytes 983048 | tf_op jit(solution)/shard_map/ppermute | solution.py:23
  6.5 10.1 %collective-permute-start.5 = (bf16[256,640]{1,0:T(8,128)(2,1)S(1)}, bf16[256,640]{1,0:T(8,128)(2,1)S(1)}, u32[]{:S(2)}, u32[]{:S(2)}) collective-permute-start(bf16[256,640]{1,0:T(8,128)(2,1)S(1)} %get-tuple-element.31), channel_id=1, source_target_pairs={{0,32},{1,33},{2,34},{3,35},{4,36},{5,37},{6,38},{7,39},{8,104},{9... | collective-permute-start | bytes 983048 | tf_op jit(solution)/shard_map/ppermute | solution.py:23
  8.9 7.6 %collective-permute-start.6 = (bf16[256,640]{1,0:T(8,128)(2,1)S(1)}, bf16[256,640]{1,0:T(8,128)(2,1)S(1)}, u32[]{:S(2)}, u32[]{:S(2)}) collective-permute-start(bf16[256,640]{1,0:T(8,128)(2,1)S(1)} %get-tuple-element.31), channel_id=1, source_target_pairs={{0,96},{1,97},{2,98},{3,99},{4,100},{5,101},{6,102},{7,103},{8,40}... | collective-permute-start | bytes 983048 | tf_op jit(solution)/shard_map/ppermute | solution.py:23
  8.9 24.4 %collective-permute-start.8 = (bf16[256,640]{1,0:T(8,128)(2,1)S(1)}, bf16[256,640]{1,0:T(8,128)(2,1)S(1)}, u32[]{:S(2)}, u32[]{:S(2)}) collective-permute-start(bf16[256,640]{1,0:T(8,128)(2,1)S(1)} %get-tuple-element.69), channel_id=1, source_target_pairs={{0,20},{1,21},{2,22},{3,23},{4,16},{5,17},{6,18},{7,19},{8,12},{9,... | collective-permute-start | bytes 983048 | tf_op jit(solution)/shard_map/ppermute | solution.py:23
  10.9 22.3 %collective-permute-start.2 = (bf16[1024,256]{1,0:T(8,128)(2,1)S(1)}, bf16[1024,256]{1,0:T(8,128)(2,1)S(1)}, u32[]{:S(2)}, u32[]{:S(2)}) collective-permute-start(bf16[1024,256]{1,0:T(8,128)(2,1)S(1)} %fusion.10), channel_id=1, source_target_pairs={{0,4},{1,5},{2,6},{3,7},{4,0},{5,1},{6,2},{7,3},{8,12},{9,13},{10,... | collective-permute-start | bytes 1572872 | tf_op jit(solution)/shard_map/ppermute | solution.py:23
  16.6 16.6 %collective-permute-start.7 = (bf16[256,640]{1,0:T(8,128)(2,1)S(1)}, bf16[256,640]{1,0:T(8,128)(2,1)S(1)}, u32[]{:S(2)}, u32[]{:S(2)}) collective-permute-start(bf16[256,640]{1,0:T(8,128)(2,1)S(1)} %get-tuple-element.31), channel_id=1, source_target_pairs={{0,16},{1,17},{2,18},{3,19},{4,20},{5,21},{6,22},{7,23},{8,24},{9,... | collective-permute-start | bytes 983048 | tf_op jit(solution)/shard_map/ppermute | solution.py:23
  18.2 15.0 %copy-start.6 = (bf16[512,640]{1,0:T(8,128)(2,1)S(1)}, bf16[512,640]{1,0:T(8,128)(2,1)}, u32[]{:S(2)}) copy-start(bf16[512,640]{1,0:T(8,128)(2,1)} %param.5) | copy-start | bytes 1966084
  18.3 22.5 %collective-permute-start.10 = (bf16[1024,256]{1,0:T(8,128)(2,1)S(1)}, bf16[1024,256]{1,0:T(8,128)(2,1)S(1)}, u32[]{:S(2)}, u32[]{:S(2)}) collective-permute-start(bf16[1024,256]{1,0:T(8,128)(2,1)S(1)} %get-tuple-element.56), channel_id=1, source_target_pairs={{0,1},{1,0},{2,3},{3,2},{4,5},{5,4},{6,7},{7,6},{8,11},{9,10},{10,... | collective-permute-start | bytes 1572872 | tf_op jit(solution)/shard_map/ppermute | solution.py:23
  22.1 14.8 %collective-permute-start.11 = (bf16[1024,256]{1,0:T(8,128)(2,1)S(1)}, bf16[1024,256]{1,0:T(8,128)(2,1)S(1)}, u32[]{:S(2)}, u32[]{:S(2)}) collective-permute-start(bf16[1024,256]{1,0:T(8,128)(2,1)S(1)} %get-tuple-element.56), channel_id=1, source_target_pairs={{0,3},{1,2},{2,1},{3,0},{4,7},{5,6},{6,5},{7,4},{8,9},{9,8},{10,11... | collective-permute-start | bytes 1572872 | tf_op jit(solution)/shard_map/ppermute | solution.py:23
  33.2 15.3 %collective-permute-start.3 = (bf16[512,640]{1,0:T(8,128)(2,1)S(1)}, bf16[512,640]{1,0:T(8,128)(2,1)S(1)}, u32[]{:S(2)}, u32[]{:S(2)}) collective-permute-start(bf16[512,640]{1,0:T(8,128)(2,1)S(1)} %copy-done.6), channel_id=1, source_target_pairs={{0,4},{1,5},{2,6},{3,7},{4,0},{5,1},{6,2},{7,3},{8,12},{9,13},{10,... | collective-permute-start | bytes 1966088 | tf_op jit(solution)/shard_map/ppermute | solution.py:23
  33.4 29.0 %collective-permute-start.18 = (bf16[768,640]{1,0:T(8,128)(2,1)S(1)}, bf16[768,640]{1,0:T(8,128)(2,1)S(1)}, u32[]{:S(2)}, u32[]{:S(2)}) collective-permute-start(bf16[768,640]{1,0:T(8,128)(2,1)S(1)} %constant_dynamic-update-slice_fusion.2), channel_id=1, source_target_pairs={{0,96},{1,97},{2,98},{3,99},{4,100},{5,101},{6,102},{7,103},{8,40}... | collective-permute-start | bytes 2949128 | tf_op jit(solution)/shard_map/ppermute | solution.py:23
  34.9 28.3 %collective-permute-start.9 = (bf16[768,640]{1,0:T(8,128)(2,1)S(1)}, bf16[768,640]{1,0:T(8,128)(2,1)S(1)}, u32[]{:S(2)}, u32[]{:S(2)}) collective-permute-start(bf16[768,640]{1,0:T(8,128)(2,1)S(1)} %constant_dynamic-update-slice_fusion.2), channel_id=1, source_target_pairs={{0,32},{1,33},{2,34},{3,35},{4,36},{5,37},{6,38},{7,39},{8,104},{9... | collective-permute-start | bytes 2949128 | tf_op jit(solution)/shard_map/ppermute | solution.py:23
  36.9 7.9 %collective-permute-start.12 = (bf16[512,256]{1,0:T(8,128)(2,1)S(1)}, bf16[512,256]{1,0:T(8,128)(2,1)S(1)}, u32[]{:S(2)}, u32[]{:S(2)}) collective-permute-start(bf16[512,256]{1,0:T(8,128)(2,1)S(1)} %slice.116), channel_id=1, source_target_pairs={{0,1},{1,0},{2,3},{3,2},{4,5},{5,4},{6,7},{7,6},{8,11},{9,10},{10,... | collective-permute-start | bytes 786440 | tf_op jit(solution)/shard_map/ppermute | solution.py:23
  40.8 7.5 %collective-permute-start.13 = (bf16[512,256]{1,0:T(8,128)(2,1)S(1)}, bf16[512,256]{1,0:T(8,128)(2,1)S(1)}, u32[]{:S(2)}, u32[]{:S(2)}) collective-permute-start(bf16[512,256]{1,0:T(8,128)(2,1)S(1)} %slice.117), channel_id=1, source_target_pairs={{0,3},{1,2},{2,1},{3,0},{4,7},{5,6},{6,5},{7,4},{8,9},{9,8},{10,11... | collective-permute-start | bytes 786440 | tf_op jit(solution)/shard_map/ppermute | solution.py:23
  44.8 17.5 %collective-permute-start.14 = (bf16[1024,256]{1,0:T(8,128)(2,1)S(1)}, bf16[1024,256]{1,0:T(8,128)(2,1)S(1)}, u32[]{:S(2)}, u32[]{:S(2)}) collective-permute-start(bf16[1024,256]{1,0:T(8,128)(2,1)S(1)} %collective-permute-done.2), channel_id=1, source_target_pairs={{0,1},{1,0},{2,3},{3,2},{4,5},{5,4},{6,7},{7,6},{8,11},{9,10},{10,... | collective-permute-start | bytes 1572872 | tf_op jit(solution)/shard_map/ppermute | solution.py:23
  48.2 13.9 %collective-permute-start.15 = (bf16[1024,256]{1,0:T(8,128)(2,1)S(1)}, bf16[1024,256]{1,0:T(8,128)(2,1)S(1)}, u32[]{:S(2)}, u32[]{:S(2)}) collective-permute-start(bf16[1024,256]{1,0:T(8,128)(2,1)S(1)} %collective-permute-done.2), channel_id=1, source_target_pairs={{0,3},{1,2},{2,1},{3,0},{4,7},{5,6},{6,5},{7,4},{8,9},{9,8},{10,11... | collective-permute-start | bytes 1572872 | tf_op jit(solution)/shard_map/ppermute | solution.py:23
  48.7 22.3 %collective-permute-start.4 = (bf16[512,1280]{1,0:T(8,128)(2,1)S(1)}, bf16[512,1280]{1,0:T(8,128)(2,1)S(1)}, u32[]{:S(2)}, u32[]{:S(2)}) collective-permute-start(bf16[512,1280]{1,0:T(8,128)(2,1)S(1)} %constant_dynamic-update-slice_fusion), channel_id=1, source_target_pairs={{0,8},{1,9},{2,10},{3,11},{4,12},{5,13},{6,14},{7,15},{8,0},{9,1},... | collective-permute-start | bytes 3932168 | tf_op jit(solution)/shard_map/ppermute | solution.py:23
  62.2 8.7 %collective-permute-start.16 = (bf16[512,256]{1,0:T(8,128)(2,1)S(1)}, bf16[512,256]{1,0:T(8,128)(2,1)S(1)}, u32[]{:S(2)}, u32[]{:S(2)}) collective-permute-start(bf16[512,256]{1,0:T(8,128)(2,1)S(1)} %slice.118), channel_id=1, source_target_pairs={{0,1},{1,0},{2,3},{3,2},{4,5},{5,4},{6,7},{7,6},{8,11},{9,10},{10,... | collective-permute-start | bytes 786440 | tf_op jit(solution)/shard_map/ppermute | solution.py:23
  62.3 8.6 %collective-permute-start.17 = (bf16[512,256]{1,0:T(8,128)(2,1)S(1)}, bf16[512,256]{1,0:T(8,128)(2,1)S(1)}, u32[]{:S(2)}, u32[]{:S(2)}) collective-permute-start(bf16[512,256]{1,0:T(8,128)(2,1)S(1)} %slice.119), channel_id=1, source_target_pairs={{0,3},{1,2},{2,1},{3,0},{4,7},{5,6},{6,5},{7,4},{8,9},{9,8},{10,11... | collective-permute-start | bytes 786440 | tf_op jit(solution)/shard_map/ppermute | solution.py:23
  62.7 17.2 %collective-permute-start.19 = (bf16[512,640]{1,0:T(8,128)(2,1)S(1)}, bf16[512,640]{1,0:T(8,128)(2,1)S(1)}, u32[]{:S(2)}, u32[]{:S(2)}) collective-permute-start(bf16[512,640]{1,0:T(8,128)(2,1)S(1)} %slice.120), channel_id=1, source_target_pairs={{0,32},{1,33},{2,34},{3,35},{4,36},{5,37},{6,38},{7,39},{8,104},{9... | collective-permute-start | bytes 1966088 | tf_op jit(solution)/shard_map/ppermute | solution.py:23
  63.3 16.6 %collective-permute-start.20 = (bf16[512,640]{1,0:T(8,128)(2,1)S(1)}, bf16[512,640]{1,0:T(8,128)(2,1)S(1)}, u32[]{:S(2)}, u32[]{:S(2)}) collective-permute-start(bf16[512,640]{1,0:T(8,128)(2,1)S(1)} %slice.121), channel_id=1, source_target_pairs={{0,96},{1,97},{2,98},{3,99},{4,100},{5,101},{6,102},{7,103},{8,40}... | collective-permute-start | bytes 1966088 | tf_op jit(solution)/shard_map/ppermute | solution.py:23
  79.8 30.0 %collective-permute-start.31 = (bf16[2,2,256,640]{3,2,1,0:T(8,128)(2,1)S(1)}, bf16[2,2,256,640]{3,2,1,0:T(8,128)(2,1)}, u32[]{:S(2)}, u32[]{:S(2)}) collective-permute-start(bf16[2,2,256,640]{3,2,1,0:T(8,128)(2,1)S(1)} %get-tuple-element.53), channel_id=1, source_target_pairs={{0,96},{1,97},{2,98},{3,99},{4,100},{5,101},{6,102},{7,103},{8,40}... | collective-permute-start | bytes 3932168 | tf_op jit(solution)/shard_map/ppermute | solution.py:23
  90.5 14.9 %collective-permute-start.23 = (bf16[2,1024,256]{2,1,0:T(8,128)(2,1)S(1)}, bf16[2,1024,256]{2,1,0:T(8,128)(2,1)S(1)}, u32[]{:S(2)}, u32[]{:S(2)}) collective-permute-start(bf16[2,1024,256]{2,1,0:T(8,128)(2,1)S(1)} %get-tuple-element.44), channel_id=1, source_target_pairs={{0,3},{1,2},{2,1},{3,0},{4,7},{5,6},{6,5},{7,4},{8,9},{9,8},{10,11... | collective-permute-start | bytes 3145736 | tf_op jit(solution)/shard_map/ppermute | solution.py:23
  98.3 13.6 %collective-permute-start.21 = (bf16[512,1280]{1,0:T(8,128)(2,1)S(1)}, bf16[512,1280]{1,0:T(8,128)(2,1)S(1)}, u32[]{:S(2)}, u32[]{:S(2)}) collective-permute-start(bf16[512,1280]{1,0:T(8,128)(2,1)S(1)} %get-tuple-element.42), channel_id=1, source_target_pairs={{0,8},{1,9},{2,10},{3,11},{4,12},{5,13},{6,14},{7,15},{8,0},{9,1},... | collective-permute-start | bytes 3932168 | tf_op jit(solution)/shard_map/ppermute | solution.py:23
  102.4 17.7 %collective-permute-start.29 = (bf16[2,2,256,640]{3,2,1,0:T(8,128)(2,1)S(1)}, bf16[2,2,256,640]{3,2,1,0:T(8,128)(2,1)S(1)}, u32[]{:S(2)}, u32[]{:S(2)}) collective-permute-start(bf16[2,2,256,640]{3,2,1,0:T(8,128)(2,1)S(1)} %get-tuple-element.51), channel_id=1, source_target_pairs={{0,32},{1,33},{2,34},{3,35},{4,36},{5,37},{6,38},{7,39},{8,104},{9... | collective-permute-start | bytes 3932168 | tf_op jit(solution)/shard_map/ppermute | solution.py:23
  102.7 18.6 %collective-permute-start.25 = (bf16[2,1024,256]{2,1,0:T(8,128)(2,1)}, bf16[2,1024,256]{2,1,0:T(8,128)(2,1)}, u32[]{:S(2)}, u32[]{:S(2)}) collective-permute-start(bf16[2,1024,256]{2,1,0:T(8,128)(2,1)} %get-tuple-element.47), channel_id=1, source_target_pairs={{0,1},{1,0},{2,3},{3,2},{4,5},{5,4},{6,7},{7,6},{8,11},{9,10},{10,... | collective-permute-start | bytes 3145736 | tf_op jit(solution)/shard_map/ppermute | solution.py:23
  105.4 6.5 %copy-start.4 = (bf16[2,1024,256]{2,1,0:T(8,128)(2,1)}, bf16[2,1024,256]{2,1,0:T(8,128)(2,1)S(1)}, u32[]{:S(2)}) copy-start(bf16[2,1024,256]{2,1,0:T(8,128)(2,1)S(1)} %collective-permute-done.23) | copy-start | bytes 3145732
  106.5 17.8 %collective-permute-start.24 = (bf16[1024,256]{1,0:T(8,128)(2,1)}, bf16[1024,256]{1,0:T(8,128)(2,1)}, u32[]{:S(2)}, u32[]{:S(2)}) collective-permute-start(bf16[1024,256]{1,0:T(8,128)(2,1)} %fusion.6), channel_id=1, source_target_pairs={{0,1},{1,0},{2,3},{3,2},{4,5},{5,4},{6,7},{7,6},{8,11},{9,10},{10,... | collective-permute-start | bytes 1572872 | tf_op jit(solution)/shard_map/ppermute | solution.py:23
  111.9 16.9 %collective-permute-start.32 = (bf16[2,256,640]{2,1,0:T(8,128)(2,1)}, bf16[2,256,640]{2,1,0:T(8,128)(2,1)}, u32[]{:S(2)}, u32[]{:S(2)}) collective-permute-start(bf16[2,256,640]{2,1,0:T(8,128)(2,1)} %fusion.4), channel_id=1, source_target_pairs={{0,32},{1,33},{2,34},{3,35},{4,36},{5,37},{6,38},{7,39},{8,104},{9... | collective-permute-start | bytes 1966088 | tf_op jit(solution)/shard_map/ppermute | solution.py:23
  112.2 9.0 %copy-start = (f32[512,1280]{1,0:T(8,128)}, f32[512,1280]{1,0:T(8,128)S(1)}, u32[]{:S(2)}) copy-start(f32[512,1280]{1,0:T(8,128)S(1)} %convert_add_fusion) | copy-start | bytes 7864324
  113.2 13.8 %collective-permute-start.22 = (bf16[512,640]{1,0:T(8,128)(2,1)}, bf16[512,640]{1,0:T(8,128)(2,1)S(1)}, u32[]{:S(2)}, u32[]{:S(2)}) collective-permute-start(bf16[512,640]{1,0:T(8,128)(2,1)} %slice.191), channel_id=1, source_target_pairs={{0,4},{1,5},{2,6},{3,7},{4,0},{5,1},{6,2},{7,3},{8,12},{9,13},{10,... | collective-permute-start | bytes 1966088 | tf_op jit(solution)/shard_map/ppermute | solution.py:23
  120.0 1.3 copy-start.2
  121.3 12.5 %collective-permute-start.30 = (bf16[2,256,640]{2,1,0:T(8,128)(2,1)}, bf16[2,256,640]{2,1,0:T(8,128)(2,1)}, u32[]{:S(2)}, u32[]{:S(2)}) collective-permute-start(bf16[2,256,640]{2,1,0:T(8,128)(2,1)} %fusion.3), channel_id=1, source_target_pairs={{0,96},{1,97},{2,98},{3,99},{4,100},{5,101},{6,102},{7,103},{8,40}... | collective-permute-start | bytes 1966088 | tf_op jit(solution)/shard_map/ppermute | solution.py:23
  121.3 3.0 %copy-start.5 = (bf16[2,1024,256]{2,1,0:T(8,128)(2,1)S(1)}, bf16[2,1024,256]{2,1,0:T(8,128)(2,1)}, u32[]{:S(2)}) copy-start(bf16[2,1024,256]{2,1,0:T(8,128)(2,1)} %copy-done.4) | copy-start | bytes 3145732
  122.6 11.2 %copy-start.3 = (bf16[2,2,256,640]{3,2,1,0:T(8,128)(2,1)S(1)}, bf16[2,2,256,640]{3,2,1,0:T(8,128)(2,1)}, u32[]{:S(2)}) copy-start(bf16[2,2,256,640]{3,2,1,0:T(8,128)(2,1)} %copy-done.2) | copy-start | bytes 3932164
  122.6 18.4 %collective-permute-start.26 = (bf16[1024,256]{1,0:T(8,128)(2,1)S(1)}, bf16[1024,256]{1,0:T(8,128)(2,1)S(1)}, u32[]{:S(2)}, u32[]{:S(2)}) collective-permute-start(bf16[1024,256]{1,0:T(8,128)(2,1)S(1)} %fusion.7), channel_id=1, source_target_pairs={{0,3},{1,2},{2,1},{3,0},{4,7},{5,6},{6,5},{7,4},{8,9},{9,8},{10,11... | collective-permute-start | bytes 1572872 | tf_op jit(solution)/shard_map/ppermute | solution.py:23
  127.0 14.0 %collective-permute-start.27 = (bf16[1024,256]{1,0:T(8,128)(2,1)S(1)}, bf16[1024,256]{1,0:T(8,128)(2,1)S(1)}, u32[]{:S(2)}, u32[]{:S(2)}) collective-permute-start(bf16[1024,256]{1,0:T(8,128)(2,1)S(1)} %bitcast_add_fusion.3), channel_id=1, source_target_pairs={{0,4},{1,5},{2,6},{3,7},{4,0},{5,1},{6,2},{7,3},{8,12},{9,13},{10,... | collective-permute-start | bytes 1572872 | tf_op jit(solution)/shard_map/ppermute | solution.py:23
  133.8 6.2 %copy-start.1 = (f32[512,1280]{1,0:T(8,128)S(1)}, f32[512,1280]{1,0:T(8,128)}, u32[]{:S(2)}) copy-start(f32[512,1280]{1,0:T(8,128)} %copy-done) | copy-start | bytes 7864324
  136.0 19.5 %collective-permute-start.33 = (bf16[256,640]{1,0:T(8,128)(2,1)S(1)}, bf16[256,640]{1,0:T(8,128)(2,1)S(1)}, u32[]{:S(2)}, u32[]{:S(2)}) collective-permute-start(bf16[256,640]{1,0:T(8,128)(2,1)S(1)} %get-tuple-element.67), channel_id=1, source_target_pairs={{0,16},{1,17},{2,18},{3,19},{4,20},{5,21},{6,22},{7,23},{8,24},{9,... | collective-permute-start | bytes 983048 | tf_op jit(solution)/shard_map/ppermute | solution.py:23
  139.7 15.8 %collective-permute-start.34 = (bf16[256,640]{1,0:T(8,128)(2,1)S(1)}, bf16[256,640]{1,0:T(8,128)(2,1)S(1)}, u32[]{:S(2)}, u32[]{:S(2)}) collective-permute-start(bf16[256,640]{1,0:T(8,128)(2,1)S(1)} %get-tuple-element.59), channel_id=1, source_target_pairs={{0,4},{1,5},{2,6},{3,7},{4,0},{5,1},{6,2},{7,3},{8,28},{9,29},{10,... | collective-permute-start | bytes 983048 | tf_op jit(solution)/shard_map/ppermute | solution.py:23
  140.0 15.5 %collective-permute-start.35 = (bf16[256,640]{1,0:T(8,128)(2,1)S(1)}, bf16[256,640]{1,0:T(8,128)(2,1)S(1)}, u32[]{:S(2)}, u32[]{:S(2)}) collective-permute-start(bf16[256,640]{1,0:T(8,128)(2,1)S(1)} %get-tuple-element.60), channel_id=1, source_target_pairs={{0,20},{1,21},{2,22},{3,23},{4,16},{5,17},{6,18},{7,19},{8,12},{9,... | collective-permute-start | bytes 983048 | tf_op jit(solution)/shard_map/ppermute | solution.py:23
  142.4 14.3 %collective-permute-start.28 = (bf16[512,512]{1,0:T(8,128)(2,1)S(1)}, bf16[512,512]{1,0:T(8,128)(2,1)S(1)}, u32[]{:S(2)}, u32[]{:S(2)}) collective-permute-start(bf16[512,512]{1,0:T(8,128)(2,1)S(1)} %pad_maximum_fusion.6), channel_id=1, source_target_pairs={{0,8},{1,9},{2,10},{3,11},{4,12},{5,13},{6,14},{7,15},{8,0},{9,1},... | collective-permute-start | bytes 1572872 | tf_op jit(solution)/shard_map/ppermute | solution.py:23

commit v4 on v3

--- a/solution.py
+++ b/solution.py
@@ -44,10 +44,16 @@
     return [value, one, jnp.concatenate(far, 0), two]
 
 
-def scatter4(far_one, far_two, one, two, own, axis):
-    got_one, got_two = flip(far_one, **{axis: ONE}), flip(far_two, **{axis: TWO})
-    got_bottom1 = flip(add(one[0], got_two[0]).astype(BF16), **{axis: ONE})
-    got_top2 = flip(add(two[0], got_one[0]).astype(BF16), **{axis: TWO})
+def scatter_start(far_one, far_two, axis):
+    return flip(far_one, **{axis: ONE}), flip(far_two, **{axis: TWO})
+
+
+def scatter_add(got_one, got_two, one, two):
+    return add(one[0], got_two[0]).astype(BF16), add(two[0], got_one[0]).astype(BF16)
+
+
+def scatter_end(got_one, got_two, send_one, send_two, own, axis):
+    got_bottom1, got_top2 = flip(send_one, **{axis: ONE}), flip(send_two, **{axis: TWO})
     return add(own[0], got_one[1], got_top2), add(own[1], got_two[1], got_bottom1)
 
 
@@ -62,8 +68,8 @@
     return chosen
 
 
-def cost(products):
-    return pl.CostEstimate(flops=4 * products, bytes_accessed=products // 512, transcendentals=0)
+def cost(products, factor):
+    return pl.CostEstimate(flops=int(factor * products), bytes_accessed=int(factor * products) // 2048, transcendentals=0)
 
 
 def turned(slot, m):
@@ -126,7 +132,7 @@
         ),
         out_shape=[jax.ShapeDtypeStruct((len(group), 2, d, cols), BF16) for group in groups],
         compiler_params=pltpu.CompilerParams(vmem_limit_bytes=32 << 20),
-        cost_estimate=cost(8 * t * d * 2 * cols),
+        cost_estimate=cost(8 * t * d * 2 * cols, 2),
         name="weight_terms",
     )(scalars, a, g)
 
@@ -164,7 +170,7 @@
         ),
         out_shape=[jax.ShapeDtypeStruct((len(group), t, d), BF16) for group in groups],
         compiler_params=pltpu.CompilerParams(vmem_limit_bytes=32 << 20),
-        cost_estimate=cost(8 * t * d * 2 * cols),
+        cost_estimate=cost(8 * t * d * 2 * cols, 8),
         name="input_terms",
     )(scalars, g, w, w)
 
@@ -211,7 +217,7 @@
         ),
         out_shape=[jax.ShapeDtypeStruct((t // 2, 2 * cols), BF16)] * 2,
         compiler_params=pltpu.CompilerParams(vmem_limit_bytes=40 << 20),
-        cost_estimate=cost(8 * t * d * 2 * cols),
+        cost_estimate=cost(8 * t * d * 2 * cols, 2),
         name="forward_terms",
     )(scalars, a, w)
 
@@ -229,7 +235,6 @@
     w_diff = lax.dynamic_slice_in_dim(qkv_weight, (1 - y_lo) * sub, sub, 0)
     ws_one, ws_two = flip(w_same, x=ONE), flip(w_same, x=TWO)
     w_one, w_two = flip(w_diff, y=ONE), flip(w_diff, y=TWO)
-    ws_one, ws_two, w_same = tie(ws_one, ws_two, w_same)
     w_far = flip(w_same, y=2)
 
     halves = [activations[:, : 2 * sub], activations[:, 2 * sub :]]
@@ -237,12 +242,14 @@
     a_rows = jnp.concatenate([a_mine, flip(a_theirs, c=1)], 0)
     a_keep = lax.dynamic_slice_in_dim(a_rows, y_lo * sub, sub, 1)
     a_send = lax.dynamic_slice_in_dim(a_rows, (1 - y_lo) * sub, sub, 1)
-    w_one, a_send = tie(w_one, a_send)
+    ws_one, ws_two, a_keep = tie(ws_one, ws_two, a_keep)
+    w_far, a_send = tie(w_far, a_send)
     a_y = flip(a_send, y=1)
     w_near = jnp.concatenate([w_one, w_far, w_two], 0)
     wn_one, wn_two = flip(w_near, x=ONE), flip(w_near, x=TWO)
     ka_one, ka_two = flip(a_keep, z=ONE), flip(a_keep, z=TWO)
-    a_y, grad = tie(a_y, qkv_grad)
+    grad = qkv_grad
+    a_y, grad = tie(a_y, grad)
     g_y = flip(grad, y=1)
     ya_one, ya_two = flip(a_y, z=ONE), flip(a_y, z=TWO)
     far_one, far_two = flip(ka_two[:tok], z=ONE), flip(ka_one[tok:], z=TWO)
@@ -261,29 +268,36 @@
     w = jnp.stack([w_own, w_1, jnp.concatenate([far_one, far_two], 0), w_2]).reshape(4, 4, sub, cols)
     da_first, *da = input_terms(scalars, g, w)
     da_first, scalars = tie(da_first, scalars)
-    da_keep, da_send = scatter4(da_first, *da, "z")
-    dw_0, dw_1 = scatter4(dw_first, *dw, "x")
+    dw_got = scatter_start(dw_first, dw[0], "x")
+    da_got = scatter_start(da_first, da[0], "z")
+    dw_sum = scatter_add(*dw_got, dw[1], dw[2])
+    da_sum = scatter_add(*da_got, da[1], da[2])
+    dw_0, dw_1 = scatter_end(*dw_got, *dw_sum, dw[3], "x")
+    da_keep, da_send = scatter_end(*da_got, *da_sum, da[3], "z")
+    da_keep, da_send = da_keep.astype(BF16), da_send.astype(BF16)
+    dw_send = [dw_0[1].astype(BF16), dw_1[1].astype(BF16), dw_1[0].astype(BF16)]
 
     mine, theirs = forward_terms(scalars, a, w)
-    fwd = add(mine, flip(theirs, c=1))
+    got = flip(theirs, c=1)
+    fwd = add(mine, got)
     fwd_y = flip(fwd[:, cols:].astype(BF16), y=1)
     fwd_y, da_send = tie(fwd_y, da_send)
     projected = add(fwd[:, :cols], fwd_y).astype(BF16)
 
-    da_y = flip(da_send.astype(BF16), y=1)
-    da_keep = da_keep.astype(BF16)
-    r0, r1 = jnp.where(y_lo == 0, da_keep, da_y), jnp.where(y_lo == 0, da_y, da_keep)
-    both = jnp.concatenate([r0, r1], 1)
+    def by_r(keep, other):
+        return jnp.concatenate([jnp.where(y_lo == 0, keep, other), jnp.where(y_lo == 0, other, keep)], 1)
+
+    da_y = flip(da_send, y=1)
+    both = by_r(da_keep, da_y)
     mine, theirs = both[:tok], flip(both[tok:], c=1)
     input_grad = jnp.concatenate([jnp.where(c == 0, mine, theirs), jnp.where(c == 0, theirs, mine)], 1)
 
-    send1, send3 = dw_0[1].astype(BF16), dw_1[1].astype(BF16)
+    send1, send3, send2 = dw_send
     got_one = flip(jnp.where(c == 0, send1, send3), y=ONE)
     got_two = flip(jnp.where(c == 0, send3, send1), y=TWO)
-    got_far = flip(dw_1[0].astype(BF16), y=2)
+    got_far = flip(send2, y=2)
     same, diff = add(dw_0[0], got_far), add(got_one, got_two)
     weight_grad = jnp.where(y_lo == 0, jnp.concatenate([same, diff], 0), jnp.concatenate([diff, same], 0))
-
     return projected, input_grad, weight_grad
 
 

time: 159 us -> 156 us (0.981)
  starting transfers between devices: 48 us -> 43.5 us
  waiting for transfers between devices: 63.8 us -> 65.7 us
    ppermute x36, starting transfers between devices: 48 us -> 43.5 us  [flip(): return lax.ppermute(value, AXES, pairs)]
    ppermute x36, waiting for transfers between devices: 63.8 us -> 65.7 us  [flip(): return lax.ppermute(value, AXES, pairs)]
    add x5 -> x4, other arithmetic: 3.71 us -> 2.48 us  [add(): total = total + term.astype(F32)]
    convert_element_type x4 -> x5, other arithmetic: 5.75 us -> 6.98 us  [the longest x2 3.27 us: scatter_add(): add(one[0], got_two[0]).astype(BF16)]
  transfers between devices with their start and end apart: 36 -> 36, of which waited for: 13 -> 14; matrix products, arithmetic and copies ran while one was open for 11% -> 11% of each run, Pallas kernels for 16% -> 17%
where the time goes in v4:
time: 156 us; the launch traced here: 155 us
  waiting for transfers between devices  65.7 us (42%)
  starting transfers between devices  43.5 us (28%)
  Pallas kernels  25.7 us (16%)
  other arithmetic  17.5 us (11%)
  local copies, waits for them, and re-layouts  1.96 us (1%)
    ppermute x36, waiting for transfers between devices, flip(): return lax.ppermute(value, AXES, pairs)  65.7 us
    ppermute x36, starting transfers between devices, flip(): return lax.ppermute(value, AXES, pairs)  43.5 us
    pallas_call x1, Pallas kernels, input_terms(): pl.pallas_call(functools.partial(da_kernel, groups), grid_spec=pltpu.Pref...  9.4 us
    pallas_call x1, Pallas kernels, weight_terms(): pl.pallas_call(functools.partial(dw_kernel, groups), grid_spec=pltpu.Pref...  8.63 us
    pallas_call x1, Pallas kernels, forward_terms(): pl.pallas_call(fwd_kernel, grid_spec=pltpu.PrefetchScalarGridSpec(num_sca...  7.66 us
    convert_element_type x2, other arithmetic, scatter_add(): add(one[0], got_two[0]).astype(BF16)  3.27 us
  transfers between devices with their start and end apart: 36, of which 14 were waited for; matrix products, arithmetic and copies ran while one was open for 11% of the time, Pallas kernels for 17%

profile of v4, /device:TPU:1, one launch (start us, length us, event | category | flops | bytes accessed | tf_op | source)
XLA Modules:
  0.0 155.5 jit_solution(4199295394878089791)
XLA Ops:
  0.7 1.3 broadcast_select_fusion.4
  2.0 1.5 collective-permute-start.1
  3.6 3.1 %collective-permute-start = (bf16[256,640]{1,0:T(8,128)(2,1)S(1)}, bf16[256,640]{1,0:T(8,128)(2,1)S(1)}, u32[]{:S(2)}, u32[]{:S(2)}) collective-permute-start(bf16[256,640]{1,0:T(8,128)(2,1)S(1)} %get-tuple-element.69), channel_id=1, source_target_pairs={{0,16},{1,17},{2,18},{3,19},{4,20},{5,21},{6,22},{7,23},{8,24},{9,... | collective-permute-start | bytes 983048 | tf_op jit(solution)/shard_map/ppermute | solution.py:23
  6.6 0.8 collective-permute-start.5
  7.4 2.5 %collective-permute-start.7 = (bf16[256,640]{1,0:T(8,128)(2,1)S(1)}, bf16[256,640]{1,0:T(8,128)(2,1)S(1)}, u32[]{:S(2)}, u32[]{:S(2)}) collective-permute-start(bf16[256,640]{1,0:T(8,128)(2,1)S(1)} %get-tuple-element.69), channel_id=1, source_target_pairs={{0,32},{1,33},{2,34},{3,35},{4,36},{5,37},{6,38},{7,39},{8,104},{9... | collective-permute-start | bytes 983048 | tf_op jit(solution)/shard_map/ppermute | solution.py:23
  10.1 4.4 %collective-permute-done = bf16[256,640]{1,0:T(8,128)(2,1)S(1)} collective-permute-done((bf16[256,640]{1,0:T(8,128)(2,1)S(1)}, bf16[256,640]{1,0:T(8,128)(2,1)S(1)}, u32[]{:S(2)}, u32[]{:S(2)}) %collective-permute-start) | collective-permute-done | bytes 327712 | tf_op jit(solution)/shard_map/ppermute | solution.py:23
  14.5 1.3 collective-permute-start.2
  15.8 5.4 %collective-permute-done.5 = bf16[256,640]{1,0:T(8,128)(2,1)S(1)} collective-permute-done((bf16[256,640]{1,0:T(8,128)(2,1)S(1)}, bf16[256,640]{1,0:T(8,128)(2,1)S(1)}, u32[]{:S(2)}, u32[]{:S(2)}) %collective-permute-start.5) | collective-permute-done | bytes 327712 | tf_op jit(solution)/shard_map/ppermute | solution.py:23
  21.3 3.8 %collective-permute-start.10 = (bf16[1024,256]{1,0:T(8,128)(2,1)S(1)}, bf16[1024,256]{1,0:T(8,128)(2,1)S(1)}, u32[]{:S(2)}, u32[]{:S(2)}) collective-permute-start(bf16[1024,256]{1,0:T(8,128)(2,1)S(1)} %get-tuple-element.33), channel_id=1, source_target_pairs={{0,1},{1,0},{2,3},{3,2},{4,5},{5,4},{6,7},{7,6},{8,11},{9,10},{10,... | collective-permute-start | bytes 1572872 | tf_op jit(solution)/shard_map/ppermute | solution.py:23
  25.2 1.9 %collective-permute-start.18 = (bf16[768,640]{1,0:T(8,128)(2,1)S(1)}, bf16[768,640]{1,0:T(8,128)(2,1)S(1)}, u32[]{:S(2)}, u32[]{:S(2)}) collective-permute-start(bf16[768,640]{1,0:T(8,128)(2,1)S(1)} %constant_dynamic-update-slice_fusion.2), channel_id=1, source_target_pairs={{0,96},{1,97},{2,98},{3,99},{4,100},{5,101},{6,102},{7,103},{8,40}... | collective-permute-start | bytes 2949128 | tf_op jit(solution)/shard_map/ppermute | solution.py:23
  27.1 1.9 %collective-permute-start.9 = (bf16[768,640]{1,0:T(8,128)(2,1)S(1)}, bf16[768,640]{1,0:T(8,128)(2,1)S(1)}, u32[]{:S(2)}, u32[]{:S(2)}) collective-permute-start(bf16[768,640]{1,0:T(8,128)(2,1)S(1)} %constant_dynamic-update-slice_fusion.2), channel_id=1, source_target_pairs={{0,32},{1,33},{2,34},{3,35},{4,36},{5,37},{6,38},{7,39},{8,104},{9... | collective-permute-start | bytes 2949128 | tf_op jit(solution)/shard_map/ppermute | solution.py:23
  29.0 4.1 %collective-permute-done.2 = bf16[1024,256]{1,0:T(8,128)(2,1)S(1)} collective-permute-done((bf16[1024,256]{1,0:T(8,128)(2,1)S(1)}, bf16[1024,256]{1,0:T(8,128)(2,1)S(1)}, u32[]{:S(2)}, u32[]{:S(2)}) %collective-permute-start.2) | collective-permute-done | bytes 524320 | tf_op jit(solution)/shard_map/ppermute | solution.py:23
  33.2 1.1 collective-permute-start.3
  34.3 0.1 pad_maximum_fusion.2
  34.4 3.4 %collective-permute-done.11 = bf16[1024,256]{1,0:T(8,128)(2,1)S(1)} collective-permute-done((bf16[1024,256]{1,0:T(8,128)(2,1)S(1)}, bf16[1024,256]{1,0:T(8,128)(2,1)S(1)}, u32[]{:S(2)}, u32[]{:S(2)}) %collective-permute-start.11) | collective-permute-done | bytes 524320 | tf_op jit(solution)/shard_map/ppermute | solution.py:23
  37.8 0.5 collective-permute-start.12
  38.3 0.7 collective-permute-start.13
  39.0 7.5 %collective-permute-done.12 = bf16[512,256]{1,0:T(8,128)(2,1)S(1)} collective-permute-done((bf16[512,256]{1,0:T(8,128)(2,1)S(1)}, bf16[512,256]{1,0:T(8,128)(2,1)S(1)}, u32[]{:S(2)}, u32[]{:S(2)}) %collective-permute-start.12) | collective-permute-done | bytes 262176 | tf_op jit(solution)/shard_map/ppermute | solution.py:23
  46.7 1.9 %collective-permute-done.3 = bf16[512,640]{1,0:T(8,128)(2,1)S(1)} collective-permute-done((bf16[512,640]{1,0:T(8,128)(2,1)S(1)}, bf16[512,640]{1,0:T(8,128)(2,1)S(1)}, u32[]{:S(2)}, u32[]{:S(2)}) %collective-permute-start.3) | collective-permute-done | bytes 655392 | tf_op jit(solution)/shard_map/ppermute | solution.py:23
  48.7 1.8 %collective-permute-start.4 = (bf16[512,1280]{1,0:T(8,128)(2,1)S(1)}, bf16[512,1280]{1,0:T(8,128)(2,1)S(1)}, u32[]{:S(2)}, u32[]{:S(2)}) collective-permute-start(bf16[512,1280]{1,0:T(8,128)(2,1)S(1)} %constant_dynamic-update-slice_fusion), channel_id=1, source_target_pairs={{0,8},{1,9},{2,10},{3,11},{4,12},{5,13},{6,14},{7,15},{8,0},{9,1},... | collective-permute-start | bytes 3932168 | tf_op jit(solution)/shard_map/ppermute | solution.py:23
  50.6 0.2 constant_dynamic-update-slice_fusion.5
  50.8 3.2 %collective-permute-start.19 = (bf16[512,640]{1,0:T(8,128)(2,1)S(1)}, bf16[512,640]{1,0:T(8,128)(2,1)S(1)}, u32[]{:S(2)}, u32[]{:S(2)}) collective-permute-start(bf16[512,640]{1,0:T(8,128)(2,1)S(1)} %slice.120), channel_id=1, source_target_pairs={{0,32},{1,33},{2,34},{3,35},{4,36},{5,37},{6,38},{7,39},{8,104},{9... | collective-permute-start | bytes 1966088 | tf_op jit(solution)/shard_map/ppermute | solution.py:23
  54.1 5.5 %collective-permute-done.15 = bf16[1024,256]{1,0:T(8,128)(2,1)S(1)} collective-permute-done((bf16[1024,256]{1,0:T(8,128)(2,1)S(1)}, bf16[1024,256]{1,0:T(8,128)(2,1)S(1)}, u32[]{:S(2)}, u32[]{:S(2)}) %collective-permute-start.15) | collective-permute-done | bytes 524320 | tf_op jit(solution)/shard_map/ppermute | solution.py:23
  59.6 3.2 %collective-permute-start.16 = (bf16[512,256]{1,0:T(8,128)(2,1)S(1)}, bf16[512,256]{1,0:T(8,128)(2,1)S(1)}, u32[]{:S(2)}, u32[]{:S(2)}) collective-permute-start(bf16[512,256]{1,0:T(8,128)(2,1)S(1)} %slice.118), channel_id=1, source_target_pairs={{0,1},{1,0},{2,3},{3,2},{4,5},{5,4},{6,7},{7,6},{8,11},{9,10},{10,... | collective-permute-start | bytes 786440 | tf_op jit(solution)/shard_map/ppermute | solution.py:23
  63.0 0.1 pad_maximum_fusion.3
  63.2 4.5 %collective-permute-done.16 = bf16[512,256]{1,0:T(8,128)(2,1)S(1)} collective-permute-done((bf16[512,256]{1,0:T(8,128)(2,1)S(1)}, bf16[512,256]{1,0:T(8,128)(2,1)S(1)}, u32[]{:S(2)}, u32[]{:S(2)}) %collective-permute-start.16) | collective-permute-done | bytes 262176 | tf_op jit(solution)/shard_map/ppermute | solution.py:23
  67.6 3.1 %collective-permute-done.17 = bf16[512,256]{1,0:T(8,128)(2,1)S(1)} collective-permute-done((bf16[512,256]{1,0:T(8,128)(2,1)S(1)}, bf16[512,256]{1,0:T(8,128)(2,1)S(1)}, u32[]{:S(2)}, u32[]{:S(2)}) %collective-permute-start.17) | collective-permute-done | bytes 262176 | tf_op jit(solution)/shard_map/ppermute | solution.py:23
  70.9 0.2 pad_maximum_fusion.1.g
  71.0 8.6 %weight_terms.1 = (bf16[2,2,256,640]{3,2,1,0:T(8,128)(2,1)S(1)}, bf16[2,2,256,640]{3,2,1,0:T(8,128)(2,1)S(1)}, bf16[1,2,256,640]{3,2,1,0:T(8,128)(2,1)S(1)}, bf1...) custom-call(s32[2]{0:T(128)S(1)} %pad_add_fusion.m, ...), custom_call_target="tpu_custom_call" | custom-call | flops 5368709120 | bytes 2621440 | tf_op jit(solution)/shard_map/weight_terms/pallas_call | solution.py:125
  79.8 0.1 pad_maximum_fusion.4
  79.9 1.0 pad_maximum_fusion.w0.w1.w
  80.9 9.4 %input_terms.1 = (bf16[2,1024,256]{2,1,0:T(8,128)(2,1)}, bf16[2,1024,256]{2,1,0:T(8,128)(2,1)S(1)}, bf16[1,1024,256]{2,1,0:T(8,128)(2,1)S(1)}, bf16[1,1024,256]{...) custom-call(s32[2]{0:T(128)S(1)} %pad_add_fusion.m, bf16[1024,1280]{1,0:T(8,128)(2,1)S(1)} %pad_maximum_fusion.1.g, ...), custom_call_target="tpu_custom_call" | custom-call | flops 21474836480 | bytes 10485760 | tf_op jit(solution)/shard_map/input_terms/pallas_call | solution.py:159
  90.4 0.2 collective-permute-start.23
  90.5 7.7 %forward_terms.1 = (bf16[512,1280]{1,0:T(8,128)(2,1)S(1)}, bf16[512,1280]{1,0:T(8,128)(2,1)S(1)}) custom-call(s32[2]{0:T(128)S(1)} %pad_add_fusion.m, bf16[8,1024,256]{2,1,0:T(8,128)(2,1)S(1)} %bitcast_dynamic-update-slice_fusion.a, bf16[4,4,256,640]{3,2,1,0:T(8,128)(2,1)S(1)} %pad_maximum_fusion.w0.w1.w), custom_call_target="tpu_custom_call" | custom-call | flops 5368709120 | bytes 2621440 | tf_op jit(solution)/shard_map/forward_terms/pallas_call | solution.py:203
  98.2 3.3 %collective-permute-start.21 = (bf16[512,1280]{1,0:T(8,128)(2,1)S(1)}, bf16[512,1280]{1,0:T(8,128)(2,1)S(1)}, u32[]{:S(2)}, u32[]{:S(2)}) collective-permute-start(bf16[512,1280]{1,0:T(8,128)(2,1)S(1)} %get-tuple-element.42), channel_id=1, source_target_pairs={{0,8},{1,9},{2,10},{3,11},{4,12},{5,13},{6,14},{7,15},{8,0},{9,1},... | collective-permute-start | bytes 3932168 | tf_op jit(solution)/shard_map/ppermute | solution.py:23
  101.5 1.9 %collective-permute-start.29 = (bf16[2,2,256,640]{3,2,1,0:T(8,128)(2,1)S(1)}, bf16[2,2,256,640]{3,2,1,0:T(8,128)(2,1)S(1)}, u32[]{:S(2)}, u32[]{:S(2)}) collective-permute-start(bf16[2,2,256,640]{3,2,1,0:T(8,128)(2,1)S(1)} %get-tuple-element.51), channel_id=1, source_target_pairs={{0,32},{1,33},{2,34},{3,35},{4,36},{5,37},{6,38},{7,39},{8,104},{9... | collective-permute-start | bytes 3932168 | tf_op jit(solution)/shard_map/ppermute | solution.py:23
  103.3 1.0 collective-permute-start.25
  104.4 1.1 fusion.7
  105.5 1.6 %collective-permute-start.24 = (bf16[1024,256]{1,0:T(8,128)(2,1)}, bf16[1024,256]{1,0:T(8,128)(2,1)}, u32[]{:S(2)}, u32[]{:S(2)}) collective-permute-start(bf16[1024,256]{1,0:T(8,128)(2,1)} %fusion.7), channel_id=1, source_target_pairs={{0,1},{1,0},{2,3},{3,2},{4,5},{5,4},{6,7},{7,6},{8,11},{9,10},{10,... | collective-permute-start | bytes 1572872 | tf_op jit(solution)/shard_map/ppermute | solution.py:23
  107.1 2.2 %fusion.5 = bf16[2,256,640]{2,1,0:T(8,128)(2,1)} fusion(bf16[1,2,256,640]{3,2,1,0:T(8,128)(2,1)S(1)} %get-tuple-element.54, bf16[2,2,256,640]{3,2,1,0:T(8,128)(2,1)} %collective-permute-done.31), kind=kLoop, calls=%fused_computation.29 | loop fusion | flops 1310720 | bytes 1966080 | tf_op jit(solution)/shard_map/convert_element_type | solution.py:52
  109.3 0.8 collective-permute-start.32
  110.1 0.3 convert_add_fusion
  110.4 1.0 slice.191
  111.4 0.8 collective-permute-start.22
  112.2 7.0 %collective-permute-done.29 = bf16[2,2,256,640]{3,2,1,0:T(8,128)(2,1)S(1)} collective-permute-done((bf16[2,2,256,640]{3,2,1,0:T(8,128)(2,1)S(1)}, bf16[2,2,256,640]{3,2,1,0:T(8,128)(2,1)S(1)}, u32[]{:S(2)}, u32[]{:S(2)}) %collective-permute-start.29) | collective-permute-done | bytes 1310752 | tf_op jit(solution)/shard_map/ppermute | solution.py:23
  119.1 1.2 fusion.4
  120.4 1.3 fusion.8
  121.7 0.3 collective-permute-start.26
  122.0 2.6 %collective-permute-done.24 = bf16[1024,256]{1,0:T(8,128)(2,1)} collective-permute-done((bf16[1024,256]{1,0:T(8,128)(2,1)}, bf16[1024,256]{1,0:T(8,128)(2,1)}, u32[]{:S(2)}, u32[]{:S(2)}) %collective-permute-start.24) | collective-permute-done | bytes 524320 | tf_op jit(solution)/shard_map/ppermute | solution.py:23
  124.6 1.2 fusion.3
  125.9 0.8 collective-permute-start.27
  126.7 1.2 collective-permute-done.32
  127.9 5.0 %collective-permute-done.30 = bf16[2,256,640]{2,1,0:T(8,128)(2,1)} collective-permute-done((bf16[2,256,640]{2,1,0:T(8,128)(2,1)}, bf16[2,256,640]{2,1,0:T(8,128)(2,1)}, u32[]{:S(2)}, u32[]{:S(2)}) %collective-permute-start.30) | collective-permute-done | bytes 655392 | tf_op jit(solution)/shard_map/ppermute | solution.py:23
  132.9 2.1 %bitcast_add_fusion.1 = (f32[2,256,640]{2,1,0:T(8,128)S(1)}, bf16[2,256,640]{2,1,0:T(8,128)(2,1)S(1)}) fusion(bf16[2,256,640]{2,1,0:T(8,128)(2,1)} %collective-permute-done.30, bf16[2,2,256,640]{3,2,1,0:T(8,128)(2,1)S(1)} %copy-done.3, bf16[2,2,256,640]{3,2,1,0:T(8,128)(2,1)S(1)} %get-tuple-element.50, bf16[2,256,640]{2,1,0:T(8,128)(2,1)} %collective-permute-done.32, ...), kind=kLoop, calls=%fused_computation.12 | loop fusion | flops 3604480 | bytes 5898240 | tf_op jit(solution)/shard_map/add | solution.py:36
  135.1 2.3 %collective-permute-start.33 = (bf16[256,640]{1,0:T(8,128)(2,1)S(1)}, bf16[256,640]{1,0:T(8,128)(2,1)S(1)}, u32[]{:S(2)}, u32[]{:S(2)}) collective-permute-start(bf16[256,640]{1,0:T(8,128)(2,1)S(1)} %get-tuple-element.67), channel_id=1, source_target_pairs={{0,16},{1,17},{2,18},{3,19},{4,20},{5,21},{6,22},{7,23},{8,24},{9,... | collective-permute-start | bytes 983048 | tf_op jit(solution)/shard_map/ppermute | solution.py:23
  137.4 0.9 collective-permute-start.34
  138.3 0.3 collective-permute-start.35
  138.7 1.0 fusion
  139.7 1.4 broadcast_select_fusion.1
  141.1 1.8 %collective-permute-start.28 = (bf16[512,512]{1,0:T(8,128)(2,1)S(1)}, bf16[512,512]{1,0:T(8,128)(2,1)S(1)}, u32[]{:S(2)}, u32[]{:S(2)}) collective-permute-start(bf16[512,512]{1,0:T(8,128)(2,1)S(1)} %pad_maximum_fusion.6), channel_id=1, source_target_pairs={{0,8},{1,9},{2,10},{3,11},{4,12},{5,13},{6,14},{7,15},{8,0},{9,1},... | collective-permute-start | bytes 1572872 | tf_op jit(solution)/shard_map/ppermute | solution.py:23
  142.9 10.0 %collective-permute-done.34 = bf16[256,640]{1,0:T(8,128)(2,1)S(1)} collective-permute-done((bf16[256,640]{1,0:T(8,128)(2,1)S(1)}, bf16[256,640]{1,0:T(8,128)(2,1)S(1)}, u32[]{:S(2)}, u32[]{:S(2)}) %collective-permute-start.34) | collective-permute-done | bytes 327712 | tf_op jit(solution)/shard_map/ppermute | solution.py:23
  153.0 1.1 maximum_select_fusion
  154.2 0.2 broadcast_select_fusion.3
  154.4 1.1 pad_maximum_fusion.5
  (74 shorter events, 1.7 us)
Async XLA Ops:
  0.6 2.9 %copy-start.7 = (bf16[512,640]{1,0:T(8,128)(2,1)S(1)}, bf16[512,640]{1,0:T(8,128)(2,1)}, u32[]{:S(2)}) copy-start(bf16[512,640]{1,0:T(8,128)(2,1)} %param.4) | copy-start | bytes 1966084
  2.0 8.0 %collective-permute-start.1 = (bf16[512,512]{1,0:T(8,128)(2,1)S(1)}, bf16[512,512]{1,0:T(8,128)(2,1)S(1)}, u32[]{:S(2)}, u32[]{:S(2)}) collective-permute-start(bf16[512,512]{1,0:T(8,128)(2,1)S(1)} %get-tuple-element.65), channel_id=1, source_target_pairs={{0,8},{1,9},{2,10},{3,11},{4,12},{5,13},{6,14},{7,15},{8,0},{9,1},... | collective-permute-start | bytes 1572872 | tf_op jit(solution)/shard_map/ppermute | solution.py:23
  3.6 11.0 %collective-permute-start = (bf16[256,640]{1,0:T(8,128)(2,1)S(1)}, bf16[256,640]{1,0:T(8,128)(2,1)S(1)}, u32[]{:S(2)}, u32[]{:S(2)}) collective-permute-start(bf16[256,640]{1,0:T(8,128)(2,1)S(1)} %get-tuple-element.69), channel_id=1, source_target_pairs={{0,16},{1,17},{2,18},{3,19},{4,20},{5,21},{6,22},{7,23},{8,24},{9,... | collective-permute-start | bytes 983048 | tf_op jit(solution)/shard_map/ppermute | solution.py:23
  6.6 14.6 %collective-permute-start.5 = (bf16[256,640]{1,0:T(8,128)(2,1)S(1)}, bf16[256,640]{1,0:T(8,128)(2,1)S(1)}, u32[]{:S(2)}, u32[]{:S(2)}) collective-permute-start(bf16[256,640]{1,0:T(8,128)(2,1)S(1)} %get-tuple-element.68), channel_id=1, source_target_pairs={{0,4},{1,5},{2,6},{3,7},{4,0},{5,1},{6,2},{7,3},{8,28},{9,29},{10,... | collective-permute-start | bytes 983048 | tf_op jit(solution)/shard_map/ppermute | solution.py:23
  7.4 13.8 %collective-permute-start.7 = (bf16[256,640]{1,0:T(8,128)(2,1)S(1)}, bf16[256,640]{1,0:T(8,128)(2,1)S(1)}, u32[]{:S(2)}, u32[]{:S(2)}) collective-permute-start(bf16[256,640]{1,0:T(8,128)(2,1)S(1)} %get-tuple-element.69), channel_id=1, source_target_pairs={{0,32},{1,33},{2,34},{3,35},{4,36},{5,37},{6,38},{7,39},{8,104},{9... | collective-permute-start | bytes 983048 | tf_op jit(solution)/shard_map/ppermute | solution.py:23
  9.9 11.4 %collective-permute-start.8 = (bf16[256,640]{1,0:T(8,128)(2,1)S(1)}, bf16[256,640]{1,0:T(8,128)(2,1)S(1)}, u32[]{:S(2)}, u32[]{:S(2)}) collective-permute-start(bf16[256,640]{1,0:T(8,128)(2,1)S(1)} %get-tuple-element.69), channel_id=1, source_target_pairs={{0,96},{1,97},{2,98},{3,99},{4,100},{5,101},{6,102},{7,103},{8,40}... | collective-permute-start | bytes 983048 | tf_op jit(solution)/shard_map/ppermute | solution.py:23
  10.0 15.2 %collective-permute-start.6 = (bf16[256,640]{1,0:T(8,128)(2,1)S(1)}, bf16[256,640]{1,0:T(8,128)(2,1)S(1)}, u32[]{:S(2)}, u32[]{:S(2)}) collective-permute-start(bf16[256,640]{1,0:T(8,128)(2,1)S(1)} %get-tuple-element.68), channel_id=1, source_target_pairs={{0,20},{1,21},{2,22},{3,23},{4,16},{5,17},{6,18},{7,19},{8,12},{9,... | collective-permute-start | bytes 983048 | tf_op jit(solution)/shard_map/ppermute | solution.py:23
  14.5 18.6 %collective-permute-start.2 = (bf16[1024,256]{1,0:T(8,128)(2,1)S(1)}, bf16[1024,256]{1,0:T(8,128)(2,1)S(1)}, u32[]{:S(2)}, u32[]{:S(2)}) collective-permute-start(bf16[1024,256]{1,0:T(8,128)(2,1)S(1)} %get-tuple-element.29), channel_id=1, source_target_pairs={{0,4},{1,5},{2,6},{3,7},{4,0},{5,1},{6,2},{7,3},{8,12},{9,13},{10,... | collective-permute-start | bytes 1572872 | tf_op jit(solution)/shard_map/ppermute | solution.py:23
  21.2 11.9 %copy-start.6 = (bf16[512,640]{1,0:T(8,128)(2,1)S(1)}, bf16[512,640]{1,0:T(8,128)(2,1)}, u32[]{:S(2)}) copy-start(bf16[512,640]{1,0:T(8,128)(2,1)} %param.5) | copy-start | bytes 1966084
  21.3 17.0 %collective-permute-start.10 = (bf16[1024,256]{1,0:T(8,128)(2,1)S(1)}, bf16[1024,256]{1,0:T(8,128)(2,1)S(1)}, u32[]{:S(2)}, u32[]{:S(2)}) collective-permute-start(bf16[1024,256]{1,0:T(8,128)(2,1)S(1)} %get-tuple-element.33), channel_id=1, source_target_pairs={{0,1},{1,0},{2,3},{3,2},{4,5},{5,4},{6,7},{7,6},{8,11},{9,10},{10,... | collective-permute-start | bytes 1572872 | tf_op jit(solution)/shard_map/ppermute | solution.py:23
  25.1 12.6 %collective-permute-start.11 = (bf16[1024,256]{1,0:T(8,128)(2,1)S(1)}, bf16[1024,256]{1,0:T(8,128)(2,1)S(1)}, u32[]{:S(2)}, u32[]{:S(2)}) collective-permute-start(bf16[1024,256]{1,0:T(8,128)(2,1)S(1)} %get-tuple-element.33), channel_id=1, source_target_pairs={{0,3},{1,2},{2,1},{3,0},{4,7},{5,6},{6,5},{7,4},{8,9},{9,8},{10,11... | collective-permute-start | bytes 1572872 | tf_op jit(solution)/shard_map/ppermute | solution.py:23
  25.2 25.4 %collective-permute-start.18 = (bf16[768,640]{1,0:T(8,128)(2,1)S(1)}, bf16[768,640]{1,0:T(8,128)(2,1)S(1)}, u32[]{:S(2)}, u32[]{:S(2)}) collective-permute-start(bf16[768,640]{1,0:T(8,128)(2,1)S(1)} %constant_dynamic-update-slice_fusion.2), channel_id=1, source_target_pairs={{0,96},{1,97},{2,98},{3,99},{4,100},{5,101},{6,102},{7,103},{8,40}... | collective-permute-start | bytes 2949128 | tf_op jit(solution)/shard_map/ppermute | solution.py:23
  27.1 26.8 %collective-permute-start.9 = (bf16[768,640]{1,0:T(8,128)(2,1)S(1)}, bf16[768,640]{1,0:T(8,128)(2,1)S(1)}, u32[]{:S(2)}, u32[]{:S(2)}) collective-permute-start(bf16[768,640]{1,0:T(8,128)(2,1)S(1)} %constant_dynamic-update-slice_fusion.2), channel_id=1, source_target_pairs={{0,32},{1,33},{2,34},{3,35},{4,36},{5,37},{6,38},{7,39},{8,104},{9... | collective-permute-start | bytes 2949128 | tf_op jit(solution)/shard_map/ppermute | solution.py:23
  33.2 15.4 %collective-permute-start.3 = (bf16[512,640]{1,0:T(8,128)(2,1)S(1)}, bf16[512,640]{1,0:T(8,128)(2,1)S(1)}, u32[]{:S(2)}, u32[]{:S(2)}) collective-permute-start(bf16[512,640]{1,0:T(8,128)(2,1)S(1)} %copy-done.6), channel_id=1, source_target_pairs={{0,4},{1,5},{2,6},{3,7},{4,0},{5,1},{6,2},{7,3},{8,12},{9,13},{10,... | collective-permute-start | bytes 1966088 | tf_op jit(solution)/shard_map/ppermute | solution.py:23
  37.8 8.8 %collective-permute-start.12 = (bf16[512,256]{1,0:T(8,128)(2,1)S(1)}, bf16[512,256]{1,0:T(8,128)(2,1)S(1)}, u32[]{:S(2)}, u32[]{:S(2)}) collective-permute-start(bf16[512,256]{1,0:T(8,128)(2,1)S(1)} %slice.116), channel_id=1, source_target_pairs={{0,1},{1,0},{2,3},{3,2},{4,5},{5,4},{6,7},{7,6},{8,11},{9,10},{10,... | collective-permute-start | bytes 786440 | tf_op jit(solution)/shard_map/ppermute | solution.py:23
  38.3 8.3 %collective-permute-start.13 = (bf16[512,256]{1,0:T(8,128)(2,1)S(1)}, bf16[512,256]{1,0:T(8,128)(2,1)S(1)}, u32[]{:S(2)}, u32[]{:S(2)}) collective-permute-start(bf16[512,256]{1,0:T(8,128)(2,1)S(1)} %slice.117), channel_id=1, source_target_pairs={{0,3},{1,2},{2,1},{3,0},{4,7},{5,6},{6,5},{7,4},{8,9},{9,8},{10,11... | collective-permute-start | bytes 786440 | tf_op jit(solution)/shard_map/ppermute | solution.py:23
  46.6 16.3 %collective-permute-start.14 = (bf16[1024,256]{1,0:T(8,128)(2,1)S(1)}, bf16[1024,256]{1,0:T(8,128)(2,1)S(1)}, u32[]{:S(2)}, u32[]{:S(2)}) collective-permute-start(bf16[1024,256]{1,0:T(8,128)(2,1)S(1)} %collective-permute-done.2), channel_id=1, source_target_pairs={{0,1},{1,0},{2,3},{3,2},{4,5},{5,4},{6,7},{7,6},{8,11},{9,10},{10,... | collective-permute-start | bytes 1572872 | tf_op jit(solution)/shard_map/ppermute | solution.py:23
  46.6 13.0 %collective-permute-start.15 = (bf16[1024,256]{1,0:T(8,128)(2,1)S(1)}, bf16[1024,256]{1,0:T(8,128)(2,1)S(1)}, u32[]{:S(2)}, u32[]{:S(2)}) collective-permute-start(bf16[1024,256]{1,0:T(8,128)(2,1)S(1)} %collective-permute-done.2), channel_id=1, source_target_pairs={{0,3},{1,2},{2,1},{3,0},{4,7},{5,6},{6,5},{7,4},{8,9},{9,8},{10,11... | collective-permute-start | bytes 1572872 | tf_op jit(solution)/shard_map/ppermute | solution.py:23
  48.7 22.2 %collective-permute-start.4 = (bf16[512,1280]{1,0:T(8,128)(2,1)S(1)}, bf16[512,1280]{1,0:T(8,128)(2,1)S(1)}, u32[]{:S(2)}, u32[]{:S(2)}) collective-permute-start(bf16[512,1280]{1,0:T(8,128)(2,1)S(1)} %constant_dynamic-update-slice_fusion), channel_id=1, source_target_pairs={{0,8},{1,9},{2,10},{3,11},{4,12},{5,13},{6,14},{7,15},{8,0},{9,1},... | collective-permute-start | bytes 3932168 | tf_op jit(solution)/shard_map/ppermute | solution.py:23
  50.8 29.0 %collective-permute-start.19 = (bf16[512,640]{1,0:T(8,128)(2,1)S(1)}, bf16[512,640]{1,0:T(8,128)(2,1)S(1)}, u32[]{:S(2)}, u32[]{:S(2)}) collective-permute-start(bf16[512,640]{1,0:T(8,128)(2,1)S(1)} %slice.120), channel_id=1, source_target_pairs={{0,32},{1,33},{2,34},{3,35},{4,36},{5,37},{6,38},{7,39},{8,104},{9... | collective-permute-start | bytes 1966088 | tf_op jit(solution)/shard_map/ppermute | solution.py:23
  54.0 25.7 %collective-permute-start.20 = (bf16[512,640]{1,0:T(8,128)(2,1)S(1)}, bf16[512,640]{1,0:T(8,128)(2,1)S(1)}, u32[]{:S(2)}, u32[]{:S(2)}) collective-permute-start(bf16[512,640]{1,0:T(8,128)(2,1)S(1)} %slice.121), channel_id=1, source_target_pairs={{0,96},{1,97},{2,98},{3,99},{4,100},{5,101},{6,102},{7,103},{8,40}... | collective-permute-start | bytes 1966088 | tf_op jit(solution)/shard_map/ppermute | solution.py:23
  59.6 8.0 %collective-permute-start.16 = (bf16[512,256]{1,0:T(8,128)(2,1)S(1)}, bf16[512,256]{1,0:T(8,128)(2,1)S(1)}, u32[]{:S(2)}, u32[]{:S(2)}) collective-permute-start(bf16[512,256]{1,0:T(8,128)(2,1)S(1)} %slice.118), channel_id=1, source_target_pairs={{0,1},{1,0},{2,3},{3,2},{4,5},{5,4},{6,7},{7,6},{8,11},{9,10},{10,... | collective-permute-start | bytes 786440 | tf_op jit(solution)/shard_map/ppermute | solution.py:23
  62.9 7.9 %collective-permute-start.17 = (bf16[512,256]{1,0:T(8,128)(2,1)S(1)}, bf16[512,256]{1,0:T(8,128)(2,1)S(1)}, u32[]{:S(2)}, u32[]{:S(2)}) collective-permute-start(bf16[512,256]{1,0:T(8,128)(2,1)S(1)} %slice.119), channel_id=1, source_target_pairs={{0,3},{1,2},{2,1},{3,0},{4,7},{5,6},{6,5},{7,4},{8,9},{9,8},{10,11... | collective-permute-start | bytes 786440 | tf_op jit(solution)/shard_map/ppermute | solution.py:23
  79.7 27.5 %collective-permute-start.31 = (bf16[2,2,256,640]{3,2,1,0:T(8,128)(2,1)S(1)}, bf16[2,2,256,640]{3,2,1,0:T(8,128)(2,1)}, u32[]{:S(2)}, u32[]{:S(2)}) collective-permute-start(bf16[2,2,256,640]{3,2,1,0:T(8,128)(2,1)S(1)} %get-tuple-element.53), channel_id=1, source_target_pairs={{0,96},{1,97},{2,98},{3,99},{4,100},{5,101},{6,102},{7,103},{8,40}... | collective-permute-start | bytes 3932168 | tf_op jit(solution)/shard_map/ppermute | solution.py:23
  90.4 14.0 %collective-permute-start.23 = (bf16[2,1024,256]{2,1,0:T(8,128)(2,1)S(1)}, bf16[2,1024,256]{2,1,0:T(8,128)(2,1)S(1)}, u32[]{:S(2)}, u32[]{:S(2)}) collective-permute-start(bf16[2,1024,256]{2,1,0:T(8,128)(2,1)S(1)} %get-tuple-element.44), channel_id=1, source_target_pairs={{0,3},{1,2},{2,1},{3,0},{4,7},{5,6},{6,5},{7,4},{8,9},{9,8},{10,11... | collective-permute-start | bytes 3145736 | tf_op jit(solution)/shard_map/ppermute | solution.py:23
  98.2 11.9 %collective-permute-start.21 = (bf16[512,1280]{1,0:T(8,128)(2,1)S(1)}, bf16[512,1280]{1,0:T(8,128)(2,1)S(1)}, u32[]{:S(2)}, u32[]{:S(2)}) collective-permute-start(bf16[512,1280]{1,0:T(8,128)(2,1)S(1)} %get-tuple-element.42), channel_id=1, source_target_pairs={{0,8},{1,9},{2,10},{3,11},{4,12},{5,13},{6,14},{7,15},{8,0},{9,1},... | collective-permute-start | bytes 3932168 | tf_op jit(solution)/shard_map/ppermute | solution.py:23
  101.5 17.7 %collective-permute-start.29 = (bf16[2,2,256,640]{3,2,1,0:T(8,128)(2,1)S(1)}, bf16[2,2,256,640]{3,2,1,0:T(8,128)(2,1)S(1)}, u32[]{:S(2)}, u32[]{:S(2)}) collective-permute-start(bf16[2,2,256,640]{3,2,1,0:T(8,128)(2,1)S(1)} %get-tuple-element.51), channel_id=1, source_target_pairs={{0,32},{1,33},{2,34},{3,35},{4,36},{5,37},{6,38},{7,39},{8,104},{9... | collective-permute-start | bytes 3932168 | tf_op jit(solution)/shard_map/ppermute | solution.py:23
  103.3 17.1 %collective-permute-start.25 = (bf16[2,1024,256]{2,1,0:T(8,128)(2,1)}, bf16[2,1024,256]{2,1,0:T(8,128)(2,1)}, u32[]{:S(2)}, u32[]{:S(2)}) collective-permute-start(bf16[2,1024,256]{2,1,0:T(8,128)(2,1)} %get-tuple-element.47), channel_id=1, source_target_pairs={{0,1},{1,0},{2,3},{3,2},{4,5},{5,4},{6,7},{7,6},{8,11},{9,10},{10,... | collective-permute-start | bytes 3145736 | tf_op jit(solution)/shard_map/ppermute | solution.py:23
  104.4 4.9 %copy-start.4 = (bf16[2,1024,256]{2,1,0:T(8,128)(2,1)}, bf16[2,1024,256]{2,1,0:T(8,128)(2,1)S(1)}, u32[]{:S(2)}) copy-start(bf16[2,1024,256]{2,1,0:T(8,128)(2,1)S(1)} %collective-permute-done.23) | copy-start | bytes 3145732
  105.5 19.1 %collective-permute-start.24 = (bf16[1024,256]{1,0:T(8,128)(2,1)}, bf16[1024,256]{1,0:T(8,128)(2,1)}, u32[]{:S(2)}, u32[]{:S(2)}) collective-permute-start(bf16[1024,256]{1,0:T(8,128)(2,1)} %fusion.7), channel_id=1, source_target_pairs={{0,1},{1,0},{2,3},{3,2},{4,5},{5,4},{6,7},{7,6},{8,11},{9,10},{10,... | collective-permute-start | bytes 1572872 | tf_op jit(solution)/shard_map/ppermute | solution.py:23
  109.3 18.6 %collective-permute-start.32 = (bf16[2,256,640]{2,1,0:T(8,128)(2,1)}, bf16[2,256,640]{2,1,0:T(8,128)(2,1)}, u32[]{:S(2)}, u32[]{:S(2)}) collective-permute-start(bf16[2,256,640]{2,1,0:T(8,128)(2,1)} %fusion.5), channel_id=1, source_target_pairs={{0,32},{1,33},{2,34},{3,35},{4,36},{5,37},{6,38},{7,39},{8,104},{9... | collective-permute-start | bytes 1966088 | tf_op jit(solution)/shard_map/ppermute | solution.py:23
  110.4 10.0 %copy-start = (f32[512,1280]{1,0:T(8,128)}, f32[512,1280]{1,0:T(8,128)S(1)}, u32[]{:S(2)}) copy-start(f32[512,1280]{1,0:T(8,128)S(1)} %convert_add_fusion) | copy-start | bytes 7864324
  111.4 14.5 %collective-permute-start.22 = (bf16[512,640]{1,0:T(8,128)(2,1)}, bf16[512,640]{1,0:T(8,128)(2,1)S(1)}, u32[]{:S(2)}, u32[]{:S(2)}) collective-permute-start(bf16[512,640]{1,0:T(8,128)(2,1)} %slice.191), channel_id=1, source_target_pairs={{0,4},{1,5},{2,6},{3,7},{4,0},{5,1},{6,2},{7,3},{8,12},{9,13},{10,... | collective-permute-start | bytes 1966088 | tf_op jit(solution)/shard_map/ppermute | solution.py:23
  119.1 1.3 copy-start.2
  120.4 12.5 %collective-permute-start.30 = (bf16[2,256,640]{2,1,0:T(8,128)(2,1)}, bf16[2,256,640]{2,1,0:T(8,128)(2,1)}, u32[]{:S(2)}, u32[]{:S(2)}) collective-permute-start(bf16[2,256,640]{2,1,0:T(8,128)(2,1)} %fusion.4), channel_id=1, source_target_pairs={{0,96},{1,97},{2,98},{3,99},{4,100},{5,101},{6,102},{7,103},{8,40}... | collective-permute-start | bytes 1966088 | tf_op jit(solution)/shard_map/ppermute | solution.py:23
  120.4 4.2 %copy-start.5 = (bf16[2,1024,256]{2,1,0:T(8,128)(2,1)S(1)}, bf16[2,1024,256]{2,1,0:T(8,128)(2,1)}, u32[]{:S(2)}) copy-start(bf16[2,1024,256]{2,1,0:T(8,128)(2,1)} %copy-done.4) | copy-start | bytes 3145732
  121.7 11.2 %copy-start.3 = (bf16[2,2,256,640]{3,2,1,0:T(8,128)(2,1)S(1)}, bf16[2,2,256,640]{3,2,1,0:T(8,128)(2,1)}, u32[]{:S(2)}) copy-start(bf16[2,2,256,640]{3,2,1,0:T(8,128)(2,1)} %copy-done.2) | copy-start | bytes 3932164
  121.7 18.0 %collective-permute-start.26 = (bf16[1024,256]{1,0:T(8,128)(2,1)S(1)}, bf16[1024,256]{1,0:T(8,128)(2,1)S(1)}, u32[]{:S(2)}, u32[]{:S(2)}) collective-permute-start(bf16[1024,256]{1,0:T(8,128)(2,1)S(1)} %fusion.8), channel_id=1, source_target_pairs={{0,3},{1,2},{2,1},{3,0},{4,7},{5,6},{6,5},{7,4},{8,9},{9,8},{10,11... | collective-permute-start | bytes 1572872 | tf_op jit(solution)/shard_map/ppermute | solution.py:23
  125.9 13.8 %collective-permute-start.27 = (bf16[1024,256]{1,0:T(8,128)(2,1)S(1)}, bf16[1024,256]{1,0:T(8,128)(2,1)S(1)}, u32[]{:S(2)}, u32[]{:S(2)}) collective-permute-start(bf16[1024,256]{1,0:T(8,128)(2,1)S(1)} %fusion.3), channel_id=1, source_target_pairs={{0,4},{1,5},{2,6},{3,7},{4,0},{5,1},{6,2},{7,3},{8,12},{9,13},{10,... | collective-permute-start | bytes 1572872 | tf_op jit(solution)/shard_map/ppermute | solution.py:23
  132.9 5.7 %copy-start.1 = (f32[512,1280]{1,0:T(8,128)S(1)}, f32[512,1280]{1,0:T(8,128)}, u32[]{:S(2)}) copy-start(f32[512,1280]{1,0:T(8,128)} %copy-done) | copy-start | bytes 7864324
  135.1 17.8 %collective-permute-start.33 = (bf16[256,640]{1,0:T(8,128)(2,1)S(1)}, bf16[256,640]{1,0:T(8,128)(2,1)S(1)}, u32[]{:S(2)}, u32[]{:S(2)}) collective-permute-start(bf16[256,640]{1,0:T(8,128)(2,1)S(1)} %get-tuple-element.67), channel_id=1, source_target_pairs={{0,16},{1,17},{2,18},{3,19},{4,20},{5,21},{6,22},{7,23},{8,24},{9,... | collective-permute-start | bytes 983048 | tf_op jit(solution)/shard_map/ppermute | solution.py:23
  137.4 15.4 %collective-permute-start.34 = (bf16[256,640]{1,0:T(8,128)(2,1)S(1)}, bf16[256,640]{1,0:T(8,128)(2,1)S(1)}, u32[]{:S(2)}, u32[]{:S(2)}) collective-permute-start(bf16[256,640]{1,0:T(8,128)(2,1)S(1)} %get-tuple-element.57), channel_id=1, source_target_pairs={{0,4},{1,5},{2,6},{3,7},{4,0},{5,1},{6,2},{7,3},{8,28},{9,29},{10,... | collective-permute-start | bytes 983048 | tf_op jit(solution)/shard_map/ppermute | solution.py:23
  138.3 14.5 %collective-permute-start.35 = (bf16[256,640]{1,0:T(8,128)(2,1)S(1)}, bf16[256,640]{1,0:T(8,128)(2,1)S(1)}, u32[]{:S(2)}, u32[]{:S(2)}) collective-permute-start(bf16[256,640]{1,0:T(8,128)(2,1)S(1)} %get-tuple-element.58), channel_id=1, source_target_pairs={{0,20},{1,21},{2,22},{3,23},{4,16},{5,17},{6,18},{7,19},{8,12},{9,... | collective-permute-start | bytes 983048 | tf_op jit(solution)/shard_map/ppermute | solution.py:23
  141.1 13.1 %collective-permute-start.28 = (bf16[512,512]{1,0:T(8,128)(2,1)S(1)}, bf16[512,512]{1,0:T(8,128)(2,1)S(1)}, u32[]{:S(2)}, u32[]{:S(2)}) collective-permute-start(bf16[512,512]{1,0:T(8,128)(2,1)S(1)} %pad_maximum_fusion.6), channel_id=1, source_target_pairs={{0,8},{1,9},{2,10},{3,11},{4,12},{5,13},{6,14},{7,15},{8,0},{9,1},... | collective-permute-start | bytes 1572872 | tf_op jit(solution)/shard_map/ppermute | solution.py:23

commit v5 on v4

--- a/solution.py
+++ b/solution.py
@@ -97,9 +97,21 @@
 
             @pl.when(step == at)
             def _():
-                store(out.at[place])
+                store(out.at[0])
 
             at += 1
+
+
+def out_specs(groups, shape):
+    specs, first = [], 0
+    for group in groups:
+
+        def index(k, m, first=first, last=len(group) - 1):
+            return (jnp.clip(k - first, 0, last), *(0 for _ in shape))
+
+        specs.append(pl.BlockSpec((1, *shape), index))
+        first += len(group)
+    return specs
 
 
 def dw_kernel(groups, m, a, g, *outs):
@@ -128,7 +140,7 @@
             num_scalar_prefetch=1,
             grid=(8,),
             in_specs=[pl.BlockSpec((1, t, d), a_index), pl.BlockSpec(g.shape, lambda k, m: (0, 0))],
-            out_specs=[pl.BlockSpec((len(group), 2, d, cols), lambda k, m: (0, 0, 0, 0)) for group in groups],
+            out_specs=out_specs(groups, (2, d, cols)),
         ),
         out_shape=[jax.ShapeDtypeStruct((len(group), 2, d, cols), BF16) for group in groups],
         compiler_params=pltpu.CompilerParams(vmem_limit_bytes=32 << 20),
@@ -166,7 +178,7 @@
                 pl.BlockSpec((1, 1, d, cols), functools.partial(w_index, 0)),
                 pl.BlockSpec((1, 1, d, cols), functools.partial(w_index, 1)),
             ],
-            out_specs=[pl.BlockSpec((len(group), t, d), lambda k, m: (0, 0, 0)) for group in groups],
+            out_specs=out_specs(groups, (t, d)),
         ),
         out_shape=[jax.ShapeDtypeStruct((len(group), t, d), BF16) for group in groups],
         compiler_params=pltpu.CompilerParams(vmem_limit_bytes=32 << 20),
@@ -296,6 +308,7 @@
     got_one = flip(jnp.where(c == 0, send1, send3), y=ONE)
     got_two = flip(jnp.where(c == 0, send3, send1), y=TWO)
     got_far = flip(send2, y=2)
+    input_grad, got_one, got_two, got_far = tie(input_grad, got_one, got_two, got_far)
     same, diff = add(dw_0[0], got_far), add(got_one, got_two)
     weight_grad = jnp.where(y_lo == 0, jnp.concatenate([same, diff], 0), jnp.concatenate([diff, same], 0))
     return projected, input_grad, weight_grad

time: 156 us -> 163 us (1.045)
  waiting for transfers between devices: 65.7 us -> 72.9 us
  starting transfers between devices: 43.5 us -> 45.6 us
    ppermute x36, waiting for transfers between devices: 65.7 us -> 72.9 us  [flip(): return lax.ppermute(value, AXES, pairs)]
    ppermute x36, starting transfers between devices: 43.5 us -> 45.6 us  [flip(): return lax.ppermute(value, AXES, pairs)]
  transfers between devices with their start and end apart: 36 -> 36, of which waited for: 14 -> 16; matrix products, arithmetic and copies ran while one was open for 11% -> 9% of each run, Pallas kernels for 17% -> 15%
where the time goes in v5:
time: 163 us; the launch traced here: 162 us
  waiting for transfers between devices  72.9 us (45%)
  starting transfers between devices  45.6 us (28%)
  Pallas kernels  24.8 us (15%)
  other arithmetic  17.1 us (10%)
    ppermute x36, waiting for transfers between devices, flip(): return lax.ppermute(value, AXES, pairs)  72.9 us
    ppermute x36, starting transfers between devices, flip(): return lax.ppermute(value, AXES, pairs)  45.6 us
    pallas_call x1, Pallas kernels, weight_terms(): pl.pallas_call(functools.partial(dw_kernel, groups), grid_spec=pltpu.Pref...  8.63 us
    pallas_call x1, Pallas kernels, input_terms(): pl.pallas_call(functools.partial(da_kernel, groups), grid_spec=pltpu.Pref...  8.46 us
    pallas_call x1, Pallas kernels, forward_terms(): pl.pallas_call(fwd_kernel, grid_spec=pltpu.PrefetchScalarGridSpec(num_sca...  7.66 us
  transfers between devices with their start and end apart: 36, of which 16 were waited for; matrix products, arithmetic and copies ran while one was open for 9% of the time, Pallas kernels for 15%

profile of v5, /device:TPU:1, one launch (start us, length us, event | category | flops | bytes accessed | tf_op | source)
XLA Modules:
  0.0 162.4 jit_solution(13254266952710217263)
XLA Ops:
  0.7 1.3 broadcast_select_fusion.4
  2.0 1.5 collective-permute-start.1
  3.6 3.1 %collective-permute-start = (bf16[256,640]{1,0:T(8,128)(2,1)S(1)}, bf16[256,640]{1,0:T(8,128)(2,1)S(1)}, u32[]{:S(2)}, u32[]{:S(2)}) collective-permute-start(bf16[256,640]{1,0:T(8,128)(2,1)S(1)} %get-tuple-element.77), channel_id=1, source_target_pairs={{0,16},{1,17},{2,18},{3,19},{4,20},{5,21},{6,22},{7,23},{8,24},{9,... | collective-permute-start | bytes 983048 | tf_op jit(solution)/shard_map/ppermute | solution.py:23
  6.6 0.8 collective-permute-start.5
  7.4 2.5 %collective-permute-start.7 = (bf16[256,640]{1,0:T(8,128)(2,1)S(1)}, bf16[256,640]{1,0:T(8,128)(2,1)S(1)}, u32[]{:S(2)}, u32[]{:S(2)}) collective-permute-start(bf16[256,640]{1,0:T(8,128)(2,1)S(1)} %get-tuple-element.77), channel_id=1, source_target_pairs={{0,32},{1,33},{2,34},{3,35},{4,36},{5,37},{6,38},{7,39},{8,104},{9... | collective-permute-start | bytes 983048 | tf_op jit(solution)/shard_map/ppermute | solution.py:23
  10.1 4.4 %collective-permute-done = bf16[256,640]{1,0:T(8,128)(2,1)S(1)} collective-permute-done((bf16[256,640]{1,0:T(8,128)(2,1)S(1)}, bf16[256,640]{1,0:T(8,128)(2,1)S(1)}, u32[]{:S(2)}, u32[]{:S(2)}) %collective-permute-start) | collective-permute-done | bytes 327712 | tf_op jit(solution)/shard_map/ppermute | solution.py:23
  14.5 1.3 collective-permute-start.2
  15.8 5.4 %collective-permute-done.5 = bf16[256,640]{1,0:T(8,128)(2,1)S(1)} collective-permute-done((bf16[256,640]{1,0:T(8,128)(2,1)S(1)}, bf16[256,640]{1,0:T(8,128)(2,1)S(1)}, u32[]{:S(2)}, u32[]{:S(2)}) %collective-permute-start.5) | collective-permute-done | bytes 327712 | tf_op jit(solution)/shard_map/ppermute | solution.py:23
  21.3 3.8 %collective-permute-start.10 = (bf16[1024,256]{1,0:T(8,128)(2,1)S(1)}, bf16[1024,256]{1,0:T(8,128)(2,1)S(1)}, u32[]{:S(2)}, u32[]{:S(2)}) collective-permute-start(bf16[1024,256]{1,0:T(8,128)(2,1)S(1)} %get-tuple-element.37), channel_id=1, source_target_pairs={{0,1},{1,0},{2,3},{3,2},{4,5},{5,4},{6,7},{7,6},{8,11},{9,10},{10,... | collective-permute-start | bytes 1572872 | tf_op jit(solution)/shard_map/ppermute | solution.py:23
  25.2 1.9 %collective-permute-start.18 = (bf16[768,640]{1,0:T(8,128)(2,1)S(1)}, bf16[768,640]{1,0:T(8,128)(2,1)S(1)}, u32[]{:S(2)}, u32[]{:S(2)}) collective-permute-start(bf16[768,640]{1,0:T(8,128)(2,1)S(1)} %constant_dynamic-update-slice_fusion.2), channel_id=1, source_target_pairs={{0,96},{1,97},{2,98},{3,99},{4,100},{5,101},{6,102},{7,103},{8,40}... | collective-permute-start | bytes 2949128 | tf_op jit(solution)/shard_map/ppermute | solution.py:23
  27.1 1.9 %collective-permute-start.9 = (bf16[768,640]{1,0:T(8,128)(2,1)S(1)}, bf16[768,640]{1,0:T(8,128)(2,1)S(1)}, u32[]{:S(2)}, u32[]{:S(2)}) collective-permute-start(bf16[768,640]{1,0:T(8,128)(2,1)S(1)} %constant_dynamic-update-slice_fusion.2), channel_id=1, source_target_pairs={{0,32},{1,33},{2,34},{3,35},{4,36},{5,37},{6,38},{7,39},{8,104},{9... | collective-permute-start | bytes 2949128 | tf_op jit(solution)/shard_map/ppermute | solution.py:23
  29.0 4.1 %collective-permute-done.2 = bf16[1024,256]{1,0:T(8,128)(2,1)S(1)} collective-permute-done((bf16[1024,256]{1,0:T(8,128)(2,1)S(1)}, bf16[1024,256]{1,0:T(8,128)(2,1)S(1)}, u32[]{:S(2)}, u32[]{:S(2)}) %collective-permute-start.2) | collective-permute-done | bytes 524320 | tf_op jit(solution)/shard_map/ppermute | solution.py:23
  33.2 1.1 collective-permute-start.3
  34.3 0.1 pad_maximum_fusion.2
  34.4 3.4 %collective-permute-done.11 = bf16[1024,256]{1,0:T(8,128)(2,1)S(1)} collective-permute-done((bf16[1024,256]{1,0:T(8,128)(2,1)S(1)}, bf16[1024,256]{1,0:T(8,128)(2,1)S(1)}, u32[]{:S(2)}, u32[]{:S(2)}) %collective-permute-start.11) | collective-permute-done | bytes 524320 | tf_op jit(solution)/shard_map/ppermute | solution.py:23
  37.8 0.5 collective-permute-start.12
  38.3 0.7 collective-permute-start.13
  39.0 7.5 %collective-permute-done.12 = bf16[512,256]{1,0:T(8,128)(2,1)S(1)} collective-permute-done((bf16[512,256]{1,0:T(8,128)(2,1)S(1)}, bf16[512,256]{1,0:T(8,128)(2,1)S(1)}, u32[]{:S(2)}, u32[]{:S(2)}) %collective-permute-start.12) | collective-permute-done | bytes 262176 | tf_op jit(solution)/shard_map/ppermute | solution.py:23
  46.7 1.9 %collective-permute-done.3 = bf16[512,640]{1,0:T(8,128)(2,1)S(1)} collective-permute-done((bf16[512,640]{1,0:T(8,128)(2,1)S(1)}, bf16[512,640]{1,0:T(8,128)(2,1)S(1)}, u32[]{:S(2)}, u32[]{:S(2)}) %collective-permute-start.3) | collective-permute-done | bytes 655392 | tf_op jit(solution)/shard_map/ppermute | solution.py:23
  48.7 1.8 %collective-permute-start.4 = (bf16[512,1280]{1,0:T(8,128)(2,1)S(1)}, bf16[512,1280]{1,0:T(8,128)(2,1)S(1)}, u32[]{:S(2)}, u32[]{:S(2)}) collective-permute-start(bf16[512,1280]{1,0:T(8,128)(2,1)S(1)} %constant_dynamic-update-slice_fusion), channel_id=1, source_target_pairs={{0,8},{1,9},{2,10},{3,11},{4,12},{5,13},{6,14},{7,15},{8,0},{9,1},... | collective-permute-start | bytes 3932168 | tf_op jit(solution)/shard_map/ppermute | solution.py:23
  50.6 0.2 constant_dynamic-update-slice_fusion.5
  50.8 3.2 %collective-permute-start.19 = (bf16[512,640]{1,0:T(8,128)(2,1)S(1)}, bf16[512,640]{1,0:T(8,128)(2,1)S(1)}, u32[]{:S(2)}, u32[]{:S(2)}) collective-permute-start(bf16[512,640]{1,0:T(8,128)(2,1)S(1)} %slice.120), channel_id=1, source_target_pairs={{0,32},{1,33},{2,34},{3,35},{4,36},{5,37},{6,38},{7,39},{8,104},{9... | collective-permute-start | bytes 1966088 | tf_op jit(solution)/shard_map/ppermute | solution.py:23
  54.1 5.5 %collective-permute-done.15 = bf16[1024,256]{1,0:T(8,128)(2,1)S(1)} collective-permute-done((bf16[1024,256]{1,0:T(8,128)(2,1)S(1)}, bf16[1024,256]{1,0:T(8,128)(2,1)S(1)}, u32[]{:S(2)}, u32[]{:S(2)}) %collective-permute-start.15) | collective-permute-done | bytes 524320 | tf_op jit(solution)/shard_map/ppermute | solution.py:23
  59.6 3.2 %collective-permute-start.16 = (bf16[512,256]{1,0:T(8,128)(2,1)S(1)}, bf16[512,256]{1,0:T(8,128)(2,1)S(1)}, u32[]{:S(2)}, u32[]{:S(2)}) collective-permute-start(bf16[512,256]{1,0:T(8,128)(2,1)S(1)} %slice.118), channel_id=1, source_target_pairs={{0,1},{1,0},{2,3},{3,2},{4,5},{5,4},{6,7},{7,6},{8,11},{9,10},{10,... | collective-permute-start | bytes 786440 | tf_op jit(solution)/shard_map/ppermute | solution.py:23
  63.0 0.1 pad_maximum_fusion.3
  63.2 4.5 %collective-permute-done.16 = bf16[512,256]{1,0:T(8,128)(2,1)S(1)} collective-permute-done((bf16[512,256]{1,0:T(8,128)(2,1)S(1)}, bf16[512,256]{1,0:T(8,128)(2,1)S(1)}, u32[]{:S(2)}, u32[]{:S(2)}) %collective-permute-start.16) | collective-permute-done | bytes 262176 | tf_op jit(solution)/shard_map/ppermute | solution.py:23
  67.6 3.1 %collective-permute-done.17 = bf16[512,256]{1,0:T(8,128)(2,1)S(1)} collective-permute-done((bf16[512,256]{1,0:T(8,128)(2,1)S(1)}, bf16[512,256]{1,0:T(8,128)(2,1)S(1)}, u32[]{:S(2)}, u32[]{:S(2)}) %collective-permute-start.17) | collective-permute-done | bytes 262176 | tf_op jit(solution)/shard_map/ppermute | solution.py:23
  70.9 0.2 pad_maximum_fusion.1.g
  71.0 8.6 %weight_terms.1 = (bf16[2,2,256,640]{3,2,1,0:T(8,128)(2,1)S(1)}, bf16[2,2,256,640]{3,2,1,0:T(8,128)(2,1)S(1)}, bf16[1,2,256,640]{3,2,1,0:T(8,128)(2,1)S(1)}, bf1...) custom-call(s32[2]{0:T(128)S(1)} %pad_add_fusion.m, ...), custom_call_target="tpu_custom_call" | custom-call | flops 5368709120 | bytes 2621440 | tf_op jit(solution)/shard_map/weight_terms/pallas_call | solution.py:137
  79.8 0.1 pad_maximum_fusion.4
  79.9 1.0 pad_maximum_fusion.w0.w1.w
  81.0 8.5 %input_terms.1 = (bf16[2,1024,256]{2,1,0:T(8,128)(2,1)S(1)}, bf16[2,1024,256]{2,1,0:T(8,128)(2,1)S(1)}, bf16[1,1024,256]{2,1,0:T(8,128)(2,1)S(1)}, bf16[1,1024,2...) custom-call(s32[2]{0:T(128)S(1)} %pad_add_fusion.m, bf16[1024,1280]{1,0:T(8,128)(2,1)S(1)} %pad_maximum_fusion.1.g, ...), custom_call_target="tpu_custom_call" | custom-call | flops 21474836480 | bytes 10485760 | tf_op jit(solution)/shard_map/input_terms/pallas_call | solution.py:171
  89.4 0.4 collective-permute-start.23
  89.8 7.7 %forward_terms.1 = (bf16[512,1280]{1,0:T(8,128)(2,1)S(1)}, bf16[512,1280]{1,0:T(8,128)(2,1)S(1)}) custom-call(s32[2]{0:T(128)S(1)} %pad_add_fusion.m, bf16[8,1024,256]{2,1,0:T(8,128)(2,1)S(1)} %bitcast_dynamic-update-slice_fusion.a, bf16[4,4,256,640]{3,2,1,0:T(8,128)(2,1)S(1)} %pad_maximum_fusion.w0.w1.w), custom_call_target="tpu_custom_call" | custom-call | flops 5368709120 | bytes 2621440 | tf_op jit(solution)/shard_map/forward_terms/pallas_call | solution.py:215
  97.5 3.3 %collective-permute-start.21 = (bf16[512,1280]{1,0:T(8,128)(2,1)S(1)}, bf16[512,1280]{1,0:T(8,128)(2,1)S(1)}, u32[]{:S(2)}, u32[]{:S(2)}) collective-permute-start(bf16[512,1280]{1,0:T(8,128)(2,1)S(1)} %get-tuple-element.46), channel_id=1, source_target_pairs={{0,8},{1,9},{2,10},{3,11},{4,12},{5,13},{6,14},{7,15},{8,0},{9,1},... | collective-permute-start | bytes 3932168 | tf_op jit(solution)/shard_map/ppermute | solution.py:23
  100.8 1.9 %collective-permute-start.29 = (bf16[2,2,256,640]{3,2,1,0:T(8,128)(2,1)S(1)}, bf16[2,2,256,640]{3,2,1,0:T(8,128)(2,1)S(1)}, u32[]{:S(2)}, u32[]{:S(2)}) collective-permute-start(bf16[2,2,256,640]{3,2,1,0:T(8,128)(2,1)S(1)} %get-tuple-element.55), channel_id=1, source_target_pairs={{0,32},{1,33},{2,34},{3,35},{4,36},{5,37},{6,38},{7,39},{8,104},{9... | collective-permute-start | bytes 3932168 | tf_op jit(solution)/shard_map/ppermute | solution.py:23
  102.7 1.0 collective-permute-start.25
  103.7 0.1 fusion.7
  103.9 1.7 %collective-permute-start.24 = (bf16[1024,256]{1,0:T(8,128)(2,1)S(1)}, bf16[1024,256]{1,0:T(8,128)(2,1)S(1)}, u32[]{:S(2)}, u32[]{:S(2)}) collective-permute-start(bf16[1024,256]{1,0:T(8,128)(2,1)S(1)} %fusion.7), channel_id=1, source_target_pairs={{0,1},{1,0},{2,3},{3,2},{4,5},{5,4},{6,7},{7,6},{8,11},{9,10},{10,... | collective-permute-start | bytes 1572872 | tf_op jit(solution)/shard_map/ppermute | solution.py:23
  105.6 2.1 %fusion.5 = bf16[2,256,640]{2,1,0:T(8,128)(2,1)} fusion(bf16[1,2,256,640]{3,2,1,0:T(8,128)(2,1)S(1)} %get-tuple-element.58, bf16[2,2,256,640]{3,2,1,0:T(8,128)(2,1)} %collective-permute-done.31), kind=kLoop, calls=%fused_computation.29 | loop fusion | flops 1310720 | bytes 1966080 | tf_op jit(solution)/shard_map/convert_element_type | solution.py:52
  107.7 0.8 collective-permute-start.32
  108.5 0.3 convert_add_fusion
  108.8 0.9 collective-permute-start.22
  109.7 8.7 %collective-permute-done.29 = bf16[2,2,256,640]{3,2,1,0:T(8,128)(2,1)S(1)} collective-permute-done((bf16[2,2,256,640]{3,2,1,0:T(8,128)(2,1)S(1)}, bf16[2,2,256,640]{3,2,1,0:T(8,128)(2,1)S(1)}, u32[]{:S(2)}, u32[]{:S(2)}) %collective-permute-start.29) | collective-permute-done | bytes 1310752 | tf_op jit(solution)/shard_map/ppermute | solution.py:23
  118.5 1.1 fusion.4
  119.6 0.9 fusion.8
  120.5 0.2 collective-permute-start.26
  120.8 3.1 %collective-permute-done.24 = bf16[1024,256]{1,0:T(8,128)(2,1)S(1)} collective-permute-done((bf16[1024,256]{1,0:T(8,128)(2,1)S(1)}, bf16[1024,256]{1,0:T(8,128)(2,1)S(1)}, u32[]{:S(2)}, u32[]{:S(2)}) %collective-permute-start.24) | collective-permute-done | bytes 524320 | tf_op jit(solution)/shard_map/ppermute | solution.py:23
  123.8 1.1 fusion.3
  124.9 0.7 collective-permute-start.27
  125.7 1.7 %collective-permute-done.32 = bf16[2,256,640]{2,1,0:T(8,128)(2,1)} collective-permute-done((bf16[2,256,640]{2,1,0:T(8,128)(2,1)}, bf16[2,256,640]{2,1,0:T(8,128)(2,1)}, u32[]{:S(2)}, u32[]{:S(2)}) %collective-permute-start.32) | collective-permute-done | bytes 655392 | tf_op jit(solution)/shard_map/ppermute | solution.py:23
  127.4 4.8 %collective-permute-done.30 = bf16[2,256,640]{2,1,0:T(8,128)(2,1)} collective-permute-done((bf16[2,256,640]{2,1,0:T(8,128)(2,1)}, bf16[2,256,640]{2,1,0:T(8,128)(2,1)}, u32[]{:S(2)}, u32[]{:S(2)}) %collective-permute-start.30) | collective-permute-done | bytes 655392 | tf_op jit(solution)/shard_map/ppermute | solution.py:23
  132.3 2.1 %bitcast_add_fusion.1 = (f32[2,256,640]{2,1,0:T(8,128)S(1)}, bf16[2,256,640]{2,1,0:T(8,128)(2,1)S(1)}) fusion(bf16[2,256,640]{2,1,0:T(8,128)(2,1)} %collective-permute-done.30, bf16[2,2,256,640]{3,2,1,0:T(8,128)(2,1)} %copy-done.2, bf16[2,2,256,640]{3,2,1,0:T(8,128)(2,1)S(1)} %get-tuple-element.54, bf16[2,256,640]{2,1,0:T(8,128)(2,1)} %collective-permute-done.32, ...), kind=kLoop, calls=%fused_computation.12 | loop fusion | flops 3604480 | bytes 5898240 | tf_op jit(solution)/shard_map/add | solution.py:36
  134.4 3.0 %collective-permute-done.27 = bf16[1024,256]{1,0:T(8,128)(2,1)} collective-permute-done((bf16[1024,256]{1,0:T(8,128)(2,1)}, bf16[1024,256]{1,0:T(8,128)(2,1)}, u32[]{:S(2)}, u32[]{:S(2)}) %collective-permute-start.27) | collective-permute-done | bytes 524320 | tf_op jit(solution)/shard_map/ppermute | solution.py:23
  137.4 1.5 broadcast_select_fusion.1
  139.0 2.2 %collective-permute-start.28 = (bf16[512,512]{1,0:T(8,128)(2,1)S(1)}, bf16[512,512]{1,0:T(8,128)(2,1)S(1)}, u32[]{:S(2)}, u32[]{:S(2)}) collective-permute-start(bf16[512,512]{1,0:T(8,128)(2,1)S(1)} %pad_maximum_fusion.6), channel_id=1, source_target_pairs={{0,8},{1,9},{2,10},{3,11},{4,12},{5,13},{6,14},{7,15},{8,0},{9,1},... | collective-permute-start | bytes 1572872 | tf_op jit(solution)/shard_map/ppermute | solution.py:23
  141.3 3.6 %collective-permute-start.33 = (bf16[256,640]{1,0:T(8,128)(2,1)S(1)}, bf16[256,640]{1,0:T(8,128)(2,1)S(1)}, u32[]{:S(2)}, u32[]{:S(2)}) collective-permute-start(bf16[256,640]{1,0:T(8,128)(2,1)S(1)} %get-tuple-element.66), channel_id=1, source_target_pairs={{0,4},{1,5},{2,6},{3,7},{4,0},{5,1},{6,2},{7,3},{8,28},{9,29},{10,... | collective-permute-start | bytes 983048 | tf_op jit(solution)/shard_map/ppermute | solution.py:23
  144.9 1.3 collective-permute-start.35
  146.2 2.1 %fusion = bf16[512,640]{1,0:T(8,128)(2,1)} fusion(f32[512,1280]{1,0:T(8,128)S(1)} %copy-done.1, bf16[512,640]{1,0:T(8,128)(2,1)} %collective-permute-done.22), kind=kLoop, calls=%fused_computation.5 | loop fusion | flops 983040 | bytes 2621440 | tf_op jit(solution)/shard_map/convert_element_type | solution.py:297
  148.3 0.2 broadcast_select_fusion.3
  148.5 1.1 pad_maximum_fusion.5
  149.6 9.0 %collective-permute-done.33 = bf16[256,640]{1,0:T(8,128)(2,1)S(1)} collective-permute-done((bf16[256,640]{1,0:T(8,128)(2,1)S(1)}, bf16[256,640]{1,0:T(8,128)(2,1)S(1)}, u32[]{:S(2)}, u32[]{:S(2)}) %collective-permute-start.33) | collective-permute-done | bytes 327712 | tf_op jit(solution)/shard_map/ppermute | solution.py:23
  158.6 2.6 %collective-permute-done.35 = bf16[256,640]{1,0:T(8,128)(2,1)S(1)} collective-permute-done((bf16[256,640]{1,0:T(8,128)(2,1)S(1)}, bf16[256,640]{1,0:T(8,128)(2,1)S(1)}, u32[]{:S(2)}, u32[]{:S(2)}) %collective-permute-start.35) | collective-permute-done | bytes 327712 | tf_op jit(solution)/shard_map/ppermute | solution.py:23
  161.3 1.1 maximum_select_fusion
  (67 shorter events, 1.7 us)
Async XLA Ops:
  0.6 2.9 %copy-start.4 = (bf16[512,640]{1,0:T(8,128)(2,1)S(1)}, bf16[512,640]{1,0:T(8,128)(2,1)}, u32[]{:S(2)}) copy-start(bf16[512,640]{1,0:T(8,128)(2,1)} %param.4) | copy-start | bytes 1966084
  2.0 8.0 %collective-permute-start.1 = (bf16[512,512]{1,0:T(8,128)(2,1)S(1)}, bf16[512,512]{1,0:T(8,128)(2,1)S(1)}, u32[]{:S(2)}, u32[]{:S(2)}) collective-permute-start(bf16[512,512]{1,0:T(8,128)(2,1)S(1)} %get-tuple-element.73), channel_id=1, source_target_pairs={{0,8},{1,9},{2,10},{3,11},{4,12},{5,13},{6,14},{7,15},{8,0},{9,1},... | collective-permute-start | bytes 1572872 | tf_op jit(solution)/shard_map/ppermute | solution.py:23
  3.6 11.0 %collective-permute-start = (bf16[256,640]{1,0:T(8,128)(2,1)S(1)}, bf16[256,640]{1,0:T(8,128)(2,1)S(1)}, u32[]{:S(2)}, u32[]{:S(2)}) collective-permute-start(bf16[256,640]{1,0:T(8,128)(2,1)S(1)} %get-tuple-element.77), channel_id=1, source_target_pairs={{0,16},{1,17},{2,18},{3,19},{4,20},{5,21},{6,22},{7,23},{8,24},{9,... | collective-permute-start | bytes 983048 | tf_op jit(solution)/shard_map/ppermute | solution.py:23
  6.6 14.6 %collective-permute-start.5 = (bf16[256,640]{1,0:T(8,128)(2,1)S(1)}, bf16[256,640]{1,0:T(8,128)(2,1)S(1)}, u32[]{:S(2)}, u32[]{:S(2)}) collective-permute-start(bf16[256,640]{1,0:T(8,128)(2,1)S(1)} %get-tuple-element.76), channel_id=1, source_target_pairs={{0,4},{1,5},{2,6},{3,7},{4,0},{5,1},{6,2},{7,3},{8,28},{9,29},{10,... | collective-permute-start | bytes 983048 | tf_op jit(solution)/shard_map/ppermute | solution.py:23
  7.4 13.8 %collective-permute-start.7 = (bf16[256,640]{1,0:T(8,128)(2,1)S(1)}, bf16[256,640]{1,0:T(8,128)(2,1)S(1)}, u32[]{:S(2)}, u32[]{:S(2)}) collective-permute-start(bf16[256,640]{1,0:T(8,128)(2,1)S(1)} %get-tuple-element.77), channel_id=1, source_target_pairs={{0,32},{1,33},{2,34},{3,35},{4,36},{5,37},{6,38},{7,39},{8,104},{9... | collective-permute-start | bytes 983048 | tf_op jit(solution)/shard_map/ppermute | solution.py:23
  9.9 11.4 %collective-permute-start.8 = (bf16[256,640]{1,0:T(8,128)(2,1)S(1)}, bf16[256,640]{1,0:T(8,128)(2,1)S(1)}, u32[]{:S(2)}, u32[]{:S(2)}) collective-permute-start(bf16[256,640]{1,0:T(8,128)(2,1)S(1)} %get-tuple-element.77), channel_id=1, source_target_pairs={{0,96},{1,97},{2,98},{3,99},{4,100},{5,101},{6,102},{7,103},{8,40}... | collective-permute-start | bytes 983048 | tf_op jit(solution)/shard_map/ppermute | solution.py:23
  10.0 15.2 %collective-permute-start.6 = (bf16[256,640]{1,0:T(8,128)(2,1)S(1)}, bf16[256,640]{1,0:T(8,128)(2,1)S(1)}, u32[]{:S(2)}, u32[]{:S(2)}) collective-permute-start(bf16[256,640]{1,0:T(8,128)(2,1)S(1)} %get-tuple-element.76), channel_id=1, source_target_pairs={{0,20},{1,21},{2,22},{3,23},{4,16},{5,17},{6,18},{7,19},{8,12},{9,... | collective-permute-start | bytes 983048 | tf_op jit(solution)/shard_map/ppermute | solution.py:23
  14.5 18.6 %collective-permute-start.2 = (bf16[1024,256]{1,0:T(8,128)(2,1)S(1)}, bf16[1024,256]{1,0:T(8,128)(2,1)S(1)}, u32[]{:S(2)}, u32[]{:S(2)}) collective-permute-start(bf16[1024,256]{1,0:T(8,128)(2,1)S(1)} %get-tuple-element.33), channel_id=1, source_target_pairs={{0,4},{1,5},{2,6},{3,7},{4,0},{5,1},{6,2},{7,3},{8,12},{9,13},{10,... | collective-permute-start | bytes 1572872 | tf_op jit(solution)/shard_map/ppermute | solution.py:23
  21.2 11.9 %copy-start.3 = (bf16[512,640]{1,0:T(8,128)(2,1)S(1)}, bf16[512,640]{1,0:T(8,128)(2,1)}, u32[]{:S(2)}) copy-start(bf16[512,640]{1,0:T(8,128)(2,1)} %param.5) | copy-start | bytes 1966084
  21.3 17.0 %collective-permute-start.10 = (bf16[1024,256]{1,0:T(8,128)(2,1)S(1)}, bf16[1024,256]{1,0:T(8,128)(2,1)S(1)}, u32[]{:S(2)}, u32[]{:S(2)}) collective-permute-start(bf16[1024,256]{1,0:T(8,128)(2,1)S(1)} %get-tuple-element.37), channel_id=1, source_target_pairs={{0,1},{1,0},{2,3},{3,2},{4,5},{5,4},{6,7},{7,6},{8,11},{9,10},{10,... | collective-permute-start | bytes 1572872 | tf_op jit(solution)/shard_map/ppermute | solution.py:23
  25.1 12.6 %collective-permute-start.11 = (bf16[1024,256]{1,0:T(8,128)(2,1)S(1)}, bf16[1024,256]{1,0:T(8,128)(2,1)S(1)}, u32[]{:S(2)}, u32[]{:S(2)}) collective-permute-start(bf16[1024,256]{1,0:T(8,128)(2,1)S(1)} %get-tuple-element.37), channel_id=1, source_target_pairs={{0,3},{1,2},{2,1},{3,0},{4,7},{5,6},{6,5},{7,4},{8,9},{9,8},{10,11... | collective-permute-start | bytes 1572872 | tf_op jit(solution)/shard_map/ppermute | solution.py:23
  25.2 25.4 %collective-permute-start.18 = (bf16[768,640]{1,0:T(8,128)(2,1)S(1)}, bf16[768,640]{1,0:T(8,128)(2,1)S(1)}, u32[]{:S(2)}, u32[]{:S(2)}) collective-permute-start(bf16[768,640]{1,0:T(8,128)(2,1)S(1)} %constant_dynamic-update-slice_fusion.2), channel_id=1, source_target_pairs={{0,96},{1,97},{2,98},{3,99},{4,100},{5,101},{6,102},{7,103},{8,40}... | collective-permute-start | bytes 2949128 | tf_op jit(solution)/shard_map/ppermute | solution.py:23
  27.1 26.8 %collective-permute-start.9 = (bf16[768,640]{1,0:T(8,128)(2,1)S(1)}, bf16[768,640]{1,0:T(8,128)(2,1)S(1)}, u32[]{:S(2)}, u32[]{:S(2)}) collective-permute-start(bf16[768,640]{1,0:T(8,128)(2,1)S(1)} %constant_dynamic-update-slice_fusion.2), channel_id=1, source_target_pairs={{0,32},{1,33},{2,34},{3,35},{4,36},{5,37},{6,38},{7,39},{8,104},{9... | collective-permute-start | bytes 2949128 | tf_op jit(solution)/shard_map/ppermute | solution.py:23
  33.2 15.4 %collective-permute-start.3 = (bf16[512,640]{1,0:T(8,128)(2,1)S(1)}, bf16[512,640]{1,0:T(8,128)(2,1)S(1)}, u32[]{:S(2)}, u32[]{:S(2)}) collective-permute-start(bf16[512,640]{1,0:T(8,128)(2,1)S(1)} %copy-done.3), channel_id=1, source_target_pairs={{0,4},{1,5},{2,6},{3,7},{4,0},{5,1},{6,2},{7,3},{8,12},{9,13},{10,... | collective-permute-start | bytes 1966088 | tf_op jit(solution)/shard_map/ppermute | solution.py:23
  37.8 8.8 %collective-permute-start.12 = (bf16[512,256]{1,0:T(8,128)(2,1)S(1)}, bf16[512,256]{1,0:T(8,128)(2,1)S(1)}, u32[]{:S(2)}, u32[]{:S(2)}) collective-permute-start(bf16[512,256]{1,0:T(8,128)(2,1)S(1)} %slice.116), channel_id=1, source_target_pairs={{0,1},{1,0},{2,3},{3,2},{4,5},{5,4},{6,7},{7,6},{8,11},{9,10},{10,... | collective-permute-start | bytes 786440 | tf_op jit(solution)/shard_map/ppermute | solution.py:23
  38.3 8.3 %collective-permute-start.13 = (bf16[512,256]{1,0:T(8,128)(2,1)S(1)}, bf16[512,256]{1,0:T(8,128)(2,1)S(1)}, u32[]{:S(2)}, u32[]{:S(2)}) collective-permute-start(bf16[512,256]{1,0:T(8,128)(2,1)S(1)} %slice.117), channel_id=1, source_target_pairs={{0,3},{1,2},{2,1},{3,0},{4,7},{5,6},{6,5},{7,4},{8,9},{9,8},{10,11... | collective-permute-start | bytes 786440 | tf_op jit(solution)/shard_map/ppermute | solution.py:23
  46.6 16.3 %collective-permute-start.14 = (bf16[1024,256]{1,0:T(8,128)(2,1)S(1)}, bf16[1024,256]{1,0:T(8,128)(2,1)S(1)}, u32[]{:S(2)}, u32[]{:S(2)}) collective-permute-start(bf16[1024,256]{1,0:T(8,128)(2,1)S(1)} %collective-permute-done.2), channel_id=1, source_target_pairs={{0,1},{1,0},{2,3},{3,2},{4,5},{5,4},{6,7},{7,6},{8,11},{9,10},{10,... | collective-permute-start | bytes 1572872 | tf_op jit(solution)/shard_map/ppermute | solution.py:23
  46.6 13.0 %collective-permute-start.15 = (bf16[1024,256]{1,0:T(8,128)(2,1)S(1)}, bf16[1024,256]{1,0:T(8,128)(2,1)S(1)}, u32[]{:S(2)}, u32[]{:S(2)}) collective-permute-start(bf16[1024,256]{1,0:T(8,128)(2,1)S(1)} %collective-permute-done.2), channel_id=1, source_target_pairs={{0,3},{1,2},{2,1},{3,0},{4,7},{5,6},{6,5},{7,4},{8,9},{9,8},{10,11... | collective-permute-start | bytes 1572872 | tf_op jit(solution)/shard_map/ppermute | solution.py:23
  48.7 22.2 %collective-permute-start.4 = (bf16[512,1280]{1,0:T(8,128)(2,1)S(1)}, bf16[512,1280]{1,0:T(8,128)(2,1)S(1)}, u32[]{:S(2)}, u32[]{:S(2)}) collective-permute-start(bf16[512,1280]{1,0:T(8,128)(2,1)S(1)} %constant_dynamic-update-slice_fusion), channel_id=1, source_target_pairs={{0,8},{1,9},{2,10},{3,11},{4,12},{5,13},{6,14},{7,15},{8,0},{9,1},... | collective-permute-start | bytes 3932168 | tf_op jit(solution)/shard_map/ppermute | solution.py:23
  50.8 29.0 %collective-permute-start.19 = (bf16[512,640]{1,0:T(8,128)(2,1)S(1)}, bf16[512,640]{1,0:T(8,128)(2,1)S(1)}, u32[]{:S(2)}, u32[]{:S(2)}) collective-permute-start(bf16[512,640]{1,0:T(8,128)(2,1)S(1)} %slice.120), channel_id=1, source_target_pairs={{0,32},{1,33},{2,34},{3,35},{4,36},{5,37},{6,38},{7,39},{8,104},{9... | collective-permute-start | bytes 1966088 | tf_op jit(solution)/shard_map/ppermute | solution.py:23
  54.0 25.7 %collective-permute-start.20 = (bf16[512,640]{1,0:T(8,128)(2,1)S(1)}, bf16[512,640]{1,0:T(8,128)(2,1)S(1)}, u32[]{:S(2)}, u32[]{:S(2)}) collective-permute-start(bf16[512,640]{1,0:T(8,128)(2,1)S(1)} %slice.121), channel_id=1, source_target_pairs={{0,96},{1,97},{2,98},{3,99},{4,100},{5,101},{6,102},{7,103},{8,40}... | collective-permute-start | bytes 1966088 | tf_op jit(solution)/shard_map/ppermute | solution.py:23
  59.6 8.0 %collective-permute-start.16 = (bf16[512,256]{1,0:T(8,128)(2,1)S(1)}, bf16[512,256]{1,0:T(8,128)(2,1)S(1)}, u32[]{:S(2)}, u32[]{:S(2)}) collective-permute-start(bf16[512,256]{1,0:T(8,128)(2,1)S(1)} %slice.118), channel_id=1, source_target_pairs={{0,1},{1,0},{2,3},{3,2},{4,5},{5,4},{6,7},{7,6},{8,11},{9,10},{10,... | collective-permute-start | bytes 786440 | tf_op jit(solution)/shard_map/ppermute | solution.py:23
  62.9 7.9 %collective-permute-start.17 = (bf16[512,256]{1,0:T(8,128)(2,1)S(1)}, bf16[512,256]{1,0:T(8,128)(2,1)S(1)}, u32[]{:S(2)}, u32[]{:S(2)}) collective-permute-start(bf16[512,256]{1,0:T(8,128)(2,1)S(1)} %slice.119), channel_id=1, source_target_pairs={{0,3},{1,2},{2,1},{3,0},{4,7},{5,6},{6,5},{7,4},{8,9},{9,8},{10,11... | collective-permute-start | bytes 786440 | tf_op jit(solution)/shard_map/ppermute | solution.py:23
  79.7 25.9 %collective-permute-start.31 = (bf16[2,2,256,640]{3,2,1,0:T(8,128)(2,1)S(1)}, bf16[2,2,256,640]{3,2,1,0:T(8,128)(2,1)}, u32[]{:S(2)}, u32[]{:S(2)}) collective-permute-start(bf16[2,2,256,640]{3,2,1,0:T(8,128)(2,1)S(1)} %get-tuple-element.57), channel_id=1, source_target_pairs={{0,96},{1,97},{2,98},{3,99},{4,100},{5,101},{6,102},{7,103},{8,40}... | collective-permute-start | bytes 3932168 | tf_op jit(solution)/shard_map/ppermute | solution.py:23
  89.4 14.3 %collective-permute-start.23 = (bf16[2,1024,256]{2,1,0:T(8,128)(2,1)S(1)}, bf16[2,1024,256]{2,1,0:T(8,128)(2,1)S(1)}, u32[]{:S(2)}, u32[]{:S(2)}) collective-permute-start(bf16[2,1024,256]{2,1,0:T(8,128)(2,1)S(1)} %get-tuple-element.48), channel_id=1, source_target_pairs={{0,3},{1,2},{2,1},{3,0},{4,7},{5,6},{6,5},{7,4},{8,9},{9,8},{10,11... | collective-permute-start | bytes 3145736 | tf_op jit(solution)/shard_map/ppermute | solution.py:23
  97.5 11.0 %collective-permute-start.21 = (bf16[512,1280]{1,0:T(8,128)(2,1)S(1)}, bf16[512,1280]{1,0:T(8,128)(2,1)S(1)}, u32[]{:S(2)}, u32[]{:S(2)}) collective-permute-start(bf16[512,1280]{1,0:T(8,128)(2,1)S(1)} %get-tuple-element.46), channel_id=1, source_target_pairs={{0,8},{1,9},{2,10},{3,11},{4,12},{5,13},{6,14},{7,15},{8,0},{9,1},... | collective-permute-start | bytes 3932168 | tf_op jit(solution)/shard_map/ppermute | solution.py:23
  100.8 17.7 %collective-permute-start.29 = (bf16[2,2,256,640]{3,2,1,0:T(8,128)(2,1)S(1)}, bf16[2,2,256,640]{3,2,1,0:T(8,128)(2,1)S(1)}, u32[]{:S(2)}, u32[]{:S(2)}) collective-permute-start(bf16[2,2,256,640]{3,2,1,0:T(8,128)(2,1)S(1)} %get-tuple-element.55), channel_id=1, source_target_pairs={{0,32},{1,33},{2,34},{3,35},{4,36},{5,37},{6,38},{7,39},{8,104},{9... | collective-permute-start | bytes 3932168 | tf_op jit(solution)/shard_map/ppermute | solution.py:23
  102.7 16.9 %collective-permute-start.25 = (bf16[2,1024,256]{2,1,0:T(8,128)(2,1)S(1)}, bf16[2,1024,256]{2,1,0:T(8,128)(2,1)S(1)}, u32[]{:S(2)}, u32[]{:S(2)}) collective-permute-start(bf16[2,1024,256]{2,1,0:T(8,128)(2,1)S(1)} %get-tuple-element.51), channel_id=1, source_target_pairs={{0,1},{1,0},{2,3},{3,2},{4,5},{5,4},{6,7},{7,6},{8,11},{9,10},{10,... | collective-permute-start | bytes 3145736 | tf_op jit(solution)/shard_map/ppermute | solution.py:23
  103.9 20.0 %collective-permute-start.24 = (bf16[1024,256]{1,0:T(8,128)(2,1)S(1)}, bf16[1024,256]{1,0:T(8,128)(2,1)S(1)}, u32[]{:S(2)}, u32[]{:S(2)}) collective-permute-start(bf16[1024,256]{1,0:T(8,128)(2,1)S(1)} %fusion.7), channel_id=1, source_target_pairs={{0,1},{1,0},{2,3},{3,2},{4,5},{5,4},{6,7},{7,6},{8,11},{9,10},{10,... | collective-permute-start | bytes 1572872 | tf_op jit(solution)/shard_map/ppermute | solution.py:23
  107.7 19.7 %collective-permute-start.32 = (bf16[2,256,640]{2,1,0:T(8,128)(2,1)}, bf16[2,256,640]{2,1,0:T(8,128)(2,1)}, u32[]{:S(2)}, u32[]{:S(2)}) collective-permute-start(bf16[2,256,640]{2,1,0:T(8,128)(2,1)} %fusion.5), channel_id=1, source_target_pairs={{0,32},{1,33},{2,34},{3,35},{4,36},{5,37},{6,38},{7,39},{8,104},{9... | collective-permute-start | bytes 1966088 | tf_op jit(solution)/shard_map/ppermute | solution.py:23
  108.7 10.8 %copy-start = (f32[512,1280]{1,0:T(8,128)}, f32[512,1280]{1,0:T(8,128)S(1)}, u32[]{:S(2)}) copy-start(f32[512,1280]{1,0:T(8,128)S(1)} %convert_add_fusion) | copy-start | bytes 7864324
  108.8 16.1 %collective-permute-start.22 = (bf16[512,640]{1,0:T(8,128)(2,1)S(1)}, bf16[512,640]{1,0:T(8,128)(2,1)}, u32[]{:S(2)}, u32[]{:S(2)}) collective-permute-start(bf16[512,640]{1,0:T(8,128)(2,1)S(1)} %slice.191), channel_id=1, source_target_pairs={{0,4},{1,5},{2,6},{3,7},{4,0},{5,1},{6,2},{7,3},{8,12},{9,13},{10,... | collective-permute-start | bytes 1966088 | tf_op jit(solution)/shard_map/ppermute | solution.py:23
  118.5 2.1 %copy-start.2 = (bf16[2,2,256,640]{3,2,1,0:T(8,128)(2,1)}, bf16[2,2,256,640]{3,2,1,0:T(8,128)(2,1)S(1)}, u32[]{:S(2)}) copy-start(bf16[2,2,256,640]{3,2,1,0:T(8,128)(2,1)S(1)} %collective-permute-done.29) | copy-start | bytes 3932164
  119.6 12.7 %collective-permute-start.30 = (bf16[2,256,640]{2,1,0:T(8,128)(2,1)}, bf16[2,256,640]{2,1,0:T(8,128)(2,1)}, u32[]{:S(2)}, u32[]{:S(2)}) collective-permute-start(bf16[2,256,640]{2,1,0:T(8,128)(2,1)} %fusion.4), channel_id=1, source_target_pairs={{0,96},{1,97},{2,98},{3,99},{4,100},{5,101},{6,102},{7,103},{8,40}... | collective-permute-start | bytes 1966088 | tf_op jit(solution)/shard_map/ppermute | solution.py:23
  120.5 13.9 %collective-permute-start.26 = (bf16[1024,256]{1,0:T(8,128)(2,1)}, bf16[1024,256]{1,0:T(8,128)(2,1)}, u32[]{:S(2)}, u32[]{:S(2)}) collective-permute-start(bf16[1024,256]{1,0:T(8,128)(2,1)} %fusion.8), channel_id=1, source_target_pairs={{0,3},{1,2},{2,1},{3,0},{4,7},{5,6},{6,5},{7,4},{8,9},{9,8},{10,11... | collective-permute-start | bytes 1572872 | tf_op jit(solution)/shard_map/ppermute | solution.py:23
  124.9 12.5 %collective-permute-start.27 = (bf16[1024,256]{1,0:T(8,128)(2,1)}, bf16[1024,256]{1,0:T(8,128)(2,1)}, u32[]{:S(2)}, u32[]{:S(2)}) collective-permute-start(bf16[1024,256]{1,0:T(8,128)(2,1)} %fusion.3), channel_id=1, source_target_pairs={{0,4},{1,5},{2,6},{3,7},{4,0},{5,1},{6,2},{7,3},{8,12},{9,13},{10,... | collective-permute-start | bytes 1572872 | tf_op jit(solution)/shard_map/ppermute | solution.py:23
  139.0 7.3 %copy-start.1 = (f32[512,1280]{1,0:T(8,128)S(1)}, f32[512,1280]{1,0:T(8,128)}, u32[]{:S(2)}) copy-start(f32[512,1280]{1,0:T(8,128)} %copy-done) | copy-start | bytes 7864324
  139.0 9.3 %collective-permute-start.28 = (bf16[512,512]{1,0:T(8,128)(2,1)S(1)}, bf16[512,512]{1,0:T(8,128)(2,1)S(1)}, u32[]{:S(2)}, u32[]{:S(2)}) collective-permute-start(bf16[512,512]{1,0:T(8,128)(2,1)S(1)} %pad_maximum_fusion.6), channel_id=1, source_target_pairs={{0,8},{1,9},{2,10},{3,11},{4,12},{5,13},{6,14},{7,15},{8,0},{9,1},... | collective-permute-start | bytes 1572872 | tf_op jit(solution)/shard_map/ppermute | solution.py:23
  141.3 17.3 %collective-permute-start.33 = (bf16[256,640]{1,0:T(8,128)(2,1)S(1)}, bf16[256,640]{1,0:T(8,128)(2,1)S(1)}, u32[]{:S(2)}, u32[]{:S(2)}) collective-permute-start(bf16[256,640]{1,0:T(8,128)(2,1)S(1)} %get-tuple-element.66), channel_id=1, source_target_pairs={{0,4},{1,5},{2,6},{3,7},{4,0},{5,1},{6,2},{7,3},{8,28},{9,29},{10,... | collective-permute-start | bytes 983048 | tf_op jit(solution)/shard_map/ppermute | solution.py:23
  144.9 13.7 %collective-permute-start.34 = (bf16[256,640]{1,0:T(8,128)(2,1)S(1)}, bf16[256,640]{1,0:T(8,128)(2,1)S(1)}, u32[]{:S(2)}, u32[]{:S(2)}) collective-permute-start(bf16[256,640]{1,0:T(8,128)(2,1)S(1)} %get-tuple-element.65), channel_id=1, source_target_pairs={{0,20},{1,21},{2,22},{3,23},{4,16},{5,17},{6,18},{7,19},{8,12},{9,... | collective-permute-start | bytes 983048 | tf_op jit(solution)/shard_map/ppermute | solution.py:23
  144.9 16.3 %collective-permute-start.35 = (bf16[256,640]{1,0:T(8,128)(2,1)S(1)}, bf16[256,640]{1,0:T(8,128)(2,1)S(1)}, u32[]{:S(2)}, u32[]{:S(2)}) collective-permute-start(bf16[256,640]{1,0:T(8,128)(2,1)S(1)} %get-tuple-element.75), channel_id=1, source_target_pairs={{0,16},{1,17},{2,18},{3,19},{4,20},{5,21},{6,22},{7,23},{8,24},{9,... | collective-permute-start | bytes 983048 | tf_op jit(solution)/shard_map/ppermute | solution.py:23
